TPU v7x, 128 devices: a whole 4x4x4 slice. The times are simulated.
128 devices in a mesh: sub: 4 (over y), tok: 32 (over z, x, core).
Axes of the slice: x: 4, y: 4, z: 4, core: 2. Of those that a mesh axis runs over, the one named last changes fastest.
Arguments:
- token_ids: int32 [8192], P('tok'), may hold values from 0 to 32767
- target_ids: int32 [4096], P('tok'), may hold values from 0 to 32767
- doc_lengths: int32 [512], P('tok'), may hold values from 0 to 128, as said below
- width_tiles: int32 [4, 5], replicated, may hold values from 0 to 1, as said below
- head_mask: int32 [4, 8], replicated, may hold values from 0 to 1, as said below
- ffn_tiles: int32 [4, 24], replicated, may hold values from 0 to 1, as said below
- slot_block: int32 [800], replicated, may hold values from 0 to 780, as said below
- master: float32 [800, 128, 128], P('tok')
- momentum: float32 [800, 128, 128], P('tok'), may hold values from -1.9073486e-05 to 1.9073486e-05
- left_stat: float32 [800, 128, 128], P('tok')
- right_stat: float32 [800, 128, 128], P('tok')
- left_root: float32 [800, 128, 128], P('tok')
- right_root: float32 [800, 128, 128], P('tok')
- table: float32 [32768, 640], P('tok')
- table_m: float32 [32768, 640], P('tok'), may hold values from -2.3841858e-06 to 2.3841858e-06
- table_v: float32 [32768, 640], P('tok'), may hold values from 2.4177034e-13 to 9.658962e-13
- vec: float32 [14, 640], replicated
- vec_m: float32 [14, 640], replicated, may hold values from -2.2888184e-05 to 2.2888184e-05
- vec_v: float32 [14, 640], replicated, may hold values from 2.4177032e-11 to 9.658962e-11
Outputs:
- loss_sum: float32 [], replicated
- token_count: float32 [], replicated
- grad_norm: float32 [], replicated
- new_master: float32 [800, 128, 128], P('tok')
- new_momentum: float32 [800, 128, 128], P('tok')
- new_left: float32 [800, 128, 128], P('tok')
- new_right: float32 [800, 128, 128], P('tok')
- new_table: float32 [32768, 640], P('tok')
- new_table_m: float32 [32768, 640], P('tok')
- new_table_v: float32 [32768, 640], P('tok')
- new_vec: float32 [14, 640], replicated
- new_vec_m: float32 [14, 640], replicated
- new_vec_v: float32 [14, 640], replicated
Inputs may be any that keep to these rules, and one draw needn't show every extreme that they name: `doc_lengths`: the lengths of one block sum to at most 128; the last block holds one document of 128. `width_tiles`: each row is a run of ones then zeros; row 0 is all ones; row 4 - 1 has the fewest ones, 4. `head_mask`: each row is a run of ones then zeros; row 0 is all ones; row 4 - 1 has 4 ones. `ffn_tiles`: each row is a run of ones then zeros; row 0 is all ones; row 4 - 1 has 8 ones. `slot_block`: every block number below 780 stands in exactly one slot; the other slots hold 780.
All inputs are finite; a program needn't handle non-finite values.
Results may differ from a plain program's by a relative error of at most 0.0025.
The roundings to bfloat16 on the way count: a program that leaves them out, or rounds other values in their place, can miss the bound.
Values may be sent and summed in bfloat16 or wider, within the bound.
A program may use at most 384 MiB of HBM per device.

v0:
```python
import math

import jax
import jax.numpy as jnp
from jax import lax
from jax.sharding import Mesh
from jax.sharding import PartitionSpec as P

D = 640
HEADS = 8
HEAD = 80
FF = 3072
BLK = 128
DOCS = 16
STEP = 10
HALF = 128
NBLK = 780
TOK = ("tok_0", "tok_1", "tok_2")
SUB_TOK = ("sub", "tok_0", "tok_1", "tok_2")


eps_norm = 1e-05
clip_limit = 0.02
beta_one = 0.9
beta_two = 0.98
beta_stat = 0.95
decay_rate = 0.01
adam_eps = 1e-08
rate_table = 0.05
rate_gains = 0.3
rate_blocks = 0.05
high = lax.Precision.HIGHEST
low_type = jnp.bfloat16
wide_type = jnp.float32


def joined_along(tiles, dim):
    tiles = jnp.moveaxis(tiles, 0, dim)
    dims = tiles.shape
    return tiles.reshape(*dims[:dim], dims[dim] * dims[dim + 1], *dims[dim + 2 :])


def gather_packed(arrays, axis, dims):
    vector = jnp.concatenate([a.reshape(-1) for a in arrays])
    lines, at, outs = (lax.all_gather(vector, axis), 0, [])
    for a, dim in zip(arrays, dims):
        tiles = lines[:, at : at + a.size].reshape(-1, *a.shape)
        outs.append(joined_along(tiles, dim))
        at += a.size
    return tuple(outs)


def all_blocks(value, axes, turns):
    tiles = value[None]
    for k in turns:
        tiles = lax.all_gather(tiles, axes[k], axis=0, tiled=True)
    held = [lax.axis_size(axes[k]) for k in reversed(turns)]
    tiles = tiles.reshape(*held, *value.shape)
    turned = sorted(range(len(turns)), key=lambda place: turns[len(turns) - 1 - place])
    return tiles.transpose(*turned, *range(len(turns), tiles.ndim)).reshape(-1, *value.shape)


def whole_of(value, axes, turns, dim):
    return joined_along(all_blocks(value, axes, turns), dim)


def broadcast(value, axis, root):
    return lax.dynamic_index_in_dim(lax.all_gather(value, axis), root, 0, keepdims=False)


def sent_together(arrays, axis, dim, along):
    ends, at = ([], 0)
    for a in arrays[:-1]:
        at += a.shape[along]
        ends.append(at)
    both = jnp.concatenate(arrays, axis=along)
    return tuple(jnp.split(lax.all_gather(both, axis, axis=dim, tiled=True), ends, axis=along))


def gathered_once(value, axis):
    leaves = jax.tree.leaves(value)
    turns = sorted(range(len(leaves)), key=lambda k: -leaves[k].size)
    width = (1, *leaves[turns[0]].shape)[-1]
    lines = [
        jnp.pad(leaves[k].reshape(-1), (0, -leaves[k].size % width)).reshape(-1, width)
        for k in turns
    ]
    both, at, found = (lax.all_gather(jnp.concatenate(lines), axis), 0, {})
    for k, line in zip(turns, lines):
        section = both[:, at : at + len(line)].reshape(len(both), -1)
        found[k] = section[:, : leaves[k].size].reshape(-1, *leaves[k].shape)
        at += len(line)
    numbers = iter(range(len(leaves)))
    return jax.tree.map(lambda _: found[next(numbers)], value)


def joined_all(value, axes, combine):
    for axis in axes:
        pieces = gathered_once(value, axis)
        value = jax.tree.map(lambda part: part[0], pieces)
        for k in range(1, lax.axis_size(axis)):
            value = combine(value, jax.tree.map(lambda part: part[k], pieces))
    return value


def copy_for_each(value, axis):
    copies = jnp.broadcast_to(value, (lax.axis_size(axis), *value.shape))
    return lax.all_to_all(copies, axis, split_axis=0, concat_axis=0, tiled=True)


def of_everyone(value, axis):
    return copy_for_each(value, axis).sum(axis=0)


def by_axis(value, axes):
    for axis in axes:
        value = lax.psum(value, axis)
    return value


def doc_layout(lengths):
    ends = jnp.cumsum(lengths, axis=-1)
    starts = ends - lengths
    place = jnp.arange(HALF, dtype=jnp.int32)
    member = (
        (place[:, None] >= starts[..., None, :]) & (place[:, None] < ends[..., None, :])
    ).astype(jnp.int32)
    inside = jnp.sum(member, -1)
    doc_of = jnp.sum(member * jnp.arange(DOCS, dtype=jnp.int32), -1) + DOCS * (1 - inside)
    offset = place - jnp.sum(member * starts[..., None, :], -1)
    return (doc_of, offset, inside)


def sinusoid(offset):
    half = D // 2
    freq = jnp.exp(jnp.arange(half, dtype=jnp.float32) * (-2.0 * math.log(10000.0) / D))
    angle = offset.astype(jnp.float32)[..., None] * freq
    return jnp.stack([jnp.sin(angle), jnp.cos(angle)], -1).reshape(offset.shape + (D,))


def norm(stream, gain, bias, width, active):
    centre = jnp.sum(stream * width, -1, keepdims=True) / active
    centred = (stream - centre) * width
    spread = jnp.sum(centred * centred, -1, keepdims=True) / active
    return (centred * lax.rsqrt(spread + eps_norm) * gain + bias) * width


def norm_pull(stream, gain, bias, width, active, cotangent):
    _, pull = jax.vjp(
        lambda first, second, third: norm(first, second, third, width, active), stream, gain, bias
    )
    return pull(cotangent)


def layout():
    wide = D // BLK
    deep = FF // BLK
    return [
        (wide, 3 * wide),
        (wide, wide),
        (wide, deep),
        (deep, wide),
        (wide, 3 * wide),
        (wide, wide),
        (wide, wide),
        (wide, 2 * wide),
        (wide, wide),
        (wide, deep),
        (deep, wide),
    ]


def unpack(blocks):
    result = []
    start = 0
    for rows, cols in layout():
        part = blocks[start : start + rows * cols]
        start = start + rows * cols
        result.append(
            part.reshape(rows, cols, BLK, BLK).transpose(0, 2, 1, 3).reshape(rows * BLK, cols * BLK)
        )
    return result


def pack(matrices):
    pieces = []
    for matrix in matrices:
        rows = matrix.shape[0] // BLK
        cols = matrix.shape[1] // BLK
        pieces.append(
            matrix.reshape(rows, BLK, cols, BLK)
            .transpose(0, 2, 1, 3)
            .reshape(rows * cols, BLK, BLK)
        )
    return jnp.concatenate(pieces, 0)


def matmul(left, right):
    return jnp.dot(left, right, preferred_element_type=wide_type)


def attend(query, keys, values, allowed, head_keep):
    scores = jnp.einsum("qhc,khc->hqk", query, keys, preferred_element_type=wide_type) * HEAD ** (
        -0.5
    )
    scores = jnp.where(allowed[None], scores, -1e30)
    peak = jnp.max(scores, -1, keepdims=True)
    expo = jnp.exp(scores - peak)
    probs = expo / jnp.sum(expo, -1, keepdims=True)
    probs_low = probs.astype(low_type)
    mixed = jnp.einsum("hqk,khc->qhc", probs_low, values, preferred_element_type=wide_type)
    mixed = (mixed * head_keep[:, None]).reshape(query.shape[0], D).astype(low_type)
    return (mixed, (query, keys, values, probs, probs_low))


def attend_back(d_rows, inner, head_keep):
    query, keys, values, probs, probs_low = inner
    d_mixed = (d_rows.reshape(query.shape) * head_keep[:, None]).astype(low_type)
    g_probs = jnp.einsum("qhc,khc->hqk", d_mixed, values, preferred_element_type=wide_type)
    d_values = jnp.einsum("hqk,qhc->khc", probs_low, d_mixed, preferred_element_type=wide_type)
    d_scores = (probs * (g_probs - jnp.sum(probs * g_probs, -1, keepdims=True))).astype(low_type)
    scale = HEAD ** (-0.5)
    d_query = jnp.einsum("hqk,khc->qhc", d_scores, keys, preferred_element_type=wide_type) * scale
    d_keys = jnp.einsum("hqk,qhc->khc", d_scores, query, preferred_element_type=wide_type) * scale
    return (d_query, d_keys, d_values)


def branch_back(d_out, inputs, w_out, width):
    d_branch = (d_out * width).astype(low_type)
    g_out = jnp.einsum("td,te->de", inputs, d_branch, preferred_element_type=wide_type)
    d_inputs = jnp.einsum("te,de->td", d_branch, w_out, preferred_element_type=wide_type)
    return (g_out, d_inputs)


def self_block(stream, gain, bias, w_qkv, w_out, masks, allowed):
    width, active, head_keep, unit_keep = masks
    span = stream.shape[0]
    normed = norm(stream, gain, bias, width, active).astype(low_type)
    packed = matmul(normed, w_qkv).astype(low_type).reshape(span, 3, HEADS, HEAD)
    mixed, inner = attend(packed[:, 0], packed[:, 1], packed[:, 2], allowed, head_keep)
    return (stream + matmul(mixed, w_out) * width, (stream, normed, mixed, inner))


def self_back(d_out, kept, gain, bias, w_qkv, w_out, masks):
    width, active, head_keep, unit_keep = masks
    stream, normed, mixed, inner = kept
    span = stream.shape[0]
    g_out, d_mixed = branch_back(d_out, mixed, w_out, width)
    d_query, d_keys, d_values = attend_back(d_mixed, inner, head_keep)
    d_packed = jnp.stack([d_query, d_keys, d_values], 1).reshape(span, 3 * D).astype(low_type)
    g_qkv = jnp.einsum("td,te->de", normed, d_packed, preferred_element_type=wide_type)
    d_first = jnp.einsum("te,de->td", d_packed, w_qkv, preferred_element_type=wide_type)
    d_in, g_gain, g_bias = norm_pull(stream, gain, bias, width, active, d_first)
    return (d_out + d_in, [g_qkv, g_out], [g_gain, g_bias])


def cross_block(stream, memory, gain, bias, w_query, w_pair, w_out, masks, allowed):
    width, active, head_keep, unit_keep = masks
    span = stream.shape[0]
    normed = norm(stream, gain, bias, width, active).astype(low_type)
    query = matmul(normed, w_query).astype(low_type).reshape(span, HEADS, HEAD)
    paired = matmul(memory, w_pair).astype(low_type).reshape(memory.shape[0], 2, HEADS, HEAD)
    mixed, inner = attend(query, paired[:, 0], paired[:, 1], allowed, head_keep)
    return (stream + matmul(mixed, w_out) * width, (stream, normed, mixed, inner))


def cross_back(d_out, kept, memory, gain, bias, w_query, w_pair, w_out, masks):
    width, active, head_keep, unit_keep = masks
    stream, normed, mixed, inner = kept
    span = stream.shape[0]
    g_out, d_mixed = branch_back(d_out, mixed, w_out, width)
    d_query, d_keys, d_values = attend_back(d_mixed, inner, head_keep)
    d_query = d_query.reshape(span, D).astype(low_type)
    d_pair = jnp.stack([d_keys, d_values], 1).reshape(memory.shape[0], 2 * D).astype(low_type)
    g_query = jnp.einsum("td,te->de", normed, d_query, preferred_element_type=wide_type)
    g_pair = jnp.einsum("td,te->de", memory, d_pair, preferred_element_type=wide_type)
    d_memory = jnp.einsum("te,de->td", d_pair, w_pair, preferred_element_type=wide_type)
    d_first = jnp.einsum("te,de->td", d_query, w_query, preferred_element_type=wide_type)
    d_in, g_gain, g_bias = norm_pull(stream, gain, bias, width, active, d_first)
    return (d_out + d_in, d_memory, [g_query, g_pair, g_out], [g_gain, g_bias])


def feed_block(stream, gain, bias, w_up, w_down, masks):
    width, active, head_keep, unit_keep = masks
    normed = norm(stream, gain, bias, width, active).astype(low_type)
    hidden_pre = matmul(normed, w_up)
    activated = (jax.nn.gelu(hidden_pre) * unit_keep).astype(low_type)
    return (stream + matmul(activated, w_down) * width, (stream, normed, hidden_pre, activated))


def feed_back(d_out, kept, gain, bias, w_up, w_down, masks):
    width, active, head_keep, unit_keep = masks
    stream, normed, hidden_pre, activated = kept
    g_down, d_act = branch_back(d_out, activated, w_down, width)
    _, gelu_pull = jax.vjp(jax.nn.gelu, hidden_pre)
    d_pre = gelu_pull(d_act * unit_keep)[0].astype(low_type)
    g_up = jnp.einsum("td,tf->df", normed, d_pre, preferred_element_type=wide_type)
    d_normed = jnp.einsum("tf,df->td", d_pre, w_up, preferred_element_type=wide_type)
    d_in, g_gain, g_bias = norm_pull(stream, gain, bias, width, active, d_normed)
    return (d_out + d_in, [g_up, g_down], [g_gain, g_bias])


def combine_stats(first, second):
    peak_one = jnp.maximum(first[0], second[0])
    total_one = first[1] * jnp.exp(first[0] - peak_one) + second[1] * jnp.exp(second[0] - peak_one)
    peak_two = jnp.maximum(first[2], second[2])
    total_two = first[3] * jnp.exp(first[2] - peak_two) + second[3] * jnp.exp(second[2] - peak_two)
    return (peak_one, total_one, peak_two, total_two)


def adamw(param, grad, first, second, rate):
    first = beta_one * first + (1.0 - beta_one) * grad
    second = beta_two * second + (1.0 - beta_two) * grad * grad
    fixed_first = first / (1.0 - beta_one**STEP)
    fixed_second = second / (1.0 - beta_two**STEP)
    return (
        param - rate * (fixed_first / (jnp.sqrt(fixed_second) + adam_eps) + decay_rate * param),
        first,
        second,
    )


def on_device(
    token_ids,
    target_ids,
    doc_lengths,
    width_tiles,
    head_mask,
    ffn_tiles,
    slot_block,
    master,
    momentum,
    left_stat,
    right_stat,
    left_root,
    right_root,
    table,
    table_m,
    table_v,
    vec,
    vec_m,
    vec_v,
):
    half_rows = target_ids.shape[0]
    shard_rows = table.shape[0]
    group = lax.axis_index("sub")
    place = lax.axis_index(TOK)
    doc_of, offset, inside = doc_layout(doc_lengths)
    all_ids, all_targets, all_valid = gather_packed((token_ids, target_ids, inside), TOK, (0, 0, 0))
    weight = all_valid.astype(jnp.float32)
    token_count = jnp.sum(weight)
    slots = whole_of(master.astype(low_type), (("tok_0", "tok_1"), "tok_2"), (0, 1), 0)
    inverse = (
        jnp.zeros((NBLK + 1,), jnp.int32)
        .at[slot_block]
        .set(jnp.arange(slot_block.shape[0], dtype=jnp.int32))[:NBLK]
    )
    mats = unpack(slots[inverse])
    width = jnp.repeat(width_tiles[group], BLK).astype(jnp.float32)
    active = jnp.sum(width)
    head_keep = head_mask[group].astype(jnp.float32)
    unit_keep = jnp.repeat(ffn_tiles[group], BLK).astype(jnp.float32)
    masks = (width, active, head_keep, unit_keep)
    table_low = table.astype(low_type)
    local = all_ids - place * shard_rows
    in_shard = (local >= 0) & (local < shard_rows)
    local = jnp.clip(local, 0, shard_rows - 1)
    picked = jnp.where(in_shard[:, None], table_low[local].astype(jnp.float32), 0.0)
    rows = lax.psum_scatter(
        picked.astype(jnp.bfloat16), TOK, scatter_dimension=0, tiled=True
    ).astype(jnp.float32)
    wave = sinusoid(offset)
    source = (math.sqrt(D) * rows[:half_rows] + wave) * width
    target = (math.sqrt(D) * rows[half_rows:] + wave) * width
    same = doc_of[:, None] == doc_of[None, :]
    causal = same & (offset[None, :] <= offset[:, None])
    enc_one, kept_one = self_block(source, vec[0], vec[1], mats[0], mats[1], masks, same)
    enc_two, kept_two = feed_block(enc_one, vec[2], vec[3], mats[2], mats[3], masks)
    memory = norm(enc_two, vec[4], vec[5], width, active).astype(low_type)
    dec_one, kept_three = self_block(target, vec[6], vec[7], mats[4], mats[5], masks, causal)
    dec_two, kept_four = cross_block(
        dec_one, memory, vec[8], vec[9], mats[6], mats[7], mats[8], masks, same
    )
    dec_three, kept_five = feed_block(dec_two, vec[10], vec[11], mats[9], mats[10], masks)
    final = norm(dec_three, vec[12], vec[13], width, active).astype(low_type)
    teacher_final = broadcast(final, "sub", 0)
    hidden, teacher_hidden = sent_together((final, teacher_final), TOK, 0, 1)
    logits = jnp.einsum("td,vd->tv", hidden, table_low, preferred_element_type=wide_type)
    teacher = jnp.einsum("td,vd->tv", teacher_hidden, table_low, preferred_element_type=wide_type)
    peak_student = jnp.max(logits, 1)
    total_student = jnp.sum(jnp.exp(logits - peak_student[:, None]), 1)
    peak_teacher = jnp.max(teacher, 1)
    total_teacher = jnp.sum(jnp.exp(teacher - peak_teacher[:, None]), 1)
    peak_student, total_student, peak_teacher, total_teacher = joined_all(
        (peak_student, total_student, peak_teacher, total_teacher), TOK, combine_stats
    )
    student_log = peak_student + jnp.log(total_student)
    teacher_log = peak_teacher + jnp.log(total_teacher)
    teacher_on = (group > 0).astype(jnp.float32)
    columns = jnp.arange(shard_rows, dtype=jnp.int32) + place * shard_rows
    target_dist = jnp.where(
        group > 0,
        jnp.exp(teacher - teacher_log[:, None]),
        (all_targets[:, None] == columns[None, :]).astype(jnp.float32),
    )
    term = jnp.sum(target_dist * (teacher_on * teacher - logits), 1)
    term = of_everyone(term, TOK)
    token_loss = student_log + term - teacher_on * teacher_log
    loss_group = jnp.sum(token_loss * weight)
    back = (
        (jnp.exp(logits - student_log[:, None]) - target_dist) * (weight / token_count)[:, None]
    ).astype(low_type)
    d_final = lax.psum_scatter(
        jnp.dot(back, table_low, preferred_element_type=wide_type),
        TOK,
        scatter_dimension=0,
        tiled=True,
    )
    table_grad = jnp.einsum("tv,td->vd", back, hidden, preferred_element_type=wide_type)
    d_three, g_twelve, g_thirteen = norm_pull(dec_three, vec[12], vec[13], width, active, d_final)
    d_two, grads_dec_feed, gains_five = feed_back(
        d_three, kept_five, vec[10], vec[11], mats[9], mats[10], masks
    )
    d_one, d_memory, grads_cross, gains_four = cross_back(
        d_two, kept_four, memory, vec[8], vec[9], mats[6], mats[7], mats[8], masks
    )
    d_target, grads_dec_self, gains_three = self_back(
        d_one, kept_three, vec[6], vec[7], mats[4], mats[5], masks
    )
    d_enc_two, g_four, g_five = norm_pull(enc_two, vec[4], vec[5], width, active, d_memory)
    d_enc_one, grads_enc_feed, gains_two = feed_back(
        d_enc_two, kept_two, vec[2], vec[3], mats[2], mats[3], masks
    )
    d_source, grads_enc_self, gains_one = self_back(
        d_enc_one, kept_one, vec[0], vec[1], mats[0], mats[1], masks
    )
    d_rows = (jnp.concatenate([d_source, d_target], 0) * width * math.sqrt(D)).astype(low_type)
    all_rows = lax.all_gather(d_rows, TOK, axis=0, tiled=True)
    table_grad = table_grad + jax.ops.segment_sum(
        jnp.where(in_shard[:, None], all_rows.astype(jnp.float32), 0.0), local, shard_rows
    )
    block_grads = pack(
        grads_enc_self + grads_enc_feed + grads_dec_self + grads_cross + grads_dec_feed
    )
    slot_grads = jnp.take(block_grads, slot_block, axis=0, mode="fill", fill_value=0.0)
    vec_grad = jnp.stack(
        gains_one
        + gains_two
        + [g_four, g_five]
        + gains_three
        + gains_four
        + gains_five
        + [g_twelve, g_thirteen],
        0,
    )
    own = lax.psum_scatter(slot_grads, TOK, scatter_dimension=0, tiled=True)
    own, table_grad, loss_sum = lax.psum((own, table_grad, loss_group), "sub")
    vec_grad = by_axis(vec_grad, SUB_TOK)
    square = of_everyone(jnp.sum(own * own) + jnp.sum(table_grad * table_grad), TOK)
    grad_norm = jnp.sqrt(square + jnp.sum(vec_grad * vec_grad))
    scale = jnp.minimum(1.0, clip_limit / grad_norm)
    grad = own * scale
    new_left = beta_stat * left_stat + (1.0 - beta_stat) * jnp.einsum(
        "sij,skj->sik", grad, grad, precision=high
    )
    new_right = beta_stat * right_stat + (1.0 - beta_stat) * jnp.einsum(
        "sji,sjk->sik", grad, grad, precision=high
    )
    new_momentum = beta_one * momentum + (1.0 - beta_one) * grad
    direction = jnp.einsum("sij,sjk->sik", left_root, new_momentum, precision=high)
    direction = jnp.einsum("sik,skl->sil", direction, right_root, precision=high)
    new_master = master - rate_blocks * (direction + decay_rate * master)
    new_table, new_table_m, new_table_v = adamw(
        table, table_grad * scale, table_m, table_v, rate_table
    )
    new_vec, new_vec_m, new_vec_v = adamw(vec, vec_grad * scale, vec_m, vec_v, rate_gains)
    return (
        loss_sum,
        token_count,
        grad_norm,
        new_master,
        new_momentum,
        new_left,
        new_right,
        new_table,
        new_table_m,
        new_table_v,
        new_vec,
        new_vec_m,
        new_vec_v,
    )


def solution(mesh):
    split = Mesh(
        mesh.devices.reshape(mesh.shape["sub"], 4, 4, 2), ("sub", "tok_0", "tok_1", "tok_2")
    )
    placed = (
        P(TOK),
        P(TOK),
        P(TOK),
        P(),
        P(),
        P(),
        P(),
        P(TOK, None, None),
        P(TOK, None, None),
        P(TOK, None, None),
        P(TOK, None, None),
        P(TOK, None, None),
        P(TOK, None, None),
        P(TOK, None),
        P(TOK, None),
        P(TOK, None),
        P(),
        P(),
        P(),
    )
    return jax.shard_map(
        on_device,
        mesh=split,
        in_specs=placed,
        out_specs=(
            P(),
            P(),
            P(),
            P(TOK, None, None),
            P(TOK, None, None),
            P(TOK, None, None),
            P(TOK, None, None),
            P(TOK, None),
            P(TOK, None),
            P(TOK, None),
            P(),
            P(),
            P(),
        ),
        check_vma=False,
    )
```

profile of v0, /device:TPU:0, one launch (start us, length us, event | category | flops | bytes accessed | tf_op | source)
XLA Modules:
  0.0 1235.0 jit_solution(17697702889181798801)
XLA Ops:
  11.1 25.6 %all-gather.6 = s32[32,1,512]{2,1,0:T(1,128)S(1)} all-gather(s32[1,1,512]{2,1,0:T(1,128)S(1)} %bitcast.934), channel_id=2, replica_groups=mesh['sub'=4,'tok_0'=4,'tok_1'=4,'tok_2'=2] {'tok_0','tok_1','tok_2'}, dimensions={0}, use_global_device_ids=true | all-gather | bytes 67584 | tf_op jit(solution)/shard_map/all_gather | solution.py:45
  39.5 34.2 %gather_fusion = bf16[8192,640]{1,0:T(8,128)(2,1)} fusion(bf16[1024,640]{1,0:T(8,128)(2,1)S(1)} %convert_element_type.263, s32[8192]{0:T(1024)S(1)} %broadcast_clamp_fusion), kind=kCustom, calls=%fused_computation | custom fusion | bytes 21004288 | tf_op jit(solution)/shard_map/gather | solution.py:368
  73.6 11.8 select_convert_fusion
  85.5 21.6 %all-gather.21.cloned.1.call-done = bf16[400,128,128]{2,1,0:T(8,128)(2,1)} async-done(((bf16[25,128,128]{2,1,0:T(8,128)(2,1)}), bf16[400,128,128]{2,1,0:T(8,128)(2,1)}) %all-gather.21.cloned.1.call-update) | async-done | bytes 13107216 | tf_op jit(solution)/shard_map/all_gather | solution.py:56
  109.7 5.3 scatter_custom_fusion
  118.6 64.5 %reduce-scatter.4.cloned.1.call-done = bf16[256,640]{1,0:T(8,128)(2,1)} async-done(((bf16[8192,640]{1,0:T(8,128)(2,1)}), bf16[256,640]{1,0:T(8,128)(2,1)}) %reduce-scatter.4.cloned.1.call-update) | async-done | bytes 327696 | tf_op jit(solution)/shard_map/reduce_scatter | solution.py:369
  188.1 18.0 %copy.315 = bf16[16,2,25,128,128]{4,3,2,1,0:T(8,128)(2,1)} copy(bf16[16,2,25,128,128]{4,3,2,0,1:T(8,128)(2,1)} %bitcast.837) | data formatting | bytes 52428800 | tf_op jit(solution)/shard_map/transpose | solution.py:60
  206.1 29.2 %gather_fusion.1 = bf16[780,128,128]{2,1,0:T(8,128)(2,1)} fusion(bf16[800,128,128]{2,1,0:T(8,128)(2,1)} %bitcast.819, s32[1024]{0:T(1024)S(1)} %pad_clamp_fusion.1), kind=kCustom, calls=%fused_computation.1 | custom fusion | bytes 51121200 | tf_op jit(solution)/shard_map/gather | solution.py:358
  235.3 5.3 fusion.284
  240.7 3.7 fusion.283
  244.4 11.6 fusion.282
  281.3 2.8 copy.324
  295.7 6.8 copy.325
  302.5 6.6 copy.326
  309.1 3.1 fusion.28
  332.2 4.5 copy.333
  336.7 6.5 copy.334
  343.3 3.2 fusion.20
  350.5 14.6 %all-gather.2 = bf16[512,640]{1,0:T(8,128)(2,1)S(1)} all-gather(bf16[128,640]{1,0:T(8,128)(2,1)S(1)} %multiply_convert_fusion.11), channel_id=4, replica_groups=mesh['sub'=4,'tok_0'=4,'tok_1'=4,'tok_2'=2] {'sub'}, dimensions={0}, use_global_device_ids=true | all-gather | bytes 819200 | tf_op jit(solution)/shard_map/all_gather | solution.py:68
  367.8 53.8 %all-gather.17.cloned.1.call-done = bf16[4096,1280]{1,0:T(8,128)(2,1)} async-done(((bf16[128,1280]{1,0:T(8,128)(2,1)}), bf16[4096,1280]{1,0:T(8,128)(2,1)}) %all-gather.17.cloned.1.call-update) | async-done | bytes 10485776 | tf_op jit(solution)/shard_map/all_gather | solution.py:77
  421.6 12.1 fusion.290
  433.7 8.0 exponential_reduce_fusion.1
  441.7 12.1 fusion.289
  453.8 8.0 exponential_reduce_fusion
  461.9 12.3 all-gather.7
  474.6 12.9 %all-gather.8 = f32[4,4,4096]{2,1,0:T(4,128)S(1)} all-gather(f32[1,4,4096]{2,1,0:T(4,128)S(1)} %maximum_bitcast_fusion.1), channel_id=6, replica_groups=mesh['sub'=4,'tok_0'=4,'tok_1'=4,'tok_2'=2] {'tok_1'}, dimensions={0}, use_global_device_ids=true | all-gather | bytes 327680 | tf_op jit(solution)/shard_map/all_gather | solution.py:88
  490.0 12.4 %multiply_reduce_fusion = f32[4096]{0:T(1024)S(1)} fusion(f32[4096,1024]{0,1:T(8,128)} %get-tuple-element.171, f32[4096,1024]{0,1:T(8,128)} %get-tuple-element.169, f32[]{:T(128)S(6)} %convert_element_type.303, s32[4096]{0:T(1024)S(1)} %copy-done.99, f32[4096]{0:T(1024)S(1)} %log_add_fusion, s32[1024]{0:T(1024)S(1)} %copy-done.120, pred[]{:T(512)S(6)} %gt.4), kind=kLoop, calls=%fused_computation.14 | loop fusion | flops 33550336 | bytes 33607684 | tf_op jit(solution)/shard_map/reduce_sum | solution.py:406
  503.7 5.0 all-to-all-start
  509.4 11.1 all-to-all-done
  523.2 12.8 %multiply_convert_fusion = bf16[4096,1024]{0,1:T(8,128)(2,1)S(1)} fusion(f32[4096,1024]{0,1:T(8,128)} %get-tuple-element.171, f32[4096,1024]{0,1:T(8,128)} %get-tuple-element.169, f32[4096]{0:T(1024)S(1)} %get-tuple-element.137, f32[4096]{0:T(1024)S(1)} %get-tuple-element.85, s32[4096]{0:T(1024)S(1)} %copy-done.100, f32[4096]{0:T(1024)S(1)} %log_add_fusion, ...), kind=kLoop, calls=%fused_computation.13 | loop fusion | flops 33554432 | bytes 42012672 | tf_op jit(solution)/shard_map/convert_element_type | solution.py:412
  536.0 3.3 copy-done.18
  539.3 9.5 fusion.291
  551.9 3.0 dot_general.271
  554.8 3.2 dot_general.291
  558.0 86.7 %reduce-scatter.6.cloned.1.call-done = f32[128,640]{1,0:T(8,128)} async-done(((f32[4096,640]{1,0:T(8,128)}), f32[128,640]{1,0:T(8,128)}) %reduce-scatter.6.cloned.1.call-update) | async-done | bytes 327696 | tf_op jit(solution)/shard_map/reduce_scatter | solution.py:413
  649.9 4.1 fusion.79
  704.4 4.8 copy.405
  709.2 9.2 copy.347
  721.6 4.6 copy.345
  729.7 4.5 copy.358
  735.5 5.3 copy.407
  740.9 9.2 copy.360
  750.9 2.8 constant_dynamic-update-slice_fusion.10
  756.7 4.0 constant_dynamic-update-slice_fusion.8
  760.8 3.6 constant_dynamic-update-slice_fusion.7
  776.6 3.8 constant_dynamic-update-slice_fusion.1
  780.4 3.7 constant_dynamic-update-slice_fusion
  784.1 41.1 %gather_fusion.2 = f32[800,128,128]{2,1,0:T(8,128)} fusion(f32[780,128,128]{2,1,0:T(8,128)} %constant_dynamic-update-slice_fusion, s32[1024]{0:T(1024)S(1)} %copy-done.126), kind=kCustom, calls=%fused_computation.2 | custom fusion | bytes 104860800 | tf_op jit(solution)/shard_map/jit(_take)/gather | solution.py:445
  825.1 35.4 %broadcast_select_fusion = f32[800,128,128]{2,1,0:T(8,128)} fusion(f32[800,128,128]{2,1,0:T(8,128)} %gather_fusion.2, pred[800]{0:T(1024)(128)(4,1)S(1)} %copy-done.182), kind=kLoop, calls=%fused_computation.8 | loop fusion | flops 13107200 | bytes 104858400 | tf_op jit(solution)/shard_map/jit(_take)/select_n | solution.py:445
  861.3 11.8 fusion.10
  873.1 65.9 %scatter_custom_fusion.1 = f32[1024,640]{1,0:T(8,128)} fusion(f32[1024,640]{1,0:T(8,128)} %fusion.10, s32[8192]{0:T(1024)S(1)} %bitcast.933, bf16[8192,640]{1,0:T(8,128)(2,1)} %all-gather.19.cloned.1.call-done, f32[]{:T(128)} %constant.47.clone.1, pred[8192]{0:T(1024)(128)(4,1)S(1)} %copy-done.109), kind=kCustom, calls=%fused_computation.9 | custom fusion | flops 15728640 | bytes 13115904 | tf_op jit(solution)/shard_map/scatter-add | solution.py:439
  939.1 148.4 %reduce-scatter.8.cloned.1.call-done = f32[25,128,128]{2,1,0:T(8,128)} async-done(((f32[800,128,128]{2,1,0:T(8,128)}), f32[25,128,128]{2,1,0:T(8,128)}) %reduce-scatter.8.cloned.1.call-update) | async-done | bytes 1638416 | tf_op jit(solution)/shard_map/reduce_scatter | solution.py:456
  1087.9 18.7 %all-reduce = (f32[]{:T(128)}, f32[14,640]{1,0:T(8,128)S(1)}) all-reduce(f32[]{:T(128)} %get-tuple-element.84, f32[14,640]{1,0:T(8,128)S(1)} %stack.67), channel_id=1, replica_groups=mesh['sub'=4,'tok_0'=4,'tok_1'=4,'tok_2'=2] {'sub'}, use_global_device_ids=true, to_apply=%region_34.35 | all-reduce | flops 8961 | bytes 71688 | tf_op jit(solution)/shard_map/psum | solution.py:457
  1106.6 17.3 %psum.53 = f32[14,640]{1,0:T(8,128)S(1)} all-reduce(f32[14,640]{1,0:T(8,128)S(1)} %get-tuple-element.57), channel_id=1, replica_groups=mesh['sub'=4,'tok_0'=4,'tok_1'=4,'tok_2'=2] {'tok_0'}, use_global_device_ids=true, to_apply=%region_76.77 | all-reduce | flops 8960 | bytes 71680 | tf_op jit(solution)/shard_map/psum | solution.py:117
  1123.9 15.5 %psum.54 = f32[14,640]{1,0:T(8,128)S(1)} all-reduce(f32[14,640]{1,0:T(8,128)S(1)} %psum.53), channel_id=1, replica_groups=mesh['sub'=4,'tok_0'=4,'tok_1'=4,'tok_2'=2] {'tok_1'}, use_global_device_ids=true, to_apply=%region_77.78 | all-reduce | flops 8960 | bytes 71680 | tf_op jit(solution)/shard_map/psum | solution.py:117
  1139.5 3.5 psum.55
  1143.0 38.6 %all-reduce.4.cloned.1.call-done = (f32[25,128,128]{2,1,0:T(8,128)}, f32[1024,640]{1,0:T(8,128)}) async-done(((f32[25,128,128]{2,1,0:T(8,128)}, f32[1024,640]{1,0:T(8,128)}), (f32[25,128,128]{2,1,0:T(8,128)}, f32[1024,640]{1,0:T(8,128)})) %all-reduce.4.cloned.1.call-update) | async-done | bytes 4259856 | tf_op jit(solution)/shard_map/psum | solution.py:457
  1181.6 3.1 multiply_reduce_fusion.1
  1187.7 7.4 all-to-all-start.1
  1195.7 6.7 all-to-all-done.1
  1204.5 5.5 multiply_add_fusion.1
  1210.0 4.7 multiply_add_fusion.2
  1216.6 4.6 multiply_subtract_fusion
  1223.1 3.2 multiply_subtract_fusion.1
  (634 shorter events, 176.8 us)
Async XLA Ops:
  8.0 1213.1 %copy-start = (f32[25,128,128]{2,1,0:T(8,128)S(1)}, f32[25,128,128]{2,1,0:T(8,128)}, u32[]{:S(2)}) copy-start(f32[25,128,128]{2,1,0:T(8,128)} %param.30) | copy-start | bytes 4915204
  8.1 99.1 %all-gather.21.cloned.1.call-start = ((), (), s32[]{:S(2)}) async-start(), calls=%async_computation.11 | async-start | bytes 13926400 | tf_op jit(solution)/shard_map/all_gather | solution.py:56
  10.7 172.4 %reduce-scatter.4.cloned.1.call-start = ((), (), s32[]{:S(2)}) async-start(), calls=%async_computation.5 | async-start | bytes 10813440 | tf_op jit(solution)/shard_map/reduce_scatter | solution.py:369
  36.7 36.9 %copy-start.91 = (s32[32,1,512]{2,0,1:T(8,128)}, s32[32,1,512]{2,0,1:T(8,128)S(1)}, u32[]{:S(2)}) copy-start(s32[32,1,512]{2,0,1:T(8,128)S(1)} %copy.526) | copy-start | bytes 196612
  39.4 34.2 %copy-start.108 = (pred[8192]{0:T(1024)(128)(4,1)}, pred[8192]{0:T(1024)(128)(4,1)S(1)}, u32[]{:S(2)}) copy-start(pred[8192]{0:T(1024)(128)(4,1)S(1)} %and.31) | copy-start | bytes 24580
  85.5 102.7 %all-gather.15.cloned.1.call-start = ((), (), s32[]{:S(2)}) async-start(), calls=%async_computation.6 | async-start | bytes 39321600 | tf_op jit(solution)/shard_map/all_gather | solution.py:56
  107.1 10.6 copy-start.105
  107.2 314.4 %all-gather.17.cloned.1.call-start = ((), (), s32[]{:S(2)}) async-start(), calls=%async_computation.7 | async-start | bytes 10813440 | tf_op jit(solution)/shard_map/all_gather | solution.py:77
  116.3 170.6 %copy-start.146 = (f32[8]{0:T(128)}, f32[8]{0:T(128)S(1)}, u32[]{:S(2)}) copy-start(f32[8]{0:T(128)S(1)} %fusion.240) | copy-start | bytes 100
  118.4 139.2 %copy-start.117 = (f32[640]{0:T(1024)}, f32[640]{0:T(1024)S(1)}, u32[]{:S(2)}) copy-start(f32[640]{0:T(1024)S(1)} %get-tuple-element.46) | copy-start | bytes 7684
  118.4 139.2 %copy-start.124 = (f32[640]{0:T(1024)}, f32[640]{0:T(1024)S(1)}, u32[]{:S(2)}) copy-start(f32[640]{0:T(1024)S(1)} %get-tuple-element.45) | copy-start | bytes 7684
  118.4 157.2 %copy-start.115 = (f32[640]{0:T(1024)}, f32[640]{0:T(1024)S(1)}, u32[]{:S(2)}) copy-start(f32[640]{0:T(1024)S(1)} %get-tuple-element.44) | copy-start | bytes 7684
  118.4 157.2 %copy-start.123 = (f32[640]{0:T(1024)}, f32[640]{0:T(1024)S(1)}, u32[]{:S(2)}) copy-start(f32[640]{0:T(1024)S(1)} %get-tuple-element.43) | copy-start | bytes 7684
  118.6 167.1 %copy-start.130 = (pred[128,128]{0,1:T(8,128)(4,1)}, pred[128,128]{0,1:T(8,128)(4,1)S(1)}, u32[]{:S(2)}) copy-start(pred[128,128]{0,1:T(8,128)(4,1)S(1)} %get-tuple-element.147) | copy-start | bytes 49156
  186.1 83.0 %copy-start.21 = (f32[128,640]{1,0:T(8,128)}, f32[128,640]{1,0:T(8,128)S(1)}, u32[]{:S(2)}) copy-start(f32[128,640]{1,0:T(8,128)S(1)} %get-tuple-element.110) | copy-start | bytes 983044
  186.7 70.9 %copy-start.156 = (f32[128]{0:T(128)}, f32[128]{0:T(128)S(1)}, u32[]{:S(2)}) copy-start(f32[128]{0:T(128)S(1)} %broadcast_divide_fusion.9) | copy-start | bytes 1540
  188.1 69.5 %copy-start.160 = (f32[128]{0:T(128)}, f32[128]{0:T(128)S(1)}, u32[]{:S(2)}) copy-start(f32[128]{0:T(128)S(1)} %get-tuple-element.107) | copy-start | bytes 1540
  290.9 11.5 copy-start.72
  294.3 14.7 %copy-start.132 = (f32[128]{0:T(128)}, f32[128]{0:T(128)S(1)}, u32[]{:S(2)}) copy-start(f32[128]{0:T(128)S(1)} %broadcast_divide_fusion.7) | copy-start | bytes 1540
  295.7 13.3 %copy-start.138 = (f32[128]{0:T(128)}, f32[128]{0:T(128)S(1)}, u32[]{:S(2)}) copy-start(f32[128]{0:T(128)S(1)} %get-tuple-element.102) | copy-start | bytes 1540
  328.2 8.6 copy-start.82
  330.7 12.6 %copy-start.135 = (f32[128]{0:T(128)}, f32[128]{0:T(128)S(1)}, u32[]{:S(2)}) copy-start(f32[128]{0:T(128)S(1)} %broadcast_divide_fusion.4) | copy-start | bytes 1540
  332.2 11.1 copy-start.141
  349.0 84.7 %copy-start.144 = (f32[128]{0:T(128)}, f32[128]{0:T(128)S(1)}, u32[]{:S(2)}) copy-start(f32[128]{0:T(128)S(1)} %broadcast_divide_fusion.3) | copy-start | bytes 1540
  350.3 83.4 %copy-start.145 = (f32[128]{0:T(128)}, f32[128]{0:T(128)S(1)}, u32[]{:S(2)}) copy-start(f32[128]{0:T(128)S(1)} %get-tuple-element.94) | copy-start | bytes 1540
  453.8 36.1 %copy-start.99 = (s32[4096]{0:T(1024)S(1)}, s32[4096]{0:T(1024)}, u32[]{:S(2)}) copy-start(s32[4096]{0:T(1024)} %slice_bitcast_fusion.34) | copy-start | bytes 49156
  453.8 36.2 %copy-start.120 = (s32[1024]{0:T(1024)S(1)}, s32[1024]{0:T(1024)}, u32[]{:S(2)}) copy-start(s32[1024]{0:T(1024)} %iota_add_fusion) | copy-start | bytes 12292
  490.0 18.8 %copy-start.92 = (s32[32,1,512]{2,0,1:T(8,128)S(1)}, s32[32,1,512]{2,0,1:T(8,128)}, u32[]{:S(2)}) copy-start(s32[32,1,512]{2,0,1:T(8,128)} %copy-done.91) | copy-start | bytes 196612
  490.0 33.2 %copy-start.100 = (s32[4096]{0:T(1024)S(1)}, s32[4096]{0:T(1024)}, u32[]{:S(2)}) copy-start(s32[4096]{0:T(1024)} %slice_bitcast_fusion.34) | copy-start | bytes 49156
  490.0 33.2 %copy-start.121 = (s32[1024]{0:T(1024)S(1)}, s32[1024]{0:T(1024)}, u32[]{:S(2)}) copy-start(s32[1024]{0:T(1024)} %iota_add_fusion) | copy-start | bytes 12292
  503.7 16.8 %all-to-all-start = ((f32[32,1,4096]{2,1,0:T(1,128)}), f32[32,1,4096]{2,1,0:T(1,128)}, u32[]{:S(2)}, u32[]{:S(2)}) async-start(f32[32,1,4096]{2,1,0:T(1,128)} %broadcast_in_dim.102), calls=%async_computation.1 | async-start | bytes 1048576 | tf_op jit(solution)/shard_map/all_to_all | solution.py:108
  508.8 135.9 %reduce-scatter.6.cloned.1.call-start = ((), (), s32[]{:S(2)}) async-start(), calls=%async_computation.8 | async-start | bytes 10813440 | tf_op jit(solution)/shard_map/reduce_scatter | solution.py:413
  548.8 324.3 %all-gather.19.cloned.1.call-start = ((), (), s32[]{:S(2)}) async-start(), calls=%async_computation.10 | async-start | bytes 10813440 | tf_op jit(solution)/shard_map/all_gather | solution.py:438
  551.9 98.0 %copy-start.10 = (f32[128,3072]{1,0:T(8,128)S(1)}, f32[128,3072]{1,0:T(8,128)}, u32[]{:S(2)}) copy-start(f32[128,3072]{1,0:T(8,128)} %copy-done.9) | copy-start | bytes 4718596
  649.2 8.5 copy-start.37
  649.9 7.9 copy-start.183
  685.5 402.0 %reduce-scatter.8.cloned.1.call-start = ((), (), s32[]{:S(2)}) async-start(), calls=%async_computation.9 | async-start | bytes 54067200 | tf_op jit(solution)/shard_map/reduce_scatter | solution.py:456
  709.2 9.2 copy-start.70
  709.2 9.2 copy-start.98
  709.2 9.2 copy-start.104
  709.2 9.2 copy-start.134
  709.2 9.2 copy-start.140
  740.9 9.2 copy-start.54
  740.9 9.2 copy-start.75
  784.1 41.1 %copy-start.182 = (pred[800]{0:T(1024)(128)(4,1)S(1)}, pred[800]{0:T(1024)(128)(4,1)}, u32[]{:S(2)}) copy-start(pred[800]{0:T(1024)(128)(4,1)} %compare_and_fusion.2) | copy-start | bytes 2404
  860.5 321.1 %all-reduce.4.cloned.1.call-start = ((), (), s32[]{:S(2)}) async-start(), calls=%async_computation.12 | async-start | bytes 8519680 | tf_op jit(solution)/shard_map/psum | solution.py:457
  861.3 11.8 copy-start.109
  939.0 148.5 %copy-start.181 = (f32[640]{0:T(1024)S(1)}, f32[640]{0:T(1024)}, u32[]{:S(2)}) copy-start(f32[640]{0:T(1024)} %get-tuple-element.19) | copy-start | bytes 7684
  939.0 148.6 %copy-start.180 = (f32[640]{0:T(1024)S(1)}, f32[640]{0:T(1024)}, u32[]{:S(2)}) copy-start(f32[640]{0:T(1024)} %get-tuple-element.30) | copy-start | bytes 7684
  939.0 148.6 %copy-start.179 = (f32[640]{0:T(1024)S(1)}, f32[640]{0:T(1024)}, u32[]{:S(2)}) copy-start(f32[640]{0:T(1024)} %get-tuple-element.25) | copy-start | bytes 7684
  939.0 148.6 %copy-start.178 = (f32[640]{0:T(1024)S(1)}, f32[640]{0:T(1024)}, u32[]{:S(2)}) copy-start(f32[640]{0:T(1024)} %get-tuple-element.33) | copy-start | bytes 7684
  939.0 148.6 %copy-start.177 = (f32[640]{0:T(1024)S(1)}, f32[640]{0:T(1024)}, u32[]{:S(2)}) copy-start(f32[640]{0:T(1024)} %get-tuple-element.50) | copy-start | bytes 7684
  939.0 148.6 %copy-start.176 = (f32[640]{0:T(1024)S(1)}, f32[640]{0:T(1024)}, u32[]{:S(2)}) copy-start(f32[640]{0:T(1024)} %get-tuple-element.48) | copy-start | bytes 7684
  939.0 148.6 %copy-start.175 = (f32[640]{0:T(1024)S(1)}, f32[640]{0:T(1024)}, u32[]{:S(2)}) copy-start(f32[640]{0:T(1024)} %get-tuple-element.23) | copy-start | bytes 7684
  939.1 148.7 %copy-start.174 = (f32[640]{0:T(1024)S(1)}, f32[640]{0:T(1024)}, u32[]{:S(2)}) copy-start(f32[640]{0:T(1024)} %get-tuple-element.32) | copy-start | bytes 7684
  939.1 148.7 %copy-start.173 = (f32[640]{0:T(1024)S(1)}, f32[640]{0:T(1024)}, u32[]{:S(2)}) copy-start(f32[640]{0:T(1024)} %get-tuple-element.21) | copy-start | bytes 7684
  939.1 148.7 %copy-start.172 = (f32[640]{0:T(1024)S(1)}, f32[640]{0:T(1024)}, u32[]{:S(2)}) copy-start(f32[640]{0:T(1024)} %get-tuple-element.31) | copy-start | bytes 7684
  939.1 148.7 %copy-start.171 = (f32[640]{0:T(1024)S(1)}, f32[640]{0:T(1024)}, u32[]{:S(2)}) copy-start(f32[640]{0:T(1024)} %get-tuple-element.15) | copy-start | bytes 7684
  939.1 148.7 %copy-start.170 = (f32[640]{0:T(1024)S(1)}, f32[640]{0:T(1024)}, u32[]{:S(2)}) copy-start(f32[640]{0:T(1024)} %get-tuple-element.28) | copy-start | bytes 7684
  939.1 148.7 %copy-start.128 = (f32[640]{0:T(1024)S(1)}, f32[640]{0:T(1024)}, u32[]{:S(2)}) copy-start(f32[640]{0:T(1024)} %get-tuple-element.13) | copy-start | bytes 7684
  939.1 148.7 %copy-start.127 = (f32[640]{0:T(1024)S(1)}, f32[640]{0:T(1024)}, u32[]{:S(2)}) copy-start(f32[640]{0:T(1024)} %get-tuple-element.27) | copy-start | bytes 7684
  1187.7 14.8 %all-to-all-start.1 = ((f32[32,1,1]{2,1,0:T(1,128)}), f32[32,1,1]{2,1,0:T(1,128)S(1)}, u32[]{:S(2)}, u32[]{:S(2)}) async-start(f32[32,1,1]{2,1,0:T(1,128)} %broadcast_in_dim.120), calls=%async_computation.4 | async-start | bytes 32768 | tf_op jit(solution)/shard_map/all_to_all | solution.py:108
  1204.5 10.2 copy-start.58
  1204.5 11.7 copy-start.52
  (150 other events, 492.8 us)
Sparse Core Ops, SparseCore 0:
  11.8 95.2 all-gather.20
  108.9 46.0 all-gather.14
  1087.7 93.8 all-reduce.3
Sparse Core Ops, SparseCore 1:
  85.5 97.5 reduce-scatter.3
  366.0 55.5 all-gather.16
  548.9 95.7 reduce-scatter.5
  685.6 57.1 all-gather.18
  860.6 226.9 reduce-scatter.7
where the time goes:
time: 1250 us; the launch traced here: 1230 us
  waiting for transfers between devices  432 us (35%)
  local copies, waits for them, and re-layouts  304 us (24%)
  other arithmetic  223 us (18%)
  blocking collectives  122 us (10%)
  matrix products  120 us (10%)
  between operations  22.2 us (2%)
  starting transfers between devices  12.8 us (1%)
    reduce_scatter x1, waiting for transfers between devices, on_device(): own = lax.psum_scatter(slot_grads, TOK, scatter_dimension=0, tiled=True)  148 us
    reduce_scatter x1, waiting for transfers between devices, on_device(): lax.psum_scatter(jnp.dot(back, table_low, preferred_element_type=wide_typ...  86.7 us
    scatter-add x1, other arithmetic, on_device(): jax.ops.segment_sum(jnp.where(in_shard[:, None], all_rows.astype(jnp.floa...  65.9 us
    reduce_scatter x1, waiting for transfers between devices, on_device(): lax.psum_scatter(picked.astype(jnp.bfloat16), TOK, scatter_dimension=0, t...  64.5 us
    unnamed x423, local copies, waits for them, and re-layouts  56.1 us
    all_gather x1, waiting for transfers between devices, sent_together(): lax.all_gather(both, axis, axis=dim, tiled=True)  53.8 us
    gather x1, local copies, waits for them, and re-layouts, on_device(): jnp.take(block_grads, slot_block, axis=0, mode='fill', fill_value=0.0)  41.1 us
    psum x1, waiting for transfers between devices, on_device(): own, table_grad, loss_sum = lax.psum((own, table_grad, loss_group), 'sub')  38.6 us
  transfers between devices with their start and end apart: 10, of which 8 were waited for; matrix products, arithmetic and copies ran while one was open for 26% of the time, Pallas kernels for 0%

commit v1 on v0

--- a/solution.py
+++ b/solution.py
@@ -16,7 +16,6 @@
 HALF = 128
 NBLK = 780
 TOK = ("tok_0", "tok_1", "tok_2")
-SUB_TOK = ("sub", "tok_0", "tok_1", "tok_2")
 
 
 eps_norm = 1e-05
@@ -34,88 +33,20 @@
 wide_type = jnp.float32
 
 
-def joined_along(tiles, dim):
-    tiles = jnp.moveaxis(tiles, 0, dim)
-    dims = tiles.shape
-    return tiles.reshape(*dims[:dim], dims[dim] * dims[dim + 1], *dims[dim + 2 :])
-
-
-def gather_packed(arrays, axis, dims):
-    vector = jnp.concatenate([a.reshape(-1) for a in arrays])
-    lines, at, outs = (lax.all_gather(vector, axis), 0, [])
-    for a, dim in zip(arrays, dims):
-        tiles = lines[:, at : at + a.size].reshape(-1, *a.shape)
-        outs.append(joined_along(tiles, dim))
-        at += a.size
-    return tuple(outs)
-
-
-def all_blocks(value, axes, turns):
-    tiles = value[None]
-    for k in turns:
-        tiles = lax.all_gather(tiles, axes[k], axis=0, tiled=True)
-    held = [lax.axis_size(axes[k]) for k in reversed(turns)]
-    tiles = tiles.reshape(*held, *value.shape)
-    turned = sorted(range(len(turns)), key=lambda place: turns[len(turns) - 1 - place])
-    return tiles.transpose(*turned, *range(len(turns), tiles.ndim)).reshape(-1, *value.shape)
-
-
-def whole_of(value, axes, turns, dim):
-    return joined_along(all_blocks(value, axes, turns), dim)
-
-
-def broadcast(value, axis, root):
-    return lax.dynamic_index_in_dim(lax.all_gather(value, axis), root, 0, keepdims=False)
-
-
-def sent_together(arrays, axis, dim, along):
-    ends, at = ([], 0)
-    for a in arrays[:-1]:
-        at += a.shape[along]
-        ends.append(at)
-    both = jnp.concatenate(arrays, axis=along)
-    return tuple(jnp.split(lax.all_gather(both, axis, axis=dim, tiled=True), ends, axis=along))
-
-
-def gathered_once(value, axis):
-    leaves = jax.tree.leaves(value)
-    turns = sorted(range(len(leaves)), key=lambda k: -leaves[k].size)
-    width = (1, *leaves[turns[0]].shape)[-1]
-    lines = [
-        jnp.pad(leaves[k].reshape(-1), (0, -leaves[k].size % width)).reshape(-1, width)
-        for k in turns
-    ]
-    both, at, found = (lax.all_gather(jnp.concatenate(lines), axis), 0, {})
-    for k, line in zip(turns, lines):
-        section = both[:, at : at + len(line)].reshape(len(both), -1)
-        found[k] = section[:, : leaves[k].size].reshape(-1, *leaves[k].shape)
-        at += len(line)
-    numbers = iter(range(len(leaves)))
-    return jax.tree.map(lambda _: found[next(numbers)], value)
-
-
-def joined_all(value, axes, combine):
-    for axis in axes:
-        pieces = gathered_once(value, axis)
-        value = jax.tree.map(lambda part: part[0], pieces)
-        for k in range(1, lax.axis_size(axis)):
-            value = combine(value, jax.tree.map(lambda part: part[k], pieces))
-    return value
-
-
-def copy_for_each(value, axis):
-    copies = jnp.broadcast_to(value, (lax.axis_size(axis), *value.shape))
-    return lax.all_to_all(copies, axis, split_axis=0, concat_axis=0, tiled=True)
-
-
-def of_everyone(value, axis):
-    return copy_for_each(value, axis).sum(axis=0)
-
-
-def by_axis(value, axes):
-    for axis in axes:
-        value = lax.psum(value, axis)
-    return value
+def quarter(value, part, count):
+    return lax.dynamic_slice_in_dim(value, part * count, count, 0)
+
+
+def gather_tok(value):
+    return lax.all_gather(value, TOK, axis=0)
+
+
+def scatter_tok(value):
+    return lax.psum_scatter(value, TOK, scatter_dimension=0)
+
+
+def swap_sub(value):
+    return lax.all_to_all(value, "sub", split_axis=0, concat_axis=0, tiled=True)
 
 
 def doc_layout(lengths):
@@ -298,14 +229,6 @@
     d_normed = jnp.einsum("tf,df->td", d_pre, w_up, preferred_element_type=wide_type)
     d_in, g_gain, g_bias = norm_pull(stream, gain, bias, width, active, d_normed)
     return (d_out + d_in, [g_up, g_down], [g_gain, g_bias])
-
-
-def combine_stats(first, second):
-    peak_one = jnp.maximum(first[0], second[0])
-    total_one = first[1] * jnp.exp(first[0] - peak_one) + second[1] * jnp.exp(second[0] - peak_one)
-    peak_two = jnp.maximum(first[2], second[2])
-    total_two = first[3] * jnp.exp(first[2] - peak_two) + second[3] * jnp.exp(second[2] - peak_two)
-    return (peak_one, total_one, peak_two, total_two)
 
 
 def adamw(param, grad, first, second, rate):
@@ -341,19 +264,40 @@
     vec_m,
     vec_v,
 ):
-    half_rows = target_ids.shape[0]
-    shard_rows = table.shape[0]
     group = lax.axis_index("sub")
     place = lax.axis_index(TOK)
+    groups = lax.axis_size("sub")
+    shards = lax.axis_size(TOK)
+    shard_rows = table.shape[0]
+    piece = HALF // groups
     doc_of, offset, inside = doc_layout(doc_lengths)
-    all_ids, all_targets, all_valid = gather_packed((token_ids, target_ids, inside), TOK, (0, 0, 0))
-    weight = all_valid.astype(jnp.float32)
-    token_count = jnp.sum(weight)
-    slots = whole_of(master.astype(low_type), (("tok_0", "tok_1"), "tok_2"), (0, 1), 0)
-    inverse = (
-        jnp.zeros((NBLK + 1,), jnp.int32)
-        .at[slot_block]
-        .set(jnp.arange(slot_block.shape[0], dtype=jnp.int32))[:NBLK]
+    mine = jnp.concatenate(
+        [
+            quarter(token_ids[:HALF], group, piece),
+            quarter(token_ids[HALF:], group, piece),
+            quarter(jnp.where(inside > 0, target_ids, -1), group, piece),
+            jnp.broadcast_to(jnp.sum(inside), (HALF - 3 * piece,)),
+        ]
+    )
+    table_low = table.astype(low_type)
+    heads_up = gather_tok(mine)
+    slots = gather_tok(master.astype(low_type)).reshape(-1, BLK, BLK)
+    all_targets = heads_up[:, 2 * piece : 3 * piece]
+    weight = (all_targets >= 0).astype(jnp.float32)
+    token_count = jnp.sum(heads_up[:, 3 * piece]).astype(jnp.float32)
+    first_row = place * shard_rows
+    local = (heads_up[:, : 2 * piece] - first_row).reshape(-1)
+    picks = (local[:, None] == jnp.arange(shard_rows, dtype=jnp.int32)).astype(low_type)
+    picked = matmul(picks, table_low).astype(low_type).reshape(shards, 2 * piece, D)
+    rows = lax.all_gather(scatter_tok(picked), "sub").astype(jnp.float32)
+    rows = rows.reshape(groups, 2, piece, D).transpose(1, 0, 2, 3).reshape(2, HALF, D)
+    inverse = jnp.sum(
+        jnp.where(
+            slot_block[None, :] == jnp.arange(NBLK, dtype=jnp.int32)[:, None],
+            jnp.arange(slot_block.shape[0], dtype=jnp.int32)[None, :],
+            0,
+        ),
+        1,
     )
     mats = unpack(slots[inverse])
     width = jnp.repeat(width_tiles[group], BLK).astype(jnp.float32)
@@ -361,17 +305,9 @@
     head_keep = head_mask[group].astype(jnp.float32)
     unit_keep = jnp.repeat(ffn_tiles[group], BLK).astype(jnp.float32)
     masks = (width, active, head_keep, unit_keep)
-    table_low = table.astype(low_type)
-    local = all_ids - place * shard_rows
-    in_shard = (local >= 0) & (local < shard_rows)
-    local = jnp.clip(local, 0, shard_rows - 1)
-    picked = jnp.where(in_shard[:, None], table_low[local].astype(jnp.float32), 0.0)
-    rows = lax.psum_scatter(
-        picked.astype(jnp.bfloat16), TOK, scatter_dimension=0, tiled=True
-    ).astype(jnp.float32)
     wave = sinusoid(offset)
-    source = (math.sqrt(D) * rows[:half_rows] + wave) * width
-    target = (math.sqrt(D) * rows[half_rows:] + wave) * width
+    source = (math.sqrt(D) * rows[0] + wave) * width
+    target = (math.sqrt(D) * rows[1] + wave) * width
     same = doc_of[:, None] == doc_of[None, :]
     causal = same & (offset[None, :] <= offset[:, None])
     enc_one, kept_one = self_block(source, vec[0], vec[1], mats[0], mats[1], masks, same)
@@ -383,39 +319,42 @@
     )
     dec_three, kept_five = feed_block(dec_two, vec[10], vec[11], mats[9], mats[10], masks)
     final = norm(dec_three, vec[12], vec[13], width, active).astype(low_type)
-    teacher_final = broadcast(final, "sub", 0)
-    hidden, teacher_hidden = sent_together((final, teacher_final), TOK, 0, 1)
+    hidden = gather_tok(swap_sub(final.reshape(groups, piece, D))).reshape(-1, D)
     logits = jnp.einsum("td,vd->tv", hidden, table_low, preferred_element_type=wide_type)
-    teacher = jnp.einsum("td,vd->tv", teacher_hidden, table_low, preferred_element_type=wide_type)
-    peak_student = jnp.max(logits, 1)
-    total_student = jnp.sum(jnp.exp(logits - peak_student[:, None]), 1)
-    peak_teacher = jnp.max(teacher, 1)
-    total_teacher = jnp.sum(jnp.exp(teacher - peak_teacher[:, None]), 1)
-    peak_student, total_student, peak_teacher, total_teacher = joined_all(
-        (peak_student, total_student, peak_teacher, total_teacher), TOK, combine_stats
-    )
-    student_log = peak_student + jnp.log(total_student)
-    teacher_log = peak_teacher + jnp.log(total_teacher)
-    teacher_on = (group > 0).astype(jnp.float32)
-    columns = jnp.arange(shard_rows, dtype=jnp.int32) + place * shard_rows
-    target_dist = jnp.where(
-        group > 0,
-        jnp.exp(teacher - teacher_log[:, None]),
-        (all_targets[:, None] == columns[None, :]).astype(jnp.float32),
-    )
-    term = jnp.sum(target_dist * (teacher_on * teacher - logits), 1)
-    term = of_everyone(term, TOK)
-    token_loss = student_log + term - teacher_on * teacher_log
-    loss_group = jnp.sum(token_loss * weight)
-    back = (
-        (jnp.exp(logits - student_log[:, None]) - target_dist) * (weight / token_count)[:, None]
-    ).astype(low_type)
-    d_final = lax.psum_scatter(
-        jnp.dot(back, table_low, preferred_element_type=wide_type),
-        TOK,
-        scatter_dimension=0,
-        tiled=True,
-    )
+    logits = logits.reshape(shards, groups, piece, shard_rows)
+    teacher = logits[:, :1]
+    peak = jnp.max(logits, -1)
+    total = jnp.sum(jnp.exp(logits - peak[..., None]), -1)
+    hits = all_targets[..., None] - first_row == jnp.arange(shard_rows, dtype=jnp.int32)
+    hit = jnp.sum(jnp.where(hits, logits[:, 0], 0.0), -1)
+    gap = jnp.sum(jnp.exp(teacher - peak[:, :1, :, None]) * (teacher - logits[:, 1:]), -1)
+    stats = gather_tok(jnp.concatenate([peak, total, hit[:, None], gap], 1))
+    peaks, totals, extra = jnp.split(stats, [groups, 2 * groups], 2)
+    peak = jnp.max(peaks, 0)
+    rescale = jnp.exp(peaks - peak)
+    total = jnp.sum(totals * rescale, 0)
+    logs = peak + jnp.log(total)
+    hit = jnp.sum(extra[:, :, 0], 0)
+    gap = jnp.sum(extra[:, :, 1:] * rescale[:, :, :1], 0) / total[:, :1]
+    token_loss = logs[:, 0] - hit + jnp.sum(logs[:, 1:] + gap - logs[:, :1], 1)
+    loss_part = jnp.sum(token_loss * weight)
+    target_dist = jnp.concatenate(
+        [
+            hits.astype(jnp.float32)[:, None],
+            jnp.broadcast_to(
+                jnp.exp(teacher - logs[:, :1, :, None]),
+                (shards, groups - 1, piece, shard_rows),
+            ),
+        ],
+        1,
+    )
+    back = (jnp.exp(logits - logs[..., None]) - target_dist) * (weight / token_count)[
+        :, None, :, None
+    ]
+    back = back.astype(low_type).reshape(-1, shard_rows)
+    d_hidden = matmul(back, table_low).astype(low_type).reshape(shards, groups * piece, D)
+    d_final = scatter_tok(d_hidden).reshape(groups, piece, D)
+    d_final = swap_sub(d_final).reshape(HALF, D).astype(jnp.float32)
     table_grad = jnp.einsum("tv,td->vd", back, hidden, preferred_element_type=wide_type)
     d_three, g_twelve, g_thirteen = norm_pull(dec_three, vec[12], vec[13], width, active, d_final)
     d_two, grads_dec_feed, gains_five = feed_back(
@@ -434,14 +373,16 @@
     d_source, grads_enc_self, gains_one = self_back(
         d_enc_one, kept_one, vec[0], vec[1], mats[0], mats[1], masks
     )
-    d_rows = (jnp.concatenate([d_source, d_target], 0) * width * math.sqrt(D)).astype(low_type)
-    all_rows = lax.all_gather(d_rows, TOK, axis=0, tiled=True)
-    table_grad = table_grad + jax.ops.segment_sum(
-        jnp.where(in_shard[:, None], all_rows.astype(jnp.float32), 0.0), local, shard_rows
+    d_rows = (jnp.stack([d_source, d_target], 0) * width * math.sqrt(D)).astype(low_type)
+    d_rows = d_rows.reshape(2, groups, piece, D).transpose(1, 0, 2, 3)
+    d_rows = jnp.sum(swap_sub(d_rows).astype(jnp.float32), 0).astype(low_type)
+    all_rows = gather_tok(d_rows).reshape(-1, D)
+    table_grad = table_grad + jnp.einsum(
+        "rv,rd->vd", picks, all_rows, preferred_element_type=wide_type
     )
     block_grads = pack(
         grads_enc_self + grads_enc_feed + grads_dec_self + grads_cross + grads_dec_feed
-    )
+    ).astype(low_type)
     slot_grads = jnp.take(block_grads, slot_block, axis=0, mode="fill", fill_value=0.0)
     vec_grad = jnp.stack(
         gains_one
@@ -453,11 +394,13 @@
         + [g_twelve, g_thirteen],
         0,
     )
-    own = lax.psum_scatter(slot_grads, TOK, scatter_dimension=0, tiled=True)
-    own, table_grad, loss_sum = lax.psum((own, table_grad, loss_group), "sub")
-    vec_grad = by_axis(vec_grad, SUB_TOK)
-    square = of_everyone(jnp.sum(own * own) + jnp.sum(table_grad * table_grad), TOK)
-    grad_norm = jnp.sqrt(square + jnp.sum(vec_grad * vec_grad))
+    own = scatter_tok(slot_grads.reshape(shards, -1, BLK, BLK)).astype(jnp.float32)
+    own, table_grad, vec_grad, loss_sum = lax.psum((own, table_grad, vec_grad, loss_part), "sub")
+    square = jnp.sum(own * own) + jnp.sum(table_grad * table_grad)
+    small = jnp.concatenate([vec_grad.reshape(-1), jnp.broadcast_to(square, (BLK,))])
+    small = jnp.sum(gather_tok(small), 0)
+    vec_grad = small[: vec.size].reshape(vec.shape)
+    grad_norm = jnp.sqrt(small[vec.size] + jnp.sum(vec_grad * vec_grad))
     scale = jnp.minimum(1.0, clip_limit / grad_norm)
     grad = own * scale
     new_left = beta_stat * left_stat + (1.0 - beta_stat) * jnp.einsum(

time: 1250 us -> 1130 us (0.904)
  other arithmetic: 223 us -> 117 us
  waiting for transfers between devices: 432 us -> 531 us
  local copies, waits for them, and re-layouts: 304 us -> 243 us
  blocking collectives: 122 us -> 65.9 us
    all_gather x4 -> x5, waiting for transfers between devices: 75.4 us -> 199 us  [gather_tok(): return lax.all_gather(value, TOK, axis=0)]
    scatter-add x1 -> x0, other arithmetic: 65.9 us -> none  [on_device(): jax.ops.segment_sum(jnp.where(in_shard[:, None], all_rows.astype(jnp.floa...]
    reduce_scatter x3, waiting for transfers between devices: 300 us -> 263 us  [scatter_tok(): return lax.psum_scatter(value, TOK, scatter_dimension=0)]
    psum x4 -> x1, blocking collectives: 55 us -> 19.6 us  [on_device(): lax.psum((own, table_grad, vec_grad, loss_part), 'sub')]
    gather x1 -> x0, local copies, waits for them, and re-layouts: 34.2 us -> none  [on_device(): table_low[local].astype(jnp.float32)]
    all_gather x5 -> x2, blocking collectives: 67.3 us -> 35.9 us  [the longest x1 22.8 us: gather_tok(): return lax.all_gather(value, TOK, axis=0)]
    psum x1, waiting for transfers between devices: 38.6 us -> 66.2 us  [on_device(): lax.psum((own, table_grad, vec_grad, loss_part), 'sub')]
    transpose x4 -> x0, local copies, waits for them, and re-layouts: 26.4 us -> none  [the longest x1 18 us: all_blocks(): tiles.transpose(*turned, *range(len(turns), tiles.ndim))]
  transfers between devices with their start and end apart: 10 -> 11, of which waited for: 8 -> 9; matrix products, arithmetic and copies ran while one was open for 26% -> 17% of each run, Pallas kernels for 0% -> 0%
where the time goes in v1:
time: 1130 us; the launch traced here: 1120 us
  waiting for transfers between devices  531 us (47%)
  local copies, waits for them, and re-layouts  243 us (22%)
  matrix products  131 us (12%)
  other arithmetic  117 us (10%)
  blocking collectives  65.9 us (6%)
  between operations  22.3 us (2%)
    reduce_scatter x3, waiting for transfers between devices, scatter_tok(): return lax.psum_scatter(value, TOK, scatter_dimension=0)  263 us
    all_gather x5, waiting for transfers between devices, gather_tok(): return lax.all_gather(value, TOK, axis=0)  199 us
    psum x1, waiting for transfers between devices, on_device(): lax.psum((own, table_grad, vec_grad, loss_part), 'sub')  66.2 us
    unnamed x384, local copies, waits for them, and re-layouts  49.7 us
    dot_general x13, matrix products, matmul(): return jnp.dot(left, right, preferred_element_type=wide_type)  39.1 us
    reshape x11, local copies, waits for them, and re-layouts, unpack(): part.reshape(rows, cols, BLK, BLK).transpose(0, 2, 1, 3)  35.3 us
    gather x1, local copies, waits for them, and re-layouts, on_device(): mats = unpack(slots[inverse])  29.4 us
    gather x1, local copies, waits for them, and re-layouts, on_device(): jnp.take(block_grads, slot_block, axis=0, mode='fill', fill_value=0.0)  29.3 us
  transfers between devices with their start and end apart: 11, of which 9 were waited for; matrix products, arithmetic and copies ran while one was open for 17% of the time, Pallas kernels for 0%

profile of v1, /device:TPU:0, one launch (start us, length us, event | category | flops | bytes accessed | tf_op | source)
XLA Modules:
  0.0 1119.6 jit_solution(1861533920360820759)
XLA Ops:
  12.4 22.8 %all-gather.6 = s32[32,1,128]{2,1,0:T(1,128)S(1)} all-gather(s32[1,1,128]{2,1,0:T(1,128)S(1)} %add_bitcast_fusion), channel_id=2, replica_groups=mesh['sub'=4,'tok_0'=4,'tok_1'=4,'tok_2'=2] {'tok_0','tok_1','tok_2'}, dimensions={0}, use_global_device_ids=true | all-gather | bytes 16896 | tf_op jit(solution)/shard_map/all_gather | solution.py:41
  35.9 6.8 fusion.42
  57.6 64.6 %reduce-scatter.4.cloned.1.call-done = bf16[1,64,640]{2,1,0:T(8,128)(2,1)} async-done(((bf16[32,64,640]{2,1,0:T(8,128)(2,1)}), bf16[1,64,640]{2,1,0:T(8,128)(2,1)}) %reduce-scatter.4.cloned.1.call-update) | async-done | bytes 81936 | tf_op jit(solution)/shard_map/reduce_scatter | solution.py:45
  122.2 13.1 %all_gather.41 = bf16[4,64,640]{2,1,0:T(8,128)(2,1)S(1)} all-gather(bf16[1,64,640]{2,1,0:T(8,128)(2,1)} %reduce-scatter.4.cloned.1.call-done), channel_id=1, replica_groups=mesh['sub'=4,'tok_0'=4,'tok_1'=4,'tok_2'=2] {'sub'}, dimensions={0}, use_global_device_ids=true | all-gather | bytes 409600 | tf_op jit(solution)/shard_map/all_gather | solution.py:292
  152.4 67.1 %all-gather.14.cloned.1.call-done = bf16[800,128,128]{2,1,0:T(8,128)(2,1)} async-done(((bf16[25,128,128]{2,1,0:T(8,128)(2,1)}), bf16[800,128,128]{2,1,0:T(8,128)(2,1)}) %all-gather.14.cloned.1.call-update) | async-done | bytes 26214416 | tf_op jit(solution)/shard_map/all_gather | solution.py:41
  219.4 29.4 %gather_fusion = bf16[780,128,128]{2,1,0:T(8,128)(2,1)} fusion(bf16[800,128,128]{2,1,0:T(8,128)(2,1)} %all-gather.14.cloned.1.call-done, s32[1024]{0:T(1024)S(1)} %pad_clamp_fusion.1), kind=kCustom, calls=%fused_computation | custom fusion | bytes 51121200 | tf_op jit(solution)/shard_map/gather | solution.py:302
  251.0 6.7 fusion.251
  257.7 10.5 fusion.249
  268.2 2.7 copy.362
  276.5 4.4 copy.368
  280.9 6.9 copy.361
  287.9 4.9 copy.345
  299.4 3.1 fusion.52
  320.1 2.5 copy.360
  331.7 3.1 convolution_convert_fusion.5
  343.0 6.6 copy.369
  349.6 3.1 fusion.18
  356.5 10.4 all_to_all.15
  367.1 45.0 %all-gather.16.cloned.1.call-done = bf16[128,32,640]{2,1,0:T(8,128)(2,1)} async-done(((bf16[4,32,640]{2,1,0:T(8,128)(2,1)}), bf16[128,32,640]{2,1,0:T(8,128)(2,1)}) %all-gather.16.cloned.1.call-update) | async-done | bytes 5242896 | tf_op jit(solution)/shard_map/all_gather | solution.py:41
  412.0 9.7 fusion.257
  421.8 3.0 exponential_reduce_fusion
  434.6 44.1 %all-gather.18.cloned.1.call-done = f32[1024,12,32]{2,0,1:T(8,128)} async-done(((f32[32,12,32]{2,0,1:T(8,128)}), f32[1024,12,32]{2,0,1:T(8,128)}) %all-gather.18.cloned.1.call-update) | async-done | bytes 1572880 | tf_op jit(solution)/shard_map/all_gather | solution.py:41
  478.7 2.7 fusion.252
  481.5 5.5 fusion.59
  487.1 5.0 exponential_bitcast_fusion
  492.2 8.8 broadcast_in_dim.111
  501.0 7.7 fusion.4
  508.7 12.2 %convolution_convert_fusion = bf16[4096,640]{1,0:T(8,128)(2,1)} fusion(bf16[4096,1024]{1,0:T(8,128)(2,1)S(1)} %bitcast.604, f32[1024,640]{1,0:T(8,128)} %param.32), kind=kOutput, calls=%fused_computation.16 | convolution fusion | flops 5371985920 | bytes 16252928 | tf_op jit(solution)/shard_map/dot_general | solution.py:130
  526.1 2.9 dot_general.272
  530.8 73.9 %reduce-scatter.6.cloned.1.call-done = bf16[1,128,640]{2,1,0:T(8,128)(2,1)} async-done(((bf16[32,128,640]{2,1,0:T(8,128)(2,1)}), bf16[1,128,640]{2,1,0:T(8,128)(2,1)}) %reduce-scatter.6.cloned.1.call-update) | async-done | bytes 163856 | tf_op jit(solution)/shard_map/reduce_scatter | solution.py:45
  604.7 4.7 all-to-all-start.1
  613.0 2.5 all-to-all-done.1
  619.3 4.5 fusion.83
  649.7 3.3 convolution_convert_fusion.3
  653.0 3.3 convolution_convert_fusion.1
  656.3 3.2 fusion.61
  662.1 2.8 multiply_reduce_fusion.6
  668.9 3.5 all-to-all-start.2
  672.4 3.2 copy.440
  682.8 6.3 copy.386
  689.1 5.1 copy.441
  694.3 6.6 copy.387
  700.8 4.7 constant_dynamic-update-slice_fusion.7
  706.5 3.2 fusion.62
  710.1 6.3 copy.394
  716.3 5.1 copy.443
  721.5 6.5 copy.395
  728.0 3.2 copy.442
  740.9 2.3 constant_dynamic-update-slice_fusion.1
  746.8 29.3 %gather_fusion.1 = bf16[800,128,128]{2,1,0:T(8,128)(2,1)} fusion(bf16[780,128,128]{2,1,0:T(8,128)(2,1)} %constant_dynamic-update-slice_fusion, s32[1024]{0:T(1024)S(1)} %pad_clamp_fusion), kind=kCustom, calls=%fused_computation.1 | custom fusion | bytes 52432000 | tf_op jit(solution)/shard_map/jit(_take)/gather | solution.py:386
  776.0 17.9 %broadcast_select_fusion = bf16[32,25,128,128]{3,2,1,0:T(8,128)(2,1)} fusion(bf16[32,25,128,128]{3,2,1,0:T(8,128)(2,1)} %bitcast.570, pred[32,25]{1,0:T(8,128)(4,1)S(1)} %broadcast_in_dim.122), kind=kLoop, calls=%fused_computation.5 | loop fusion | flops 13107200 | bytes 52429600 | tf_op jit(solution)/shard_map/jit(_take)/select_n | solution.py:386
  794.7 5.8 fusion.7
  800.4 12.8 %bitcast_add_fusion = f32[1024,640]{1,0:T(8,128)} fusion(f32[1024,640]{1,0:T(8,128)S(1)} %fusion.7, bf16[32,4,32,1024]{3,2,1,0:T(8,128)(2,1)} %copy-done.17, bf16[32,4,32,640]{3,2,1,0:T(8,128)(2,1)} %bitcast.686), kind=kOutput, calls=%fused_computation.61 | convolution fusion | flops 5369364480 | bytes 18874368 | tf_op jit(solution)/shard_map/tv,td->vd/dot_general | solution.py:358
  813.2 124.5 %reduce-scatter.8.cloned.1.call-done = bf16[1,25,128,128]{3,2,1,0:T(8,128)(2,1)} async-done(((bf16[32,25,128,128]{3,2,1,0:T(8,128)(2,1)}), bf16[1,25,128,128]{3,2,1,0:T(8,128)(2,1)}) %reduce-scatter.8.cloned.1.call-update) | async-done | bytes 819216 | tf_op jit(solution)/shard_map/reduce_scatter | solution.py:45
  937.7 2.5 bitcast_convert_fusion
  948.9 19.6 %all-reduce.1 = (f32[]{:T(128)}, f32[8960]{0:T(1024)S(1)}) all-reduce(f32[]{:T(128)} %select_reduce_fusion.2, f32[8960]{0:T(1024)S(1)} %reshape.1326), channel_id=1, replica_groups=mesh['sub'=4,'tok_0'=4,'tok_1'=4,'tok_2'=2] {'sub'}, use_global_device_ids=true, to_apply=%region_38.39 | all-reduce | flops 8961 | bytes 71688 | tf_op jit(solution)/shard_map/psum | solution.py:398
  968.5 66.2 %all-reduce.5.cloned.1.call-done = (f32[25,128,128]{2,1,0:T(8,128)}, f32[1024,640]{1,0:T(8,128)}) async-done(((f32[25,128,128]{2,1,0:T(8,128)}, f32[1024,640]{1,0:T(8,128)}), (f32[25,128,128]{2,1,0:T(8,128)}, f32[1024,640]{1,0:T(8,128)})) %all-reduce.5.cloned.1.call-update) | async-done | bytes 4259856 | tf_op jit(solution)/shard_map/psum | solution.py:398
  1034.6 2.6 multiply_reduce_fusion.1
  1037.2 3.0 multiply_reduce_fusion
  1042.2 43.0 %all-gather.22.cloned.1.call-done = f32[32,1,9088]{2,1,0:T(1,128)} async-done(((f32[1,1,9088]{2,1,0:T(1,128)}), f32[32,1,9088]{2,1,0:T(1,128)}) %all-gather.22.cloned.1.call-update) | async-done | bytes 1163280 | tf_op jit(solution)/shard_map/all_gather | solution.py:41
  1091.7 4.7 multiply_add_fusion.2
  1096.4 4.0 multiply_add_fusion.1
  1102.1 3.2 multiply_subtract_fusion.1
  1105.4 4.6 multiply_subtract_fusion
  (626 shorter events, 184.0 us)
Async XLA Ops:
  7.2 1093.2 %copy-start = (f32[25,128,128]{2,1,0:T(8,128)S(1)}, f32[25,128,128]{2,1,0:T(8,128)}, u32[]{:S(2)}) copy-start(f32[25,128,128]{2,1,0:T(8,128)} %param.30) | copy-start | bytes 4915204
  7.2 115.0 %reduce-scatter.4.cloned.1.call-start = ((), (), s32[]{:S(2)}) async-start(), calls=%async_computation.6 | async-start | bytes 2703360 | tf_op jit(solution)/shard_map/reduce_scatter | solution.py:45
  42.7 176.7 %all-gather.14.cloned.1.call-start = ((), (), s32[]{:S(2)}) async-start(), calls=%async_computation.9 | async-start | bytes 27033600 | tf_op jit(solution)/shard_map/all_gather | solution.py:41
  45.2 366.8 %all-gather.16.cloned.1.call-start = ((), (), s32[]{:S(2)}) async-start(), calls=%async_computation.10 | async-start | bytes 5406720 | tf_op jit(solution)/shard_map/all_gather | solution.py:41
  46.8 103.5 %copy-start.103 = (f32[640]{0:T(1024)}, f32[640]{0:T(1024)S(1)}, u32[]{:S(2)}) copy-start(f32[640]{0:T(1024)S(1)} %get-tuple-element.47) | copy-start | bytes 7684
  46.8 103.5 %copy-start.105 = (f32[640]{0:T(1024)}, f32[640]{0:T(1024)S(1)}, u32[]{:S(2)}) copy-start(f32[640]{0:T(1024)S(1)} %get-tuple-element.49) | copy-start | bytes 7684
  46.8 282.1 %copy-start.109 = (f32[640]{0:T(1024)}, f32[640]{0:T(1024)S(1)}, u32[]{:S(2)}) copy-start(f32[640]{0:T(1024)S(1)} %get-tuple-element.41) | copy-start | bytes 7684
  46.8 284.9 %copy-start.111 = (f32[640]{0:T(1024)}, f32[640]{0:T(1024)S(1)}, u32[]{:S(2)}) copy-start(f32[640]{0:T(1024)S(1)} %get-tuple-element.43) | copy-start | bytes 7684
  46.8 309.6 %copy-start.101 = (f32[640]{0:T(1024)}, f32[640]{0:T(1024)S(1)}, u32[]{:S(2)}) copy-start(f32[640]{0:T(1024)S(1)} %get-tuple-element.37) | copy-start | bytes 7684
  52.9 84.5 %copy-start.38 = (f32[1,4,32,640]{3,2,0,1:T(8,128)}, f32[1,4,32,640]{3,2,0,1:T(8,128)S(1)}, u32[]{:S(2)}) copy-start(f32[1,4,32,640]{3,2,0,1:T(8,128)S(1)} %copy.341) | copy-start | bytes 983044
  257.7 10.5 slice-start.4
  271.5 68.0 %copy-start.14 = (bf16[5,5,128,128]{3,1,2,0:T(8,128)(2,1)}, bf16[5,5,128,128]{3,1,2,0:T(8,128)(2,1)S(1)}, u32[]{:S(2)}) copy-start(bf16[5,5,128,128]{3,1,2,0:T(8,128)(2,1)S(1)} %copy.609) | copy-start | bytes 2457604
  297.3 7.2 copy-start.125
  299.4 7.4 copy-start.143
  310.6 18.3 %copy-start.18 = (f32[128,640]{1,0:T(8,128)}, f32[128,640]{1,0:T(8,128)S(1)}, u32[]{:S(2)}) copy-start(f32[128,640]{1,0:T(8,128)S(1)} %get-tuple-element.162) | copy-start | bytes 983044
  311.3 17.6 %copy-start.153 = (f32[128]{0:T(128)}, f32[128]{0:T(128)S(1)}, u32[]{:S(2)}) copy-start(f32[128]{0:T(128)S(1)} %broadcast_divide_fusion.7) | copy-start | bytes 1540
  313.5 6.6 copy-start.6
  315.0 7.6 copy-start.70
  316.9 7.7 copy-start.9
  320.1 8.8 copy-start.147
  328.9 7.1 copy-start.149
  330.3 7.9 copy-start.151
  341.6 7.9 copy-start.127
  343.0 6.6 copy-start.131
  355.0 12.0 %copy-start.137 = (f32[128]{0:T(128)}, f32[128]{0:T(128)S(1)}, u32[]{:S(2)}) copy-start(f32[128]{0:T(128)S(1)} %broadcast_divide_fusion.5) | copy-start | bytes 1540
  356.4 10.6 copy-start.139
  366.9 111.7 %all-gather.18.cloned.1.call-start = ((), (), s32[]{:S(2)}) async-start(), calls=%async_computation.11 | async-start | bytes 6488064 | tf_op jit(solution)/shard_map/all_gather | solution.py:41
  430.0 174.7 %reduce-scatter.6.cloned.1.call-start = ((), (), s32[]{:S(2)}) async-start(), calls=%async_computation.7 | async-start | bytes 5406720 | tf_op jit(solution)/shard_map/reduce_scatter | solution.py:45
  481.5 19.5 %slice-start = ((s8[16777216]{0:T(1024)(128)(4,1)}), s8[4194304]{0:T(1024)(128)(4,1)S(1)}, s32[]{:S(2)}) async-start(s8[16777216]{0:T(1024)(128)(4,1)} %bitcast.568), calls=%async_computation.15 | async-start | bytes 8388608
  487.1 13.9 %copy-start.68 = (f32[32,4,32]{2,1,0:T(4,128)}, f32[32,4,32]{2,1,0:T(4,128)S(1)}, u32[]{:S(2)}) copy-start(f32[32,4,32]{2,1,0:T(4,128)S(1)} %log_add_fusion) | copy-start | bytes 49156
  487.1 13.8 %slice-start.1 = ((s8[16777216]{0:T(1024)(128)(4,1)}), s8[4194304]{0:T(1024)(128)(4,1)S(1)}, s32[]{:S(2)}) async-start(s8[16777216]{0:T(1024)(128)(4,1)} %bitcast.568), calls=%async_computation.16 | async-start | bytes 8388608
  492.1 8.8 slice-start.2
  492.1 8.8 slice-start.3
  508.7 12.2 %copy-start.17 = (bf16[32,4,32,1024]{3,2,1,0:T(8,128)(2,1)}, bf16[32,4,32,1024]{3,2,1,0:T(8,128)(2,1)S(1)}, u32[]{:S(2)}) copy-start(bf16[32,4,32,1024]{3,2,1,0:T(8,128)(2,1)S(1)} %fusion.4) | copy-start | bytes 25165828
  526.0 83.3 %copy-start.112 = (f32[640]{0:T(1024)S(1)}, f32[640]{0:T(1024)}, u32[]{:S(2)}) copy-start(f32[640]{0:T(1024)} %copy-done.111) | copy-start | bytes 7684
  526.0 83.3 %copy-start.122 = (f32[640]{0:T(1024)S(1)}, f32[640]{0:T(1024)}, u32[]{:S(2)}) copy-start(f32[640]{0:T(1024)} %get-tuple-element.42) | copy-start | bytes 7684
  526.1 83.3 %copy-start.150 = (f32[128]{0:T(128)S(1)}, f32[128]{0:T(128)}, u32[]{:S(2)}) copy-start(f32[128]{0:T(128)} %copy-done.149) | copy-start | bytes 1540
  526.1 83.3 %copy-start.152 = (f32[128]{0:T(128)S(1)}, f32[128]{0:T(128)}, u32[]{:S(2)}) copy-start(f32[128]{0:T(128)} %copy-done.151) | copy-start | bytes 1540
  526.1 89.5 %copy-start.102 = (f32[640]{0:T(1024)S(1)}, f32[640]{0:T(1024)}, u32[]{:S(2)}) copy-start(f32[640]{0:T(1024)} %copy-done.101) | copy-start | bytes 7684
  526.1 89.4 %copy-start.138 = (f32[128]{0:T(128)S(1)}, f32[128]{0:T(128)}, u32[]{:S(2)}) copy-start(f32[128]{0:T(128)} %copy-done.137) | copy-start | bytes 1540
  526.1 89.4 %copy-start.140 = (f32[128]{0:T(128)S(1)}, f32[128]{0:T(128)}, u32[]{:S(2)}) copy-start(f32[128]{0:T(128)} %copy-done.139) | copy-start | bytes 1540
  526.1 90.6 %copy-start.179 = (f32[128]{0:T(128)S(1)}, f32[128]{0:T(128)}, u32[]{:S(2)}) copy-start(f32[128]{0:T(128)} %get-tuple-element.100) | copy-start | bytes 1540
  604.7 10.8 all-to-all-start.1
  668.9 36.6 %all-to-all-start.2 = ((bf16[4,2,32,640]{3,2,1,0:T(8,128)(2,1)}), bf16[4,2,32,640]{3,2,1,0:T(8,128)(2,1)S(1)}, u32[]{:S(2)}, u32[]{:S(2)}) async-start(bf16[4,2,32,640]{3,2,1,0:T(8,128)(2,1)} %fusion.166), calls=%async_computation.5 | async-start | bytes 655360 | tf_op jit(solution)/shard_map/all_to_all | solution.py:49
  672.4 122.1 %all-gather.20.cloned.1.call-start = ((), (), s32[]{:S(2)}) async-start(), calls=%async_computation.12 | async-start | bytes 2703360 | tf_op jit(solution)/shard_map/all_gather | solution.py:41
  706.3 231.4 %reduce-scatter.8.cloned.1.call-start = ((), (), s32[]{:S(2)}) async-start(), calls=%async_computation.8 | async-start | bytes 27033600 | tf_op jit(solution)/shard_map/reduce_scatter | solution.py:45
  794.0 240.7 %all-reduce.5.cloned.1.call-start = ((), (), s32[]{:S(2)}) async-start(), calls=%async_computation.14 | async-start | bytes 8519680 | tf_op jit(solution)/shard_map/psum | solution.py:398
  940.2 6.5 copy-start.69
  940.2 6.5 copy-start.98
  940.2 145.0 %all-gather.22.cloned.1.call-start = ((), (), s32[]{:S(2)}) async-start(), calls=%async_computation.13 | async-start | bytes 1199616 | tf_op jit(solution)/shard_map/all_gather | solution.py:41
  941.8 6.1 copy-start.126
  941.8 6.8 copy-start.162
  941.8 6.8 copy-start.161
  941.9 6.8 copy-start.166
  941.9 6.8 copy-start.165
  941.9 6.8 copy-start.164
  941.9 6.8 copy-start.163
  941.9 6.8 copy-start.170
  941.9 6.8 copy-start.169
  941.9 6.9 copy-start.168
  941.9 6.9 copy-start.167
  1034.6 55.1 %copy-start.2 = (f32[25,128,128]{2,1,0:T(8,128)S(1)}, f32[25,128,128]{2,1,0:T(8,128)}, u32[]{:S(2)}) copy-start(f32[25,128,128]{2,1,0:T(8,128)} %get-tuple-element.65) | copy-start | bytes 4915204
  1091.7 8.7 copy-start.22
  1096.4 8.9 copy-start.49
  (132 other events, 396.6 us)
Sparse Core Ops, SparseCore 0:
  42.8 79.2 reduce-scatter.3
  125.2 94.1 all-gather.13
  367.0 44.9 all-gather.15
  430.1 48.5 all-gather.17
  521.1 83.5 reduce-scatter.5
  706.4 44.2 all-gather.19
  794.1 143.5 reduce-scatter.7
  941.4 93.2 all-reduce.4
  1042.3 42.8 all-gather.21

commit v2 on v1

--- a/solution.py
+++ b/solution.py
@@ -1,8 +1,11 @@
+import functools
 import math
 
 import jax
 import jax.numpy as jnp
 from jax import lax
+from jax.experimental import pallas as pl
+from jax.experimental.pallas import tpu as pltpu
 from jax.sharding import Mesh
 from jax.sharding import PartitionSpec as P
 
@@ -37,16 +40,511 @@
     return lax.dynamic_slice_in_dim(value, part * count, count, 0)
 
 
-def gather_tok(value):
-    return lax.all_gather(value, TOK, axis=0)
-
-
-def scatter_tok(value):
-    return lax.psum_scatter(value, TOK, scatter_dimension=0)
-
-
-def swap_sub(value):
-    return lax.all_to_all(value, "sub", split_axis=0, concat_axis=0, tiled=True)
+MESH = pl.DeviceIdType.MESH
+RING = {"z": "tok_0", "x": "tok_1", "y": "sub"}
+CORE = "tok_2"
+MIB = 1 << 20
+
+
+def around(axis):
+    count = lax.axis_size(axis)
+    me = lax.axis_index(axis)
+    return me, lax.rem(me + 1, count), lax.rem(me + count - 1, count), lax.rem(me + 2, count)
+
+
+def greet(axes):
+    barrier = pltpu.get_barrier_semaphore()
+    peers = 0
+    for axis in axes:
+        me = lax.axis_index(axis)
+        count = lax.axis_size(axis)
+        for k in range(1, count):
+            pl.semaphore_signal(
+                barrier,
+                inc=1,
+                device_id={axis: lax.rem(me + k, count)},
+                device_id_type=MESH,
+            )
+        peers += count - 1
+    pl.semaphore_wait(barrier, peers)
+
+
+class Copies:
+    def __init__(self, send, recv, local):
+        self.send, self.recv, self.local = send, recv, local
+        self.sent, self.inside = [], 0
+
+    def push(self, source, target, axis, peer):
+        k = len(self.sent)
+        copy = pltpu.make_async_remote_copy(
+            src_ref=source,
+            dst_ref=target,
+            send_sem=self.send.at[k],
+            recv_sem=self.recv.at[k],
+            device_id={axis: peer},
+            device_id_type=MESH,
+        )
+        copy.start()
+        self.sent.append(copy)
+        return copy
+
+    def move(self, source, target):
+        copy = pltpu.make_async_copy(source, target, self.local.at[self.inside])
+        self.inside += 1
+        copy.start()
+        return copy
+
+    def finish(self):
+        for copy in self.sent:
+            copy.wait_send()
+
+
+def in_turn(steps):
+    steps = list(steps)
+    while steps:
+        kept = []
+        for step in steps:
+            try:
+                next(step)
+                kept.append(step)
+            except StopIteration:
+                pass
+        steps = kept
+
+
+def rows_of(start, count, half):
+    if half is None:
+        return start, count
+    return start + half * (count // 2), count // 2
+
+
+def view(ref, lead, rows):
+    start, count = rows
+    if not isinstance(start, int):
+        start = pl.multiple_of(start, 16)
+    return ref.at[(*lead, pl.ds(start, count))]
+
+
+def places(order, stage, rows, by_sub):
+    start, count = rows
+    axis = order[stage]
+
+    def part(i, half, settled):
+        lead = []
+        for name in ("z", "x"):
+            if name == axis:
+                lead.append(i)
+            elif (name in order[:stage]) == settled:
+                lead.append(slice(None))
+            else:
+                lead.append(lax.axis_index(RING[name]))
+        if not by_sub:
+            span = rows_of(start, count, half)
+        else:
+            piece = count // 4
+            if axis == "y":
+                span = rows_of(start + i * piece, piece, half)
+            elif ("y" in order[:stage]) == settled:
+                span = rows_of(start, count, half)
+            else:
+                span = rows_of(start + lax.axis_index("sub") * piece, piece, half)
+        return tuple(lead), span
+
+    return part
+
+
+def ring_gather(part, axis, copies, arrived):
+    me, right, left, far = around(axis)
+    first = copies.push(part(me, None), part(me, None), axis, right)
+    second = copies.push(part(me, None), part(me, None), axis, left)
+    yield
+    first.wait_recv()
+    third = copies.push(part(left, 0), part(left, 0), axis, right)
+    arrived(part(left, None))
+    yield
+    second.wait_recv()
+    fourth = copies.push(part(right, 1), part(right, 1), axis, left)
+    arrived(part(right, None))
+    yield
+    third.wait_recv()
+    fourth.wait_recv()
+    arrived(part(far, None))
+    yield
+
+
+def gather_kernel(colours, swap, axes, value, *refs):
+    if swap:
+        out, mine, joined, *refs = refs
+    else:
+        out, *refs = refs
+    copies = Copies(*refs)
+    z, x, c = (lax.axis_index(a) for a in ("tok_0", "tok_1", CORE))
+    greet(axes)
+    if swap:
+        me = lax.axis_index("sub")
+        piece = value.shape[0] // 4
+
+        def part_of(ref, k):
+            return ref.at[pl.ds(pl.multiple_of(k * piece, 16), piece)]
+
+        local = copies.move(part_of(value, me), part_of(mine, me))
+        arrivals = [
+            copies.push(part_of(value, peer), part_of(mine, me), "sub", peer)
+            for peer in (lax.rem(me + k, 4) for k in (1, 3, 2))
+        ]
+        local.wait()
+        for copy in arrivals:
+            copy.wait_recv()
+        value = mine
+        if swap == "sum":
+            added = mine[pl.ds(0, piece)].astype(jnp.float32)
+            for k in range(1, 4):
+                added = added + mine[pl.ds(k * piece, piece)].astype(jnp.float32)
+            joined[...] = added.astype(joined.dtype)
+            value = joined
+    crossing = []
+
+    def arrived(ref):
+        crossing.append(copies.push(ref, ref, CORE, 1 - c))
+
+    own = []
+    for order, (start, count) in colours:
+        if "y" in order:
+            count = count // 4
+            start = start + lax.axis_index("sub") * count
+        own.append(
+            (
+                view(value, (), (start, count)),
+                view(out, (z, x, c), (start, count)),
+            )
+        )
+    for copy in [copies.move(*pair) for pair in own]:
+        copy.wait()
+
+    def run(order, rows):
+        by_sub = "y" in order
+        for stage, name in enumerate(order):
+            part = places(order, stage, rows, by_sub)
+
+            def here(i, half, part=part):
+                (first, second), span = part(i, half, True)
+                return view(out, (first, second, c), span)
+
+            yield from ring_gather(here, RING[name], copies, arrived)
+
+    steps = [run(order, rows) for order, rows in colours]
+    for step in steps:
+        next(step)
+    for _, ref in own:
+        arrived(ref)
+    in_turn(steps)
+    for copy in crossing:
+        copy.wait_recv()
+    copies.finish()
+
+
+def semaphores(count, inside):
+    return [
+        pltpu.SemaphoreType.DMA((count,)),
+        pltpu.SemaphoreType.DMA((count,)),
+        pltpu.SemaphoreType.DMA((inside,)),
+    ]
+
+
+def gather_tok(value, number, colours, swap=None):
+    stages = sum(len(order) for order, _ in colours)
+    rows, lanes = value.shape
+    scratch = []
+    if swap:
+        scratch = [pltpu.VMEM((n, lanes), value.dtype) for n in (rows, rows // 4)]
+        rows = rows // 4 if swap == "sum" else rows
+    axes = (CORE, "tok_0", "tok_1")
+    if swap or any("y" in order for order, _ in colours):
+        axes += ("sub",)
+    return pl.pallas_call(
+        functools.partial(gather_kernel, colours, swap, axes),
+        out_shape=jax.ShapeDtypeStruct((4, 4, 2, rows, lanes), value.dtype),
+        in_specs=[pl.BlockSpec(memory_space=pltpu.HBM)],
+        out_specs=pl.BlockSpec(memory_space=pltpu.HBM),
+        scratch_shapes=scratch + semaphores(7 * stages + 8, 4),
+        compiler_params=pltpu.CompilerParams(
+            collective_id=number, has_side_effects=True, vmem_limit_bytes=16 * MIB
+        ),
+    )(value)
+
+
+def add_to(target, *sources):
+    lead = target.shape[:-2]
+    total = math.prod(lead)
+
+    def step(k, carry):
+        spot = []
+        for size in reversed(lead):
+            spot.append(lax.rem(k, size))
+            k = lax.div(k, size)
+        spot = tuple(reversed(spot))
+        value = target[spot]
+        for source in sources:
+            value = value + source[spot]
+        target[spot] = value
+        return carry
+
+    if lead:
+        lax.fori_loop(0, total, step, 0)
+    else:
+        value = target[...]
+        for source in sources:
+            value = value + source[...]
+        target[...] = value
+
+
+def scatter_kernel(colours, ending, value, out, total, other, *refs):
+    count = sum(len(order) for order, _ in colours) * 6
+    slots, refs = refs[:count], refs[count:]
+    if ending != "gather":
+        mine, *refs = refs
+    copies = Copies(*refs)
+    c = lax.axis_index(CORE)
+    me_y = lax.axis_index("sub")
+    greet((CORE, "tok_0", "tok_1", "sub"))
+    pending = {}
+    for turn in range(4):
+        for k, (order, rows) in enumerate(colours):
+            part = places(order, 0, rows, "y" in order)
+            i = around(RING[order[0]])[(3, 1, 2, 0)[turn]]
+            (first, second), span = part(i, None, False)
+            pending[k, turn] = (
+                copies.push(
+                    view(value, (first, second, 1 - c), span),
+                    view(other, (first, second), span),
+                    CORE,
+                    1 - c,
+                ),
+                copies.move(
+                    view(value, (first, second, c), span), view(total, (first, second), span)
+                ),
+                view(total, (first, second), span),
+                view(other, (first, second), span),
+            )
+
+    def ready(k, turn):
+        across, inside, ours, theirs = pending[k, turn]
+        inside.wait()
+        across.wait_recv()
+        add_to(ours, theirs)
+
+    def run(k, order, rows):
+        at = 6 * sum(len(o) for o, _ in colours[:k])
+        for stage, name in enumerate(order):
+            part = places(order, stage, rows, "y" in order)
+            axis = RING[name]
+            me, right, left, far = around(axis)
+            r1_in, l1_in, r2_in, l2_in, r3_in, l3_in = slots[at : at + 6]
+            at += 6
+
+            def here(i, half, part=part):
+                lead, span = part(i, half, False)
+                return view(total, lead, span)
+
+            if stage == 0:
+                ready(k, 0)
+            r1 = copies.push(here(far, 0), r1_in, axis, right)
+            l1 = copies.push(here(far, 1), l1_in, axis, left)
+            yield
+            if stage == 0:
+                ready(k, 1)
+            r2 = copies.push(here(right, 1), r2_in, axis, right)
+            if stage == 0:
+                ready(k, 2)
+            l2 = copies.push(here(left, 0), l2_in, axis, left)
+            yield
+            r1.wait_recv()
+            add_to(here(right, 0), r1_in)
+            r3 = copies.push(here(right, 0), r3_in, axis, right)
+            l1.wait_recv()
+            add_to(here(left, 1), l1_in)
+            l3 = copies.push(here(left, 1), l3_in, axis, left)
+            yield
+            if stage == 0:
+                ready(k, 3)
+            l2.wait_recv()
+            r2.wait_recv()
+            yield
+            r3.wait_recv()
+            l3.wait_recv()
+            last = stage == len(order) - 1
+            for half, one, two in ((0, l2_in, r3_in), (1, r2_in, l3_in)):
+                if not last:
+                    add_to(here(me, half), one, two)
+                    continue
+                lead, (start, size) = part(me, half, False)
+                value = here(me, half)[...].astype(jnp.float32)
+                value = value + one[...].astype(jnp.float32) + two[...].astype(jnp.float32)
+                if not isinstance(start, int):
+                    start = pl.multiple_of(start, 16)
+                if ending != "gather":
+                    mine[pl.ds(start, size)] = value.astype(mine.dtype)
+                else:
+                    out[pl.ds(start, size)] = value
+            yield
+        if ending == "gather":
+            start, size = rows
+            piece = size // 4
+
+            def held(i, half):
+                return view(out, (), rows_of(start + i * piece, piece, half))
+
+            yield from ring_gather(held, "sub", copies, lambda ref: None)
+
+    in_turn([run(k, order, rows) for k, (order, rows) in enumerate(colours)])
+    if ending != "gather":
+        piece = mine.shape[0] // 4
+
+        def given(peer):
+            if ending == "spread":
+                return mine
+            return mine.at[pl.ds(pl.multiple_of(peer * piece, 16), piece)]
+
+        local = copies.move(given(me_y), out.at[me_y])
+        arrivals = [
+            copies.push(given(peer), out.at[me_y], "sub", peer)
+            for peer in (lax.rem(me_y + k, 4) for k in (1, 3, 2))
+        ]
+        local.wait()
+        for copy in arrivals:
+            copy.wait_recv()
+    copies.finish()
+
+
+def scatter_tok(value, number, colours, ending, limit):
+    rows, lanes = value.shape[3:]
+    slots = []
+    for order, (_, size) in colours:
+        piece = size // 4 if "y" in order else size
+        lead = {"z": 4, "x": 4}
+        seen_y = "y" not in order
+        for name in order:
+            lead.pop(name, None)
+            seen_y = seen_y or name == "y"
+            height = (piece if seen_y else size) // 2
+            slots += [pltpu.VMEM((*lead.values(), height, lanes), value.dtype)] * 6
+    stages = len(slots) // 6
+    mine = [] if ending == "gather" else [pltpu.VMEM((rows, lanes), value.dtype)]
+    shape = {"gather": (rows, lanes), "spread": (4, rows, lanes), "swap": (4, rows // 4, lanes)}
+    kind = jnp.float32 if ending == "gather" else value.dtype
+    return pl.pallas_call(
+        functools.partial(scatter_kernel, colours, ending),
+        out_shape=jax.ShapeDtypeStruct(shape[ending], kind),
+        in_specs=[pl.BlockSpec(memory_space=pltpu.HBM)],
+        out_specs=pl.BlockSpec(memory_space=pltpu.VMEM),
+        scratch_shapes=[pltpu.VMEM((4, 4, rows, lanes), value.dtype)] * 2
+        + slots
+        + mine
+        + semaphores(6 * stages + 8 * len(colours) + 4, 4 * len(colours) + 1),
+        compiler_params=pltpu.CompilerParams(
+            collective_id=number, has_side_effects=True, vmem_limit_bytes=limit
+        ),
+    )(value)
+
+
+def added(values):
+    total = values[0]
+    for value in values[1:]:
+        total = total + value
+    return total
+
+
+def merged(values):
+    peaks = [value[0:32] for value in values]
+    peak = functools.reduce(jnp.maximum, peaks)
+    scales = [jnp.exp(p - peak) for p in peaks]
+    total = added([value[32:64] * scale for value, scale in zip(values, scales)])
+    hit = added([value[64:72] for value in values])
+    gaps = [
+        added([value[k : k + 8] * scale[0:8] for value, scale in zip(values, scales)])
+        for k in (72, 80, 88)
+    ]
+    return jnp.concatenate([peak, total, hit, *gaps], 0)
+
+
+def sum_kernel(axes, combine, value, out, *refs):
+    slots, (send, recv) = refs[: len(axes)], refs[len(axes) :]
+    greet(axes)
+    copies = Copies(send, recv, None)
+    out[...] = value[...]
+    for axis, slot in zip(axes, slots):
+        count = lax.axis_size(axis)
+        me = lax.axis_index(axis)
+        slot[me] = out[...]
+        arrivals = [
+            copies.push(slot.at[me], slot.at[me], axis, lax.rem(me + k, count))
+            for k in range(1, count)
+        ]
+        for copy in arrivals:
+            copy.wait_recv()
+        out[...] = combine([slot[k] for k in range(count)])
+    copies.finish()
+
+
+def sum_all(value, number, axes, combine=added):
+    counts = [lax.axis_size(axis) for axis in axes]
+    sends = sum(counts) - len(axes)
+    return pl.pallas_call(
+        functools.partial(sum_kernel, axes, combine),
+        out_shape=jax.ShapeDtypeStruct(value.shape, value.dtype),
+        in_specs=[pl.BlockSpec(memory_space=pltpu.VMEM)],
+        out_specs=pl.BlockSpec(memory_space=pltpu.VMEM),
+        scratch_shapes=[pltpu.VMEM((n, *value.shape), value.dtype) for n in counts]
+        + [pltpu.SemaphoreType.DMA((sends,))] * 2,
+        compiler_params=pltpu.CompilerParams(
+            collective_id=number, has_side_effects=True, vmem_limit_bytes=16 * MIB
+        ),
+    )(value)
+
+
+def push_kernel(axes, value, out, send, recv, local):
+    greet(axes)
+    copies = Copies(send, recv, local)
+    spot = tuple(lax.axis_index(axis) for axis in axes)
+    copies.move(value, out.at[spot]).wait()
+    for depth in reversed(range(len(axes))):
+        axis = axes[depth]
+        held = out.at[spot[: depth + 1]]
+        arrivals = [
+            copies.push(held, held, axis, lax.rem(spot[depth] + k, lax.axis_size(axis)))
+            for k in range(1, lax.axis_size(axis))
+        ]
+        for copy in arrivals:
+            copy.wait_recv()
+    copies.finish()
+
+
+def push_all(value, number, axes):
+    counts = [lax.axis_size(axis) for axis in axes]
+    sends = sum(counts) - len(axes)
+    return pl.pallas_call(
+        functools.partial(push_kernel, axes),
+        out_shape=jax.ShapeDtypeStruct((*counts, *value.shape), value.dtype),
+        in_specs=[pl.BlockSpec(memory_space=pltpu.VMEM)],
+        out_specs=pl.BlockSpec(memory_space=pltpu.VMEM),
+        scratch_shapes=semaphores(sends, 1),
+        compiler_params=pltpu.CompilerParams(
+            collective_id=number, has_side_effects=True, vmem_limit_bytes=16 * MIB
+        ),
+    )(value)
+
+
+def both_ways(rows):
+    return ((("z", "x"), (0, rows // 2)), (("x", "z"), (rows // 2, rows // 2)))
+
+
+def three_ways(first, second, last, orders):
+    starts = (0, first, first + second)
+    return tuple((o, (s, n)) for o, s, n in zip(orders, starts, (first, second, last)))
+
+
+WEIGHT_WAYS = three_ways(896, 896, 1408, (("z", "x"), ("x", "z"), ("x", "z", "y")))
+GRAD_WAYS = three_ways(1024, 1024, 1152, (("z", "x", "y"), ("x", "y", "z"), ("y", "z", "x")))
 
 
 def doc_layout(lengths):
@@ -280,16 +778,17 @@
         ]
     )
     table_low = table.astype(low_type)
-    heads_up = gather_tok(mine)
-    slots = gather_tok(master.astype(low_type)).reshape(-1, BLK, BLK)
+    heads_up = push_all(mine.reshape(1, HALF), 1, TOK).reshape(shards, HALF)
+    slots = gather_tok(master.astype(low_type).reshape(-1, BLK), 2, WEIGHT_WAYS)
+    slots = slots.reshape(-1, BLK, BLK)
     all_targets = heads_up[:, 2 * piece : 3 * piece]
     weight = (all_targets >= 0).astype(jnp.float32)
     token_count = jnp.sum(heads_up[:, 3 * piece]).astype(jnp.float32)
     first_row = place * shard_rows
     local = (heads_up[:, : 2 * piece] - first_row).reshape(-1)
     picks = (local[:, None] == jnp.arange(shard_rows, dtype=jnp.int32)).astype(low_type)
-    picked = matmul(picks, table_low).astype(low_type).reshape(shards, 2 * piece, D)
-    rows = lax.all_gather(scatter_tok(picked), "sub").astype(jnp.float32)
+    picked = matmul(picks, table_low).astype(low_type).reshape(4, 4, 2, 2 * piece, D)
+    rows = scatter_tok(picked, 3, both_ways(2 * piece), "spread", 32 * MIB).astype(jnp.float32)
     rows = rows.reshape(groups, 2, piece, D).transpose(1, 0, 2, 3).reshape(2, HALF, D)
     inverse = jnp.sum(
         jnp.where(
@@ -299,7 +798,7 @@
         ),
         1,
     )
-    mats = unpack(slots[inverse])
+    mats = lax.optimization_barrier(unpack(slots[inverse]))
     width = jnp.repeat(width_tiles[group], BLK).astype(jnp.float32)
     active = jnp.sum(width)
     head_keep = head_mask[group].astype(jnp.float32)
@@ -319,7 +818,7 @@
     )
     dec_three, kept_five = feed_block(dec_two, vec[10], vec[11], mats[9], mats[10], masks)
     final = norm(dec_three, vec[12], vec[13], width, active).astype(low_type)
-    hidden = gather_tok(swap_sub(final.reshape(groups, piece, D))).reshape(-1, D)
+    hidden = gather_tok(final, 4, both_ways(HALF), "rows").reshape(-1, D)
     logits = jnp.einsum("td,vd->tv", hidden, table_low, preferred_element_type=wide_type)
     logits = logits.reshape(shards, groups, piece, shard_rows)
     teacher = logits[:, :1]
@@ -328,14 +827,12 @@
     hits = all_targets[..., None] - first_row == jnp.arange(shard_rows, dtype=jnp.int32)
     hit = jnp.sum(jnp.where(hits, logits[:, 0], 0.0), -1)
     gap = jnp.sum(jnp.exp(teacher - peak[:, :1, :, None]) * (teacher - logits[:, 1:]), -1)
-    stats = gather_tok(jnp.concatenate([peak, total, hit[:, None], gap], 1))
-    peaks, totals, extra = jnp.split(stats, [groups, 2 * groups], 2)
-    peak = jnp.max(peaks, 0)
-    rescale = jnp.exp(peaks - peak)
-    total = jnp.sum(totals * rescale, 0)
-    logs = peak + jnp.log(total)
-    hit = jnp.sum(extra[:, :, 0], 0)
-    gap = jnp.sum(extra[:, :, 1:] * rescale[:, :, :1], 0) / total[:, :1]
+    stats = jnp.concatenate([peak, total, hit[:, None], gap], 1).transpose(1, 0, 2)
+    stats = sum_all(stats.reshape(-1, BLK), 5, TOK[::-1], merged)
+    stats = stats.reshape(-1, shards, piece).transpose(1, 0, 2)
+    logs = stats[:, :groups] + jnp.log(stats[:, groups : 2 * groups])
+    hit = stats[:, 2 * groups]
+    gap = stats[:, 2 * groups + 1 :] / stats[:, groups : groups + 1]
     token_loss = logs[:, 0] - hit + jnp.sum(logs[:, 1:] + gap - logs[:, :1], 1)
     loss_part = jnp.sum(token_loss * weight)
     target_dist = jnp.concatenate(
@@ -352,9 +849,9 @@
         :, None, :, None
     ]
     back = back.astype(low_type).reshape(-1, shard_rows)
-    d_hidden = matmul(back, table_low).astype(low_type).reshape(shards, groups * piece, D)
-    d_final = scatter_tok(d_hidden).reshape(groups, piece, D)
-    d_final = swap_sub(d_final).reshape(HALF, D).astype(jnp.float32)
+    d_hidden = matmul(back, table_low).astype(low_type).reshape(4, 4, 2, groups * piece, D)
+    d_final = scatter_tok(d_hidden, 6, both_ways(HALF), "swap", 32 * MIB)
+    d_final = d_final.reshape(HALF, D).astype(jnp.float32)
     table_grad = jnp.einsum("tv,td->vd", back, hidden, preferred_element_type=wide_type)
     d_three, g_twelve, g_thirteen = norm_pull(dec_three, vec[12], vec[13], width, active, d_final)
     d_two, grads_dec_feed, gains_five = feed_back(
@@ -375,8 +872,7 @@
     )
     d_rows = (jnp.stack([d_source, d_target], 0) * width * math.sqrt(D)).astype(low_type)
     d_rows = d_rows.reshape(2, groups, piece, D).transpose(1, 0, 2, 3)
-    d_rows = jnp.sum(swap_sub(d_rows).astype(jnp.float32), 0).astype(low_type)
-    all_rows = gather_tok(d_rows).reshape(-1, D)
+    all_rows = gather_tok(d_rows.reshape(-1, D), 7, both_ways(2 * piece), "sum").reshape(-1, D)
     table_grad = table_grad + jnp.einsum(
         "rv,rd->vd", picks, all_rows, preferred_element_type=wide_type
     )
@@ -394,12 +890,21 @@
         + [g_twelve, g_thirteen],
         0,
     )
-    own = scatter_tok(slot_grads.reshape(shards, -1, BLK, BLK)).astype(jnp.float32)
-    own, table_grad, vec_grad, loss_sum = lax.psum((own, table_grad, vec_grad, loss_part), "sub")
+    table_grad = lax.psum(table_grad, "sub")
+    own = scatter_tok(
+        slot_grads.reshape(4, 4, 2, -1, BLK), 8, GRAD_WAYS, "gather", 60 * MIB
+    ).reshape(master.shape)
     square = jnp.sum(own * own) + jnp.sum(table_grad * table_grad)
-    small = jnp.concatenate([vec_grad.reshape(-1), jnp.broadcast_to(square, (BLK,))])
-    small = jnp.sum(gather_tok(small), 0)
+    small = jnp.concatenate(
+        [
+            vec_grad.reshape(-1),
+            jnp.broadcast_to(square / groups, (BLK,)),
+            jnp.broadcast_to(loss_part / shards, (BLK,)),
+        ]
+    )
+    small = sum_all(small.reshape(-1, BLK), 9, (*TOK[::-1], "sub")).reshape(-1)
     vec_grad = small[: vec.size].reshape(vec.shape)
+    loss_sum = small[vec.size + BLK]
     grad_norm = jnp.sqrt(small[vec.size] + jnp.sum(vec_grad * vec_grad))
     scale = jnp.minimum(1.0, clip_limit / grad_norm)
     grad = own * scale

time: 1130 us -> 867 us (0.77)
  waiting for transfers between devices: 531 us -> 0.02 us
  Pallas kernels: 0 us -> 347 us
  blocking collectives: 65.9 us -> 0 us
  matrix products: 131 us -> 118 us
    pallas_call x0 -> x9, Pallas kernels: none -> 347 us  [the longest x3 161 us: gather_tok(): pl.pallas_call(functools.partial(gather_kernel, colours, swap, axes), out...]
    reduce_scatter x3 -> x0, waiting for transfers between devices: 263 us -> none  [scatter_tok(): return lax.psum_scatter(value, TOK, scatter_dimension=0)]
    all_gather x5 -> x0, waiting for transfers between devices: 199 us -> none  [gather_tok(): return lax.all_gather(value, TOK, axis=0)]
    psum x1, waiting for transfers between devices: 66.2 us -> 0.01 us  [on_device(): table_grad = lax.psum(table_grad, 'sub')]
    all_gather x2 -> x0, blocking collectives: 35.9 us -> none  [the longest x1 22.8 us: gather_tok(): return lax.all_gather(value, TOK, axis=0)]
    reshape x11 -> x2, local copies, waits for them, and re-layouts: 35.3 us -> 0.2 us  [the longest x1 0.1 us: on_device(): stats = stats.reshape(-1, shards, piece).transpose(1, 0, 2)]
    unnamed x384 -> x417, local copies, waits for them, and re-layouts: 49.7 us -> 76.6 us
    transpose x0 -> x12, local copies, waits for them, and re-layouts: none -> 25 us  [the longest x11 24.9 us: unpack(): part.reshape(rows, cols, BLK, BLK).transpose(0, 2, 1, 3)]
  transfers between devices with their start and end apart: 11 -> 1, of which waited for: 9 -> 0; matrix products, arithmetic and copies ran while one was open for 17% -> 19% of each run, Pallas kernels for 0% -> 10%
where the time goes in v2:
time: 867 us; the launch traced here: 856 us
  Pallas kernels  347 us (40%)
  local copies, waits for them, and re-layouts  245 us (28%)
  other arithmetic  123 us (14%)
  matrix products  118 us (14%)
  between operations  23.5 us (3%)
    pallas_call x3, Pallas kernels, gather_tok(): pl.pallas_call(functools.partial(gather_kernel, colours, swap, axes), out...  161 us
    pallas_call x3, Pallas kernels, scatter_tok(): pl.pallas_call(functools.partial(scatter_kernel, colours, ending), out_sh...  144 us
    unnamed x417, local copies, waits for them, and re-layouts  76.6 us
    select_n x2, other arithmetic, on_device(): jnp.take(block_grads, slot_block, axis=0, mode='fill', fill_value=0.0)  36 us
    dot_general x13, matrix products, matmul(): return jnp.dot(left, right, preferred_element_type=wide_type)  32.7 us
    pallas_call x2, Pallas kernels, sum_all(): pl.pallas_call(functools.partial(sum_kernel, axes, combine), out_shape=ja...  29.5 us
    gather x1, local copies, waits for them, and re-layouts, on_device(): mats = lax.optimization_barrier(unpack(slots[inverse]))  29.2 us
    gather x1, local copies, waits for them, and re-layouts, on_device(): jnp.take(block_grads, slot_block, axis=0, mode='fill', fill_value=0.0)  29.1 us
  transfers between devices with their start and end apart: 1, of which 0 were waited for; matrix products, arithmetic and copies ran while one was open for 19% of the time, Pallas kernels for 10%

profile of v2, /device:TPU:0, one launch (start us, length us, event | category | flops | bytes accessed | tf_op | source)
XLA Modules:
  0.0 855.8 jit_solution(9884229094345994771)
XLA Ops:
  12.5 12.2 %shard_map.282 = s32[4,4,2,1,128]{4,3,2,1,0:T(1,128)S(1)} custom-call(s32[1,128]{1,0:T(1,128)S(1)} %add_bitcast_fusion.value), custom_call_target="tpu_custom_call" | custom-call | tf_op jit(solution)/shard_map/pallas_call | solution.py:525
  24.8 5.7 fusion.12
  30.5 26.7 %shard_map.283 = bf16[4,64,640]{2,1,0:T(8,128)(2,1)S(1)} custom-call(bf16[4,4,2,64,640]{4,3,2,1,0:T(8,128)(2,1)S(1)} %bitcast.537), custom_call_target="tpu_custom_call" | custom-call | tf_op jit(solution)/shard_map/pallas_call | solution.py:435
  69.7 103.4 %shard_map.284 = bf16[4,4,2,3200,128]{4,3,2,1,0:T(8,128)(2,1)S(1)} custom-call(bf16[3200,128]{1,0:T(8,128)(2,1)S(1)} %bitcast.535), custom_call_target="tpu_custom_call" | custom-call | tf_op jit(solution)/shard_map/pallas_call | solution.py:264
  173.0 8.6 %copy-done.1 = bf16[4,4,2,3200,128]{4,3,2,1,0:T(8,128)(2,1)} copy-done((bf16[4,4,2,3200,128]{4,3,2,1,0:T(8,128)(2,1)}, bf16[4,4,2,3200,128]{4,3,2,1,0:T(8,128)(2,1)S(1)}, u32[]{:S(2)}) %copy-start.1) | copy-done | bytes 26214424
  182.3 29.2 %gather_fusion = bf16[780,128,128]{2,1,0:T(8,128)(2,1)} fusion(bf16[800,128,128]{2,1,0:T(8,128)(2,1)} %bitcast.529, s32[1024]{0:T(1024)S(1)} %get-tuple-element.189), kind=kCustom, calls=%fused_computation | custom fusion | bytes 51121200 | tf_op jit(solution)/shard_map/gather | solution.py:801
  211.5 11.8 %fusion.146 = (bf16[120,128,128]{2,1,0:T(8,128)(2,1)}, bf16[120,128,128]{2,1,0:T(8,128)(2,1)}, bf16[120,128,128]{2,1,0:T(8,128)(2,1)}, bf16[120,128,128]{2,1,0:T(8,128)(2,1)}) fusion(bf16[780,128,128]{2,1,0:T(8,128)(2,1)} %gather_fusion), kind=kLoop, calls=%fused_computation.412 | loop fusion | bytes 31457280 | tf_op jit(solution)/shard_map/slice | solution.py:606
  223.3 3.7 fusion.147
  227.0 6.6 fusion.148
  238.0 6.5 copy.306
  244.5 5.3 copy.403
  249.8 2.5 copy.305
  252.3 3.0 copy.404
  255.4 6.5 copy.299
  261.9 5.4 copy.405
  267.3 2.5 copy.298
  269.8 3.1 copy.406
  294.0 3.1 convolution_convert_fusion.6
  306.3 2.1 fusion.152
  319.1 3.2 fusion.121
  328.8 2.2 fusion.153
  341.1 32.1 %shard_map.285 = bf16[4,4,2,128,640]{4,3,2,1,0:T(8,128)(2,1)S(1)} custom-call(bf16[128,640]{1,0:T(8,128)(2,1)S(1)} %multiply_convert_fusion.13.value), custom_call_target="tpu_custom_call" | custom-call | tf_op jit(solution)/shard_map/pallas_call | solution.py:264
  373.3 10.5 %fusion.154 = (f32[32,4,32]{2,1,0:T(4,128)S(1)}, f32[32,4,32,1024]{3,2,1,0:T(8,128)S(1)}) fusion(bf16[32,4,32,640]{3,2,1,0:T(8,128)(2,1)S(1)} %bitcast.530, f32[1024,640]{1,0:T(8,128)} %param.32), kind=kOutput, calls=%fused_computation.420 | convolution fusion | flops 5373554688 | bytes 24657920 | tf_op jit(solution)/shard_map/td,vd->tv/dot_general | solution.py:822
  383.9 3.0 exponential_reduce_fusion
  386.8 3.5 exponential_bitcast_fusion.1
  392.8 2.3 fusion.6
  395.4 13.0 %shard_map.286 = f32[96,128]{1,0:T(8,128)S(1)} custom-call(f32[96,128]{1,0:T(8,128)S(1)} %reshape.967.value), custom_call_target="tpu_custom_call" | custom-call | tf_op jit(solution)/shard_map/pallas_call | solution.py:492
  409.4 2.3 fusion.11
  411.6 4.8 exponential_bitcast_fusion
  417.8 3.9 broadcast_in_dim.119
  421.7 10.5 %fusion.4 = bf16[32,4,32,1024]{3,2,1,0:T(8,128)(2,1)} fusion(f32[32,3,32,1024]{3,2,1,0:T(8,128)S(1)} %broadcast_in_dim.119, f32[32,1,32,1024]{3,2,1,0:T(8,128)S(1)} %copy-done.10, f32[32,4,32,1024]{3,2,1,0:T(8,128)} %copy-done.3, f32[32,32]{1,0:T(8,128)S(1)} %get-tuple-element.104, f32[32,4,32]{2,1,0:T(4,128)S(1)} %copy.317), kind=kLoop, calls=%fused_computation.8 | loop fusion | flops 20971520 | bytes 41963520 | tf_op jit(solution)/shard_map/convert_element_type | solution.py:851
  432.3 9.1 %convolution_convert_fusion = bf16[4096,640]{1,0:T(8,128)(2,1)S(1)} fusion(bf16[4096,1024]{1,0:T(8,128)(2,1)} %bitcast.585, f32[1024,640]{1,0:T(8,128)S(1)} %copy-done.71), kind=kOutput, calls=%fused_computation.16 | convolution fusion | flops 5371985920 | bytes 16252928 | tf_op jit(solution)/shard_map/dot_general | solution.py:628
  441.5 29.9 %shard_map.287 = bf16[4,32,640]{2,1,0:T(8,128)(2,1)S(1)} custom-call(bf16[4,4,2,128,640]{4,3,2,1,0:T(8,128)(2,1)S(1)} %bitcast.534), custom_call_target="tpu_custom_call" | custom-call | tf_op jit(solution)/shard_map/pallas_call | solution.py:435
  506.0 25.4 %shard_map.289 = bf16[4,4,2,64,640]{4,3,2,1,0:T(8,128)(2,1)S(1)} custom-call(bf16[256,640]{1,0:T(8,128)(2,1)S(1)} %bitcast.538), custom_call_target="tpu_custom_call" | custom-call | tf_op jit(solution)/shard_map/pallas_call | solution.py:264
  531.4 6.9 fusion.155
  538.4 5.0 fusion.16
  544.4 5.3 convolution_convert_fusion.1
  549.7 3.3 fusion.15
  553.8 3.3 convolution_convert_fusion.3
  557.1 3.2 fusion.14
  560.3 6.4 copy.343
  566.7 5.2 copy.390
  571.9 6.5 copy.344
  578.4 3.2 copy.389
  581.7 2.9 copy.342
  587.2 6.2 copy.335
  593.4 5.2 copy.388
  598.6 6.8 copy.336
  605.4 3.2 copy.387
  608.7 2.9 copy.334
  623.2 2.3 constant_dynamic-update-slice_fusion.8
  626.7 2.3 constant_dynamic-update-slice_fusion.7
  635.4 2.3 constant_dynamic-update-slice_fusion.1
  639.0 2.2 constant_dynamic-update-slice_fusion
  641.2 29.1 %gather_fusion.1 = bf16[800,128,128]{2,1,0:T(8,128)(2,1)} fusion(bf16[780,128,128]{2,1,0:T(8,128)(2,1)} %constant_dynamic-update-slice_fusion, s32[1024]{0:T(1024)S(1)} %copy-done.150), kind=kCustom, calls=%fused_computation.1 | custom fusion | bytes 52432000 | tf_op jit(solution)/shard_map/jit(_take)/gather | solution.py:882
  670.4 36.0 %broadcast_select_fusion.value = bf16[4,4,2,3200,128]{4,3,2,1,0:T(8,128)(2,1)} fusion(bf16[4,4,2,3200,128]{4,3,2,1,0:T(8,128)(2,1)} %bitcast.545, pred[4,4,2,3200]{3,2,1,0:T(4,128)(4,1)S(1)} %copy.331), kind=kLoop, calls=%fused_computation.5 | loop fusion | flops 13107200 | bytes 52531200 | tf_op jit(solution)/shard_map/jit(_take)/select_n | solution.py:882
  706.8 87.6 %shard_map.288 = f32[3200,128]{1,0:T(8,128)} custom-call(bf16[4,4,2,3200,128]{4,3,2,1,0:T(8,128)(2,1)} %broadcast_select_fusion.value), custom_call_target="tpu_custom_call" | custom-call | tf_op jit(solution)/shard_map/pallas_call | solution.py:435
  798.0 2.5 multiply_reduce_fusion.1
  800.4 3.0 multiply_reduce_fusion
  804.8 16.5 %shard_map.290 = f32[72,128]{1,0:T(8,128)S(1)} custom-call(f32[72,128]{1,0:T(8,128)S(1)} %maximum_bitcast_fusion.1.value), custom_call_target="tpu_custom_call" | custom-call | tf_op jit(solution)/shard_map/pallas_call | solution.py:492
  827.4 4.0 multiply_add_fusion.1
  831.4 4.7 multiply_add_fusion.2
  837.8 3.2 multiply_subtract_fusion.1
  841.7 4.6 multiply_subtract_fusion
  (621 shorter events, 152.5 us)
Async XLA Ops:
  7.2 828.9 %copy-start = (f32[25,128,128]{2,1,0:T(8,128)S(1)}, f32[25,128,128]{2,1,0:T(8,128)}, u32[]{:S(2)}) copy-start(f32[25,128,128]{2,1,0:T(8,128)} %param.30) | copy-start | bytes 4915204
  7.2 793.2 %all-reduce.2.cloned.1.call-start = ((), (), s32[]{:S(2)}) async-start(), calls=%async_computation | async-start | bytes 5242880 | tf_op jit(solution)/shard_map/psum | solution.py:893
  24.8 5.7 copy-start.157
  60.1 7.6 copy-start.130
  173.0 8.6 %copy-start.1 = (bf16[4,4,2,3200,128]{4,3,2,1,0:T(8,128)(2,1)}, bf16[4,4,2,3200,128]{4,3,2,1,0:T(8,128)(2,1)S(1)}, u32[]{:S(2)}) copy-start(bf16[4,4,2,3200,128]{4,3,2,1,0:T(8,128)(2,1)S(1)} %shard_map.284) | copy-start | bytes 78643200
  238.0 50.1 %copy-start.120 = (f32[640]{0:T(1024)}, f32[640]{0:T(1024)S(1)}, u32[]{:S(2)}) copy-start(f32[640]{0:T(1024)S(1)} %get-tuple-element.69) | copy-start | bytes 7684
  238.0 50.1 %copy-start.124 = (f32[640]{0:T(1024)}, f32[640]{0:T(1024)S(1)}, u32[]{:S(2)}) copy-start(f32[640]{0:T(1024)S(1)} %get-tuple-element.67) | copy-start | bytes 7684
  238.0 75.6 %copy-start.118 = (f32[640]{0:T(1024)}, f32[640]{0:T(1024)S(1)}, u32[]{:S(2)}) copy-start(f32[640]{0:T(1024)S(1)} %get-tuple-element.65) | copy-start | bytes 7684
  238.0 88.3 %copy-start.116 = (f32[640]{0:T(1024)}, f32[640]{0:T(1024)S(1)}, u32[]{:S(2)}) copy-start(f32[640]{0:T(1024)S(1)} %get-tuple-element.61) | copy-start | bytes 7684
  238.0 97.2 %copy-start.110 = (f32[640]{0:T(1024)}, f32[640]{0:T(1024)S(1)}, u32[]{:S(2)}) copy-start(f32[640]{0:T(1024)S(1)} %get-tuple-element.58) | copy-start | bytes 7684
  238.0 103.0 %copy-start.122 = (f32[640]{0:T(1024)}, f32[640]{0:T(1024)S(1)}, u32[]{:S(2)}) copy-start(f32[640]{0:T(1024)S(1)} %get-tuple-element.57) | copy-start | bytes 7684
  288.1 38.2 %copy-start.18 = (bf16[80,8,10,128]{3,1,2,0:T(8,128)(2,1)}, bf16[80,8,10,128]{3,1,2,0:T(8,128)(2,1)S(1)}, u32[]{:S(2)}) copy-start(bf16[80,8,10,128]{3,1,2,0:T(8,128)(2,1)S(1)} %copy.409) | copy-start | bytes 4915204
  291.2 7.9 copy-start.171
  291.2 7.9 copy-start.172
  294.0 37.1 %copy-start.190 = (f32[8]{0:T(128)}, f32[8]{0:T(128)S(1)}, u32[]{:S(2)}) copy-start(f32[8]{0:T(128)S(1)} %fusion.105) | copy-start | bytes 100
  302.0 8.0 copy-start.175
  306.3 7.3 copy-start.167
  306.3 7.3 copy-start.139
  308.5 6.0 copy-start.32
  312.3 10.0 %copy-start.132 = (f32[128]{0:T(128)}, f32[128]{0:T(128)S(1)}, u32[]{:S(2)}) copy-start(f32[128]{0:T(128)S(1)} %broadcast_divide_fusion.8) | copy-start | bytes 1540
  319.1 17.0 %copy-start.114 = (f32[3072]{0:T(1024)}, f32[3072]{0:T(1024)S(1)}, u32[]{:S(2)}) copy-start(f32[3072]{0:T(1024)S(1)} %broadcast_bitcast_fusion) | copy-start | bytes 36868
  324.8 7.7 copy-start.151
  326.3 6.2 copy-start.153
  335.2 142.6 %copy-start.136 = (f32[128]{0:T(128)}, f32[128]{0:T(128)S(1)}, u32[]{:S(2)}) copy-start(f32[128]{0:T(128)S(1)} %get-tuple-element.108) | copy-start | bytes 1540
  338.8 34.5 %copy-start.46 = (f32[128,640]{1,0:T(8,128)}, f32[128,640]{1,0:T(8,128)S(1)}, u32[]{:S(2)}) copy-start(f32[128,640]{1,0:T(8,128)S(1)} %get-tuple-element.172) | copy-start | bytes 983044
  339.5 33.8 %copy-start.159 = (f32[128]{0:T(128)}, f32[128]{0:T(128)S(1)}, u32[]{:S(2)}) copy-start(f32[128]{0:T(128)S(1)} %broadcast_divide_fusion.5) | copy-start | bytes 1540
  341.0 32.3 %copy-start.161 = (f32[128]{0:T(128)}, f32[128]{0:T(128)S(1)}, u32[]{:S(2)}) copy-start(f32[128]{0:T(128)S(1)} %get-tuple-element.106) | copy-start | bytes 1540
  373.3 10.5 %copy-start.2 = (bf16[4,4,2,128,640]{4,3,2,1,0:T(8,128)(2,1)}, bf16[4,4,2,128,640]{4,3,2,1,0:T(8,128)(2,1)S(1)}, u32[]{:S(2)}) copy-start(bf16[4,4,2,128,640]{4,3,2,1,0:T(8,128)(2,1)S(1)} %shard_map.285) | copy-start | bytes 15728644
  383.8 7.2 copy-start.3
  408.5 7.9 copy-start.88
  408.6 7.8 copy-start.91
  408.6 7.8 copy-start.108
  421.7 10.6 %copy-start.71 = (f32[1024,640]{1,0:T(8,128)S(1)}, f32[1024,640]{1,0:T(8,128)}, u32[]{:S(2)}) copy-start(f32[1024,640]{1,0:T(8,128)} %param.32) | copy-start | bytes 7864324
  432.3 39.1 %copy-start.123 = (f32[640]{0:T(1024)S(1)}, f32[640]{0:T(1024)}, u32[]{:S(2)}) copy-start(f32[640]{0:T(1024)} %copy-done.122) | copy-start | bytes 7684
  432.3 39.1 %copy-start.160 = (f32[128]{0:T(128)S(1)}, f32[128]{0:T(128)}, u32[]{:S(2)}) copy-start(f32[128]{0:T(128)} %copy-done.159) | copy-start | bytes 1540
  432.3 39.1 %copy-start.162 = (f32[128]{0:T(128)S(1)}, f32[128]{0:T(128)}, u32[]{:S(2)}) copy-start(f32[128]{0:T(128)} %copy-done.161) | copy-start | bytes 1540
  441.4 30.0 %copy-start.47 = (f32[128,640]{1,0:T(8,128)S(1)}, f32[128,640]{1,0:T(8,128)}, u32[]{:S(2)}) copy-start(f32[128,640]{1,0:T(8,128)} %copy-done.46) | copy-start | bytes 983044
  441.5 30.2 %copy-start.189 = (f32[128]{0:T(128)S(1)}, f32[128]{0:T(128)}, u32[]{:S(2)}) copy-start(f32[128]{0:T(128)} %get-tuple-element.107) | copy-start | bytes 1540
  441.5 31.9 %copy-start.44 = (f32[128,3072]{1,0:T(8,128)S(1)}, f32[128,3072]{1,0:T(8,128)}, u32[]{:S(2)}) copy-start(f32[128,3072]{1,0:T(8,128)} %copy-done.43) | copy-start | bytes 4718596
  441.5 31.9 %copy-start.56 = (bf16[80,8,24,128]{3,1,2,0:T(8,128)(2,1)S(1)}, bf16[80,8,24,128]{3,1,2,0:T(8,128)(2,1)}, u32[]{:S(2)}) copy-start(bf16[80,8,24,128]{3,1,2,0:T(8,128)(2,1)} %copy.403) | copy-start | bytes 11796484
  441.5 31.9 %copy-start.115 = (f32[3072]{0:T(1024)S(1)}, f32[3072]{0:T(1024)}, u32[]{:S(2)}) copy-start(f32[3072]{0:T(1024)} %copy-done.114) | copy-start | bytes 36868
  472.6 6.1 copy-start.65
  480.8 12.3 %copy-start.79 = (bf16[8,80,128]{2,1,0:T(8,128)(2,1)}, bf16[8,80,128]{2,1,0:T(8,128)(2,1)S(1)}, u32[]{:S(2)}) copy-start(bf16[8,80,128]{2,1,0:T(8,128)(2,1)S(1)} %fusion.53) | copy-start | bytes 491524
  483.7 6.7 copy-start.67
  494.0 37.3 %slice-start.3 = ((s8[8388608]{0:T(1024)(128)(4,1)}), s8[4194304]{0:T(1024)(128)(4,1)S(1)}, s32[]{:S(2)}) async-start(s8[8388608]{0:T(1024)(128)(4,1)} %bitcast.586), calls=%async_computation.4 | async-start | bytes 8388608
  498.6 32.7 %slice-start = ((s8[5242880]{0:T(1024)(128)(4,1)}), s8[4194304]{0:T(1024)(128)(4,1)S(1)}, s32[]{:S(2)}) async-start(s8[5242880]{0:T(1024)(128)(4,1)} %bitcast.531), calls=%async_computation.1 | async-start | bytes 8388608
  499.9 31.5 %slice-start.4 = ((s8[8388608]{0:T(1024)(128)(4,1)}), s8[4194304]{0:T(1024)(128)(4,1)S(1)}, s32[]{:S(2)}) async-start(s8[8388608]{0:T(1024)(128)(4,1)} %bitcast.586), calls=%async_computation.5 | async-start | bytes 8388608
  500.3 5.6 copy-start.51
  501.2 30.2 %slice-start.1 = ((s8[5242880]{0:T(1024)(128)(4,1)}), s8[1048576]{0:T(1024)(128)(4,1)S(1)}, s32[]{:S(2)}) async-start(s8[5242880]{0:T(1024)(128)(4,1)} %bitcast.531), calls=%async_computation.2 | async-start | bytes 2097152
  531.4 6.9 copy-start.158
  670.3 36.1 %copy-start.149 = (f32[640]{0:T(1024)S(1)}, f32[640]{0:T(1024)}, u32[]{:S(2)}) copy-start(f32[640]{0:T(1024)} %get-tuple-element.41) | copy-start | bytes 7684
  670.3 36.1 %copy-start.148 = (f32[640]{0:T(1024)S(1)}, f32[640]{0:T(1024)}, u32[]{:S(2)}) copy-start(f32[640]{0:T(1024)} %get-tuple-element.53) | copy-start | bytes 7684
  670.3 36.1 %copy-start.146 = (f32[640]{0:T(1024)S(1)}, f32[640]{0:T(1024)}, u32[]{:S(2)}) copy-start(f32[640]{0:T(1024)} %get-tuple-element.47) | copy-start | bytes 7684
  670.4 36.1 %copy-start.145 = (f32[640]{0:T(1024)S(1)}, f32[640]{0:T(1024)}, u32[]{:S(2)}) copy-start(f32[640]{0:T(1024)} %get-tuple-element.56) | copy-start | bytes 7684
  670.4 36.2 %copy-start.144 = (f32[640]{0:T(1024)S(1)}, f32[640]{0:T(1024)}, u32[]{:S(2)}) copy-start(f32[640]{0:T(1024)} %get-tuple-element.73) | copy-start | bytes 7684
  670.4 36.2 %copy-start.143 = (f32[640]{0:T(1024)S(1)}, f32[640]{0:T(1024)}, u32[]{:S(2)}) copy-start(f32[640]{0:T(1024)} %get-tuple-element.71) | copy-start | bytes 7684
  670.4 36.2 %copy-start.142 = (f32[640]{0:T(1024)S(1)}, f32[640]{0:T(1024)}, u32[]{:S(2)}) copy-start(f32[640]{0:T(1024)} %get-tuple-element.45) | copy-start | bytes 7684
  706.8 88.4 %copy-start.92 = (f32[32,4,32]{2,0,1:T(8,128)S(1)}, f32[32,4,32]{2,0,1:T(8,128)}, u32[]{:S(2)}) copy-start(f32[32,4,32]{2,0,1:T(8,128)} %copy-done.91) | copy-start | bytes 49156
  706.8 88.3 %copy-start.109 = (f32[32,32]{1,0:T(8,128)S(1)}, f32[32,32]{1,0:T(8,128)}, u32[]{:S(2)}) copy-start(f32[32,32]{1,0:T(8,128)} %copy-done.108) | copy-start | bytes 12292
  706.8 89.2 %copy-start.147 = (pred[32,32]{1,0:T(8,128)(4,1)S(1)}, pred[32,32]{1,0:T(8,128)(4,1)}, u32[]{:S(2)}) copy-start(pred[32,32]{1,0:T(8,128)(4,1)} %get-tuple-element.105) | copy-start | bytes 3076
  827.4 8.7 %copy-start.39 = (f32[25,128,128]{2,1,0:T(8,128)}, f32[25,128,128]{2,1,0:T(8,128)S(1)}, u32[]{:S(2)}) copy-start(f32[25,128,128]{2,1,0:T(8,128)S(1)} %multiply_add_fusion.3) | copy-start | bytes 4915204
  831.4 6.4 copy-start.77
  831.4 10.4 %copy-start.74 = (f32[1024,640]{1,0:T(8,128)S(1)}, f32[1024,640]{1,0:T(8,128)}, u32[]{:S(2)}) copy-start(f32[1024,640]{1,0:T(8,128)} %param.34) | copy-start | bytes 7864324
  836.1 5.7 copy-start.73
  (134 other events, 364.7 us)
Sparse Core Ops, SparseCore 0:
  543.6 64.8 all-reduce.1

commit v3 on v2

--- a/solution.py
+++ b/solution.py
@@ -567,20 +567,6 @@
     return jnp.stack([jnp.sin(angle), jnp.cos(angle)], -1).reshape(offset.shape + (D,))
 
 
-def norm(stream, gain, bias, width, active):
-    centre = jnp.sum(stream * width, -1, keepdims=True) / active
-    centred = (stream - centre) * width
-    spread = jnp.sum(centred * centred, -1, keepdims=True) / active
-    return (centred * lax.rsqrt(spread + eps_norm) * gain + bias) * width
-
-
-def norm_pull(stream, gain, bias, width, active, cotangent):
-    _, pull = jax.vjp(
-        lambda first, second, third: norm(first, second, third, width, active), stream, gain, bias
-    )
-    return pull(cotangent)
-
-
 def layout():
     wide = D // BLK
     deep = FF // BLK
@@ -599,134 +585,349 @@
     ]
 
 
-def unpack(blocks):
-    result = []
-    start = 0
-    for rows, cols in layout():
-        part = blocks[start : start + rows * cols]
-        start = start + rows * cols
-        result.append(
-            part.reshape(rows, cols, BLK, BLK).transpose(0, 2, 1, 3).reshape(rows * BLK, cols * BLK)
-        )
-    return result
-
-
-def pack(matrices):
-    pieces = []
-    for matrix in matrices:
-        rows = matrix.shape[0] // BLK
-        cols = matrix.shape[1] // BLK
-        pieces.append(
-            matrix.reshape(rows, BLK, cols, BLK)
-            .transpose(0, 2, 1, 3)
-            .reshape(rows * cols, BLK, BLK)
-        )
-    return jnp.concatenate(pieces, 0)
-
-
 def matmul(left, right):
     return jnp.dot(left, right, preferred_element_type=wide_type)
 
 
-def attend(query, keys, values, allowed, head_keep):
-    scores = jnp.einsum("qhc,khc->hqk", query, keys, preferred_element_type=wide_type) * HEAD ** (
-        -0.5
-    )
-    scores = jnp.where(allowed[None], scores, -1e30)
-    peak = jnp.max(scores, -1, keepdims=True)
-    expo = jnp.exp(scores - peak)
-    probs = expo / jnp.sum(expo, -1, keepdims=True)
-    probs_low = probs.astype(low_type)
-    mixed = jnp.einsum("hqk,khc->qhc", probs_low, values, preferred_element_type=wide_type)
-    mixed = (mixed * head_keep[:, None]).reshape(query.shape[0], D).astype(low_type)
-    return (mixed, (query, keys, values, probs, probs_low))
-
-
-def attend_back(d_rows, inner, head_keep):
-    query, keys, values, probs, probs_low = inner
-    d_mixed = (d_rows.reshape(query.shape) * head_keep[:, None]).astype(low_type)
-    g_probs = jnp.einsum("qhc,khc->hqk", d_mixed, values, preferred_element_type=wide_type)
-    d_values = jnp.einsum("hqk,qhc->khc", probs_low, d_mixed, preferred_element_type=wide_type)
-    d_scores = (probs * (g_probs - jnp.sum(probs * g_probs, -1, keepdims=True))).astype(low_type)
+def shapes():
+    return [(rows * BLK, cols * BLK) for rows, cols in layout()]
+
+
+def first_block(number):
+    return sum(rows * cols for rows, cols in layout()[:number])
+
+
+def nt(left, right):
+    return lax.dot_general(left, right, (((1,), (1,)), ((), ())), preferred_element_type=wide_type)
+
+
+def tn(left, right):
+    return lax.dot_general(left, right, (((0,), (0,)), ((), ())), preferred_element_type=wide_type)
+
+
+def block_copies(number, slots, order, matrix, semaphore, outward):
+    rows, cols = layout()[number]
+    start = first_block(number)
+
+    def step(k, carry):
+        place = matrix.at[
+            pl.ds(pl.multiple_of(lax.div(k, cols) * BLK, BLK), BLK),
+            pl.ds(pl.multiple_of(lax.rem(k, cols) * BLK, BLK), BLK),
+        ]
+        slot = slots.at[order[start + k]]
+        pair = (place, slot) if outward else (slot, place)
+        pltpu.make_async_copy(*pair, semaphore).start()
+        return carry
+
+    lax.fori_loop(0, rows * cols, step, 0, unroll=5)
+
+
+def mean_parts(stream, width, active):
+    centre = jnp.sum(stream * width, -1, keepdims=True) / active
+    centred = (stream - centre) * width
+    spread = jnp.sum(centred * centred, -1, keepdims=True) / active
+    return centred, lax.rsqrt(spread + eps_norm)
+
+
+def normed(stream, vec, row, width, active):
+    centred, rate = mean_parts(stream, width, active)
+    return (centred * rate * vec[row : row + 1] + vec[row + 1 : row + 2]) * width
+
+
+def normed_back(stream, vec, row, width, active, cotangent, vec_grad):
+    centred, rate = mean_parts(stream, width, active)
+    given = cotangent * width
+    vec_grad[row : row + 1] = jnp.sum(given * centred * rate, 0, keepdims=True)
+    vec_grad[row + 1 : row + 2] = jnp.sum(given, 0, keepdims=True)
+    scaled = given * vec[row : row + 1]
+    along = jnp.sum(scaled * centred, -1, keepdims=True) / active
+    pulled = (scaled * rate - centred * (rate * rate * rate * along)) * width
+    return pulled - width * (jnp.sum(pulled, -1, keepdims=True) / active)
+
+
+def windows():
+    for head in range(HEADS):
+        low, high_end = head * HEAD, (head + 1) * HEAD
+        first, last = low // BLK, (high_end - 1) // BLK + 1
+        yield head, low, high_end, first, last
+
+
+def lanes_between(low, high_end, first, last):
+    lane = lax.broadcasted_iota(jnp.int32, (1, (last - first) * BLK), 1) + first * BLK
+    return ((lane >= low) & (lane < high_end)).astype(jnp.float32).astype(low_type)
+
+
+def tile_add(tiles, first, value):
+    for k in range(value.shape[1] // BLK):
+        part = value[:, k * BLK : (k + 1) * BLK]
+        spot = first + k
+        tiles[spot] = part if tiles[spot] is None else tiles[spot] + part
+
+
+def weights_of(query, keys, mask, first, last, allowed):
+    span = slice(first * BLK, last * BLK)
+    scores = nt(query[:, span] * mask, keys[:, span]) * HEAD ** (-0.5)
+    scores = jnp.where(allowed, scores, -1e30)
+    expo = jnp.exp(scores - jnp.max(scores, -1, keepdims=True))
+    return expo / jnp.sum(expo, -1, keepdims=True)
+
+
+def attention(query, keys, values, allowed, keep):
+    tiles = [None] * (D // BLK)
+    for _, low, high_end, first, last in windows():
+        mask = lanes_between(low, high_end, first, last)
+        probs = weights_of(query, keys, mask, first, last, allowed).astype(low_type)
+        tile_add(tiles, first, matmul(probs, values[:, first * BLK : last * BLK] * mask))
+    return (jnp.concatenate(tiles, 1) * keep).astype(low_type)
+
+
+def attention_back(d_rows, query, keys, values, allowed, keep):
+    d_mixed = (d_rows * keep).astype(low_type)
+    d_query, d_keys, d_values = ([None] * (D // BLK) for _ in range(3))
+    for _, low, high_end, first, last in windows():
+        mask = lanes_between(low, high_end, first, last)
+        span = slice(first * BLK, last * BLK)
+        probs = weights_of(query, keys, mask, first, last, allowed)
+        given = d_mixed[:, span] * mask
+        g_probs = nt(given, values[:, span])
+        tile_add(d_values, first, tn(probs.astype(low_type), given))
+        along = jnp.sum(probs * g_probs, -1, keepdims=True)
+        d_scores = (probs * (g_probs - along)).astype(low_type)
+        tile_add(d_query, first, matmul(d_scores, keys[:, span] * mask))
+        tile_add(d_keys, first, tn(d_scores, query[:, span] * mask))
     scale = HEAD ** (-0.5)
-    d_query = jnp.einsum("hqk,khc->qhc", d_scores, keys, preferred_element_type=wide_type) * scale
-    d_keys = jnp.einsum("hqk,qhc->khc", d_scores, query, preferred_element_type=wide_type) * scale
-    return (d_query, d_keys, d_values)
-
-
-def branch_back(d_out, inputs, w_out, width):
-    d_branch = (d_out * width).astype(low_type)
-    g_out = jnp.einsum("td,te->de", inputs, d_branch, preferred_element_type=wide_type)
-    d_inputs = jnp.einsum("te,de->td", d_branch, w_out, preferred_element_type=wide_type)
-    return (g_out, d_inputs)
-
-
-def self_block(stream, gain, bias, w_qkv, w_out, masks, allowed):
-    width, active, head_keep, unit_keep = masks
-    span = stream.shape[0]
-    normed = norm(stream, gain, bias, width, active).astype(low_type)
-    packed = matmul(normed, w_qkv).astype(low_type).reshape(span, 3, HEADS, HEAD)
-    mixed, inner = attend(packed[:, 0], packed[:, 1], packed[:, 2], allowed, head_keep)
-    return (stream + matmul(mixed, w_out) * width, (stream, normed, mixed, inner))
-
-
-def self_back(d_out, kept, gain, bias, w_qkv, w_out, masks):
-    width, active, head_keep, unit_keep = masks
-    stream, normed, mixed, inner = kept
-    span = stream.shape[0]
-    g_out, d_mixed = branch_back(d_out, mixed, w_out, width)
-    d_query, d_keys, d_values = attend_back(d_mixed, inner, head_keep)
-    d_packed = jnp.stack([d_query, d_keys, d_values], 1).reshape(span, 3 * D).astype(low_type)
-    g_qkv = jnp.einsum("td,te->de", normed, d_packed, preferred_element_type=wide_type)
-    d_first = jnp.einsum("te,de->td", d_packed, w_qkv, preferred_element_type=wide_type)
-    d_in, g_gain, g_bias = norm_pull(stream, gain, bias, width, active, d_first)
-    return (d_out + d_in, [g_qkv, g_out], [g_gain, g_bias])
-
-
-def cross_block(stream, memory, gain, bias, w_query, w_pair, w_out, masks, allowed):
-    width, active, head_keep, unit_keep = masks
-    span = stream.shape[0]
-    normed = norm(stream, gain, bias, width, active).astype(low_type)
-    query = matmul(normed, w_query).astype(low_type).reshape(span, HEADS, HEAD)
-    paired = matmul(memory, w_pair).astype(low_type).reshape(memory.shape[0], 2, HEADS, HEAD)
-    mixed, inner = attend(query, paired[:, 0], paired[:, 1], allowed, head_keep)
-    return (stream + matmul(mixed, w_out) * width, (stream, normed, mixed, inner))
-
-
-def cross_back(d_out, kept, memory, gain, bias, w_query, w_pair, w_out, masks):
-    width, active, head_keep, unit_keep = masks
-    stream, normed, mixed, inner = kept
-    span = stream.shape[0]
-    g_out, d_mixed = branch_back(d_out, mixed, w_out, width)
-    d_query, d_keys, d_values = attend_back(d_mixed, inner, head_keep)
-    d_query = d_query.reshape(span, D).astype(low_type)
-    d_pair = jnp.stack([d_keys, d_values], 1).reshape(memory.shape[0], 2 * D).astype(low_type)
-    g_query = jnp.einsum("td,te->de", normed, d_query, preferred_element_type=wide_type)
-    g_pair = jnp.einsum("td,te->de", memory, d_pair, preferred_element_type=wide_type)
-    d_memory = jnp.einsum("te,de->td", d_pair, w_pair, preferred_element_type=wide_type)
-    d_first = jnp.einsum("te,de->td", d_query, w_query, preferred_element_type=wide_type)
-    d_in, g_gain, g_bias = norm_pull(stream, gain, bias, width, active, d_first)
-    return (d_out + d_in, d_memory, [g_query, g_pair, g_out], [g_gain, g_bias])
-
-
-def feed_block(stream, gain, bias, w_up, w_down, masks):
-    width, active, head_keep, unit_keep = masks
-    normed = norm(stream, gain, bias, width, active).astype(low_type)
-    hidden_pre = matmul(normed, w_up)
-    activated = (jax.nn.gelu(hidden_pre) * unit_keep).astype(low_type)
-    return (stream + matmul(activated, w_down) * width, (stream, normed, hidden_pre, activated))
-
-
-def feed_back(d_out, kept, gain, bias, w_up, w_down, masks):
-    width, active, head_keep, unit_keep = masks
-    stream, normed, hidden_pre, activated = kept
-    g_down, d_act = branch_back(d_out, activated, w_down, width)
-    _, gelu_pull = jax.vjp(jax.nn.gelu, hidden_pre)
-    d_pre = gelu_pull(d_act * unit_keep)[0].astype(low_type)
-    g_up = jnp.einsum("td,tf->df", normed, d_pre, preferred_element_type=wide_type)
-    d_normed = jnp.einsum("tf,df->td", d_pre, w_up, preferred_element_type=wide_type)
-    d_in, g_gain, g_bias = norm_pull(stream, gain, bias, width, active, d_normed)
-    return (d_out + d_in, [g_up, g_down], [g_gain, g_bias])
+    return (
+        jnp.concatenate(d_query, 1) * scale,
+        jnp.concatenate(d_keys, 1) * scale,
+        jnp.concatenate(d_values, 1),
+    )
+
+
+GELU_RATE = math.sqrt(2.0 / math.pi)
+CHUNK = 768
+
+
+def gelu_parts(value):
+    square = value * value
+    bend = jnp.tanh(GELU_RATE * (value + 0.044715 * value * square))
+    gate = 0.5 * (1.0 + bend)
+    slope = gate + value * (
+        0.5 * (1.0 - bend * bend) * GELU_RATE * (1.0 + 3.0 * 0.044715 * square)
+    )
+    return value * gate, slope
+
+
+def forward_kernel(*refs):
+    slots, order, x_zero, y_zero, vec, width, keep, unit, allowed = refs[:9]
+    final, x_one, x_two, y_one, y_two, y_three = refs[9:15]
+    qkv_enc, qkv_dec, q_cross, kv_cross, o_enc, o_dec, o_cross, memory = refs[15:23]
+    h_enc, h_dec = refs[23:25]
+    stored, held = refs[25:36], refs[36:47]
+    act, arrive, leave = refs[47:]
+    for number in (0, 1, 2, 3, 4, 5, 6, 7, 8, 9, 10):
+        block_copies(number, slots, order, held[number], arrive.at[number], False)
+    width, keep, vec = width[...], keep[...], vec[...]
+    active = jnp.sum(width)
+    same, causal = allowed[0] > 0.5, allowed[1] > 0.5
+
+    def weight(number):
+        pltpu.make_async_copy(stored[number], held[number], arrive.at[number]).wait()
+        pltpu.make_async_copy(held[number], stored[number], leave.at[number]).start()
+        return held[number]
+
+    def self_part(stream, row, number, mask, qkv, mixed):
+        near = normed(stream, vec, row, width, active).astype(low_type)
+        matrix = weight(number)
+        for k in range(3):
+            part = slice(k * D, (k + 1) * D)
+            qkv[:, part] = matmul(near, matrix[:, part]).astype(low_type)
+        mixed[...] = attention(
+            qkv[:, 0:D], qkv[:, D : 2 * D], qkv[:, 2 * D : 3 * D], mask, keep
+        )
+        return stream + matmul(mixed[...], weight(number + 1)[...]) * width
+
+    def feed_part(stream, row, number, hidden):
+        near = normed(stream, vec, row, width, active).astype(low_type)
+        matrix = weight(number)
+        for k in range(FF // CHUNK):
+            part = slice(k * CHUNK, (k + 1) * CHUNK)
+            value = matmul(near, matrix[:, part])
+            hidden[:, part] = value
+            act[:, part] = (gelu_parts(value)[0] * unit[:, part]).astype(low_type)
+        return stream + matmul(act[...], weight(number + 1)[...]) * width
+
+    x_one[...] = self_part(x_zero[...], 0, 0, same, qkv_enc, o_enc)
+    x_two[...] = feed_part(x_one[...], 2, 2, h_enc)
+    memory[...] = normed(x_two[...], vec, 4, width, active).astype(low_type)
+    y_one[...] = self_part(y_zero[...], 6, 4, causal, qkv_dec, o_dec)
+    near = normed(y_one[...], vec, 8, width, active).astype(low_type)
+    q_cross[...] = matmul(near, weight(6)[...]).astype(low_type)
+    kv_cross[...] = matmul(memory[...], weight(7)[...]).astype(low_type)
+    o_cross[...] = attention(
+        q_cross[...], kv_cross[:, 0:D], kv_cross[:, D : 2 * D], same, keep
+    )
+    y_two[...] = y_one[...] + matmul(o_cross[...], weight(8)[...]) * width
+    y_three[...] = feed_part(y_two[...], 10, 9, h_dec)
+    final[...] = normed(y_three[...], vec, 12, width, active).astype(low_type)
+    for number in range(11):
+        pltpu.make_async_copy(held[number], stored[number], leave.at[number]).wait()
+
+
+def in_vmem(count):
+    return [pl.BlockSpec(memory_space=pltpu.VMEM)] * count
+
+
+def in_hbm(count):
+    return [pl.BlockSpec(memory_space=pltpu.HBM)] * count
+
+
+SMEM = pl.BlockSpec(memory_space=pltpu.SMEM)
+
+
+def run_forward(slots, order, x_zero, y_zero, vec, width, keep, unit, allowed):
+    def like(cols, kind):
+        return jax.ShapeDtypeStruct((HALF, cols), kind)
+
+    small = (
+        [like(D, low_type)]
+        + [like(D, wide_type)] * 5
+        + [like(3 * D, low_type)] * 2
+        + [like(D, low_type), like(2 * D, low_type)]
+        + [like(D, low_type)] * 4
+        + [like(FF, wide_type)] * 2
+    )
+    mats = [jax.ShapeDtypeStruct(shape, low_type) for shape in shapes()]
+    return pl.pallas_call(
+        forward_kernel,
+        out_shape=small + mats,
+        in_specs=in_hbm(1) + [SMEM] + in_vmem(7),
+        out_specs=in_vmem(len(small)) + in_hbm(len(mats)),
+        scratch_shapes=[pltpu.VMEM(shape, low_type) for shape in shapes()]
+        + [pltpu.VMEM((HALF, FF), low_type)]
+        + [pltpu.SemaphoreType.DMA((11,))] * 2,
+        compiler_params=pltpu.CompilerParams(vmem_limit_bytes=56 * MIB),
+    )(slots, order, x_zero, y_zero, vec, width, keep, unit, allowed)
+
+
+def backward_kernel(*refs):
+    order, d_final, x_zero, y_zero, vec, width, keep, unit, allowed = refs[:9]
+    x_one, x_two, y_one, y_two, y_three = refs[9:14]
+    qkv_enc, qkv_dec, q_cross, kv_cross, o_enc, o_dec, o_cross, memory = refs[14:22]
+    h_enc, h_dec = refs[22:24]
+    stored = refs[24:35]
+    slots, vec_grad, d_rows = refs[35:38]
+    held = refs[38:49]
+    zeros, d_pack, arrive, leave, blank = refs[49:]
+    uses = (10, 9, 8, 7, 6, 5, 4, 3, 2, 1, 0)
+    for number in uses:
+        pltpu.make_async_copy(stored[number], held[number], arrive.at[number]).start()
+    zeros[...] = jnp.zeros_like(zeros)
+    empty = order.shape[0] - NBLK
+    for k in range(empty):
+        pltpu.make_async_copy(zeros, slots.at[order[NBLK + k]], blank).start()
+    width, keep, vec = width[...], keep[...], vec[...]
+    active = jnp.sum(width)
+    same, causal = allowed[0] > 0.5, allowed[1] > 0.5
+
+    def weight(number):
+        pltpu.make_async_copy(stored[number], held[number], arrive.at[number]).wait()
+        return held[number]
+
+    def send(number):
+        block_copies(number, slots, order, held[number], leave.at[number], True)
+
+    def keep_grad(number, value):
+        held[number][...] = value.astype(low_type)
+        send(number)
+
+    def feed_back(given, stream, row, number, hidden):
+        near = normed(stream, vec, row, width, active).astype(low_type)
+        branch = (given * width).astype(low_type)
+        up, down = weight(number), weight(number + 1)
+        pulled = jnp.zeros((HALF, D), wide_type)
+        for k in range(FF // CHUNK):
+            part = slice(k * CHUNK, (k + 1) * CHUNK)
+            d_act = nt(branch, down[part, :])
+            value, slope = gelu_parts(hidden[:, part])
+            act = (value * unit[:, part]).astype(low_type)
+            down[part, :] = tn(act, branch).astype(low_type)
+            d_hidden = (slope * (d_act * unit[:, part])).astype(low_type)
+            pulled = pulled + nt(d_hidden, up[:, part])
+            up[:, part] = tn(near, d_hidden).astype(low_type)
+        send(number + 1)
+        send(number)
+        return given + normed_back(stream, vec, row, width, active, pulled, vec_grad)
+
+    def self_back(given, stream, row, number, mask, qkv, mixed):
+        near = normed(stream, vec, row, width, active).astype(low_type)
+        branch = (given * width).astype(low_type)
+        d_mixed = nt(branch, weight(number + 1)[...])
+        keep_grad(number + 1, tn(mixed[...], branch))
+        parts = attention_back(
+            d_mixed, qkv[:, 0:D], qkv[:, D : 2 * D], qkv[:, 2 * D : 3 * D], mask, keep
+        )
+        for k in range(3):
+            d_pack[:, k * D : (k + 1) * D] = parts[k].astype(low_type)
+        matrix = weight(number)
+        pulled = nt(d_pack[...], matrix[...])
+        for k in range(3):
+            part = slice(k * D, (k + 1) * D)
+            matrix[:, part] = tn(near, d_pack[:, part]).astype(low_type)
+        send(number)
+        return given + normed_back(stream, vec, row, width, active, pulled, vec_grad)
+
+    d_three = normed_back(
+        y_three[...], vec, 12, width, active, d_final[...].astype(wide_type), vec_grad
+    )
+    d_two = feed_back(d_three, y_two[...], 10, 9, h_dec)
+    near = normed(y_one[...], vec, 8, width, active).astype(low_type)
+    branch = (d_two * width).astype(low_type)
+    d_mixed = nt(branch, weight(8)[...])
+    keep_grad(8, tn(o_cross[...], branch))
+    parts = attention_back(
+        d_mixed, q_cross[...], kv_cross[:, 0:D], kv_cross[:, D : 2 * D], same, keep
+    )
+    d_query = parts[0].astype(low_type)
+    for k in range(2):
+        d_pack[:, k * D : (k + 1) * D] = parts[k + 1].astype(low_type)
+    d_memory = nt(d_pack[:, 0 : 2 * D], weight(7)[...])
+    keep_grad(7, tn(memory[...], d_pack[:, 0 : 2 * D]))
+    pulled = nt(d_query, weight(6)[...])
+    keep_grad(6, tn(near, d_query))
+    d_one = d_two + normed_back(y_one[...], vec, 8, width, active, pulled, vec_grad)
+    d_target = self_back(d_one, y_zero[...], 6, 4, causal, qkv_dec, o_dec)
+    d_enc = normed_back(x_two[...], vec, 4, width, active, d_memory, vec_grad)
+    d_enc = feed_back(d_enc, x_one[...], 2, 2, h_enc)
+    d_source = self_back(d_enc, x_zero[...], 0, 0, same, qkv_enc, o_enc)
+    piece = HALF // 4
+    for half, value in ((0, d_source), (1, d_target)):
+        value = (value * width * math.sqrt(D)).astype(low_type)
+        for k in range(4):
+            at = (2 * k + half) * piece
+            d_rows[at : at + piece] = value[k * piece : (k + 1) * piece]
+    vec_grad[14:16] = jnp.zeros((2, D), wide_type)
+    for number in range(11):
+        pltpu.make_async_copy(held[number], stored[number], leave.at[number]).wait()
+    blanks = slots.at[pl.ds(0, empty)]
+    pltpu.make_async_copy(blanks, blanks, blank).wait()
+
+
+def run_backward(order, d_final, x_zero, y_zero, vec, width, keep, unit, allowed, small, mats):
+    return pl.pallas_call(
+        backward_kernel,
+        out_shape=[
+            jax.ShapeDtypeStruct((order.shape[0], BLK, BLK), low_type),
+            jax.ShapeDtypeStruct((16, D), wide_type),
+            jax.ShapeDtypeStruct((2 * HALF, D), low_type),
+        ],
+        in_specs=[SMEM] + in_vmem(8 + len(small)) + in_hbm(len(mats)),
+        out_specs=in_hbm(1) + in_vmem(2),
+        scratch_shapes=[pltpu.VMEM(shape, low_type) for shape in shapes()]
+        + [pltpu.VMEM((BLK, BLK), low_type), pltpu.VMEM((HALF, 3 * D), low_type)]
+        + [pltpu.SemaphoreType.DMA((11,))] * 2
+        + [pltpu.SemaphoreType.DMA],
+        compiler_params=pltpu.CompilerParams(vmem_limit_bytes=56 * MIB),
+    )(order, d_final, x_zero, y_zero, vec, width, keep, unit, allowed, *small, *mats)
 
 
 def adamw(param, grad, first, second, rate):
@@ -790,34 +991,23 @@
     picked = matmul(picks, table_low).astype(low_type).reshape(4, 4, 2, 2 * piece, D)
     rows = scatter_tok(picked, 3, both_ways(2 * piece), "spread", 32 * MIB).astype(jnp.float32)
     rows = rows.reshape(groups, 2, piece, D).transpose(1, 0, 2, 3).reshape(2, HALF, D)
-    inverse = jnp.sum(
-        jnp.where(
-            slot_block[None, :] == jnp.arange(NBLK, dtype=jnp.int32)[:, None],
-            jnp.arange(slot_block.shape[0], dtype=jnp.int32)[None, :],
-            0,
-        ),
-        1,
-    )
-    mats = lax.optimization_barrier(unpack(slots[inverse]))
-    width = jnp.repeat(width_tiles[group], BLK).astype(jnp.float32)
-    active = jnp.sum(width)
-    head_keep = head_mask[group].astype(jnp.float32)
-    unit_keep = jnp.repeat(ffn_tiles[group], BLK).astype(jnp.float32)
-    masks = (width, active, head_keep, unit_keep)
+    used = slot_block < NBLK
+    ranks = jnp.cumsum(1 - used.astype(jnp.int32)) - 1
+    keys = jnp.where(used, slot_block, NBLK + ranks)
+    numbers = jnp.arange(slot_block.shape[0], dtype=jnp.int32)
+    order = jnp.sum(jnp.where(keys[None, :] == numbers[:, None], numbers[None, :], 0), 1)
+    width = jnp.repeat(width_tiles[group], BLK).astype(jnp.float32)[None]
+    keep = jnp.repeat(head_mask[group], HEAD).astype(jnp.float32)[None]
+    unit = jnp.repeat(ffn_tiles[group], BLK).astype(jnp.float32)[None]
     wave = sinusoid(offset)
     source = (math.sqrt(D) * rows[0] + wave) * width
     target = (math.sqrt(D) * rows[1] + wave) * width
     same = doc_of[:, None] == doc_of[None, :]
     causal = same & (offset[None, :] <= offset[:, None])
-    enc_one, kept_one = self_block(source, vec[0], vec[1], mats[0], mats[1], masks, same)
-    enc_two, kept_two = feed_block(enc_one, vec[2], vec[3], mats[2], mats[3], masks)
-    memory = norm(enc_two, vec[4], vec[5], width, active).astype(low_type)
-    dec_one, kept_three = self_block(target, vec[6], vec[7], mats[4], mats[5], masks, causal)
-    dec_two, kept_four = cross_block(
-        dec_one, memory, vec[8], vec[9], mats[6], mats[7], mats[8], masks, same
-    )
-    dec_three, kept_five = feed_block(dec_two, vec[10], vec[11], mats[9], mats[10], masks)
-    final = norm(dec_three, vec[12], vec[13], width, active).astype(low_type)
+    allowed = jnp.stack([same, causal]).astype(jnp.float32)
+    common = (source, target, vec, width, keep, unit, allowed)
+    final, *kept = run_forward(slots, order, *common)
+    kept, mats = kept[:-11], kept[-11:]
     hidden = gather_tok(final, 4, both_ways(HALF), "rows").reshape(-1, D)
     logits = jnp.einsum("td,vd->tv", hidden, table_low, preferred_element_type=wide_type)
     logits = logits.reshape(shards, groups, piece, shard_rows)
@@ -851,44 +1041,14 @@
     back = back.astype(low_type).reshape(-1, shard_rows)
     d_hidden = matmul(back, table_low).astype(low_type).reshape(4, 4, 2, groups * piece, D)
     d_final = scatter_tok(d_hidden, 6, both_ways(HALF), "swap", 32 * MIB)
-    d_final = d_final.reshape(HALF, D).astype(jnp.float32)
     table_grad = jnp.einsum("tv,td->vd", back, hidden, preferred_element_type=wide_type)
-    d_three, g_twelve, g_thirteen = norm_pull(dec_three, vec[12], vec[13], width, active, d_final)
-    d_two, grads_dec_feed, gains_five = feed_back(
-        d_three, kept_five, vec[10], vec[11], mats[9], mats[10], masks
-    )
-    d_one, d_memory, grads_cross, gains_four = cross_back(
-        d_two, kept_four, memory, vec[8], vec[9], mats[6], mats[7], mats[8], masks
-    )
-    d_target, grads_dec_self, gains_three = self_back(
-        d_one, kept_three, vec[6], vec[7], mats[4], mats[5], masks
-    )
-    d_enc_two, g_four, g_five = norm_pull(enc_two, vec[4], vec[5], width, active, d_memory)
-    d_enc_one, grads_enc_feed, gains_two = feed_back(
-        d_enc_two, kept_two, vec[2], vec[3], mats[2], mats[3], masks
-    )
-    d_source, grads_enc_self, gains_one = self_back(
-        d_enc_one, kept_one, vec[0], vec[1], mats[0], mats[1], masks
-    )
-    d_rows = (jnp.stack([d_source, d_target], 0) * width * math.sqrt(D)).astype(low_type)
-    d_rows = d_rows.reshape(2, groups, piece, D).transpose(1, 0, 2, 3)
-    all_rows = gather_tok(d_rows.reshape(-1, D), 7, both_ways(2 * piece), "sum").reshape(-1, D)
+    slot_grads, vec_grad, d_rows = run_backward(
+        order, d_final.reshape(HALF, D), *common, kept, mats
+    )
+    vec_grad = vec_grad[: vec.shape[0]]
+    all_rows = gather_tok(d_rows, 7, both_ways(2 * piece), "sum").reshape(-1, D)
     table_grad = table_grad + jnp.einsum(
         "rv,rd->vd", picks, all_rows, preferred_element_type=wide_type
-    )
-    block_grads = pack(
-        grads_enc_self + grads_enc_feed + grads_dec_self + grads_cross + grads_dec_feed
-    ).astype(low_type)
-    slot_grads = jnp.take(block_grads, slot_block, axis=0, mode="fill", fill_value=0.0)
-    vec_grad = jnp.stack(
-        gains_one
-        + gains_two
-        + [g_four, g_five]
-        + gains_three
-        + gains_four
-        + gains_five
-        + [g_twelve, g_thirteen],
-        0,
     )
     table_grad = lax.psum(table_grad, "sub")
     own = scatter_tok(

time: 867 us -> 611 us (0.70)
  local copies, waits for them, and re-layouts: 245 us -> 32.1 us
  Pallas kernels: 347 us -> 445 us
  other arithmetic: 123 us -> 54.6 us
  matrix products: 118 us -> 52.1 us
    pallas_call x0 -> x2, Pallas kernels: none -> 65.9 us  [the longest x1 42 us: run_backward(): pl.pallas_call(backward_kernel, out_shape=[jax.ShapeDtypeStruct((order.sh...]
    unnamed x417 -> x54, local copies, waits for them, and re-layouts: 76.6 us -> 13.7 us
    gather x2 -> x0, local copies, waits for them, and re-layouts: 58.4 us -> none  [the longest x1 29.2 us: on_device(): mats = lax.optimization_barrier(unpack(slots[inverse]))]
    dot_general x37 -> x0, matrix products: 42.6 us -> none  [the longest x5 10.7 us: branch_back(): jnp.einsum('td,te->de', inputs, d_branch, preferred_element_type=wide_type)]
    transpose x13 -> x0, local copies, waits for them, and re-layouts: 38.2 us -> none  [the longest x11 24.9 us: unpack(): part.reshape(rows, cols, BLK, BLK).transpose(0, 2, 1, 3)]
    select_n x3 -> x1, other arithmetic: 36.1 us -> 0.69 us  [on_device(): keys = jnp.where(used, slot_block, NBLK + ranks)]
    pallas_call x3, Pallas kernels: 144 us -> 176 us  [scatter_tok(): pl.pallas_call(functools.partial(scatter_kernel, colours, ending), out_sh...]
    slice x6 -> x1, local copies, waits for them, and re-layouts: 23.3 us -> 0.07 us  [the longest x5 22.6 us: unpack(): part = blocks[start:start + rows * cols]]
  transfers between devices with their start and end apart: 1 -> 1, of which waited for: 0 -> 0; matrix products, arithmetic and copies ran while one was open for 19% -> 1% of each run, Pallas kernels for 10% -> 20%
where the time goes in v3:
time: 611 us; the launch traced here: 604 us
  Pallas kernels  445 us (73%)
  other arithmetic  54.6 us (9%)
  matrix products  52.1 us (9%)
  local copies, waits for them, and re-layouts  32.1 us (5%)
  between operations  21.1 us (3%)
    pallas_call x3, Pallas kernels, scatter_tok(): pl.pallas_call(functools.partial(scatter_kernel, colours, ending), out_sh...  176 us
    pallas_call x3, Pallas kernels, gather_tok(): pl.pallas_call(functools.partial(gather_kernel, colours, swap, axes), out...  161 us
    pallas_call x1, Pallas kernels, run_backward(): pl.pallas_call(backward_kernel, out_shape=[jax.ShapeDtypeStruct((order.sh...  42 us
    pallas_call x2, Pallas kernels, sum_all(): pl.pallas_call(functools.partial(sum_kernel, axes, combine), out_shape=ja...  30.1 us
    pallas_call x1, Pallas kernels, run_forward(): pl.pallas_call(forward_kernel, out_shape=small + mats, in_specs=in_hbm(1)...  23.9 us
    dot_general x2, matrix products, matmul(): return jnp.dot(left, right, preferred_element_type=wide_type)  15.8 us
    unnamed x54, local copies, waits for them, and re-layouts  13.7 us
  transfers between devices with their start and end apart: 1, of which 0 were waited for; matrix products, arithmetic and copies ran while one was open for 1% of the time, Pallas kernels for 20%

profile of v3, /device:TPU:0, one launch (start us, length us, event | category | flops | bytes accessed | tf_op | source)
XLA Modules:
  0.0 604.4 jit_solution(5623404693685973473)
XLA Ops:
  7.3 0.9 fusion.40
  8.3 0.7 copy.62
  9.2 0.7 sub.116
  9.8 0.7 select_reduce_fusion.2
  10.5 0.7 multiply_add_fusion.5
  11.3 0.6 broadcast_in_dim.41
  12.0 12.2 %shard_map.283 = s32[4,4,2,1,128]{4,3,2,1,0:T(1,128)S(1)} custom-call(s32[1,128]{1,0:T(1,128)S(1)} %add_bitcast_fusion.1.value), custom_call_target="tpu_custom_call" | custom-call | tf_op jit(solution)/shard_map/pallas_call | solution.py:525
  24.2 0.7 slice_reduce_fusion
  25.0 0.7 fusion.28
  25.6 0.7 fusion.30
  26.3 0.7 fusion.32
  27.1 0.7 convert_element_type.116.refs_6_
  27.8 0.7 fusion.26
  29.0 0.7 compare_select_fusion
  29.7 1.0 select_reduce_fusion.1.refs_1_.refs_0_
  30.8 0.6 copy.79
  31.5 0.6 multiply_sine_fusion
  32.1 1.0 copy.64
  33.1 1.9 copy.65
  35.1 5.7 fusion.9
  40.9 26.7 %shard_map.284 = bf16[4,64,640]{2,1,0:T(8,128)(2,1)S(1)} custom-call(bf16[4,4,2,64,640]{4,3,2,1,0:T(8,128)(2,1)S(1)} %bitcast.110), custom_call_target="tpu_custom_call" | custom-call | tf_op jit(solution)/shard_map/pallas_call | solution.py:435
  67.8 2.4 fusion.8
  70.2 103.5 %shard_map.282 = bf16[4,4,2,3200,128]{4,3,2,1,0:T(8,128)(2,1)S(1)} custom-call(bf16[3200,128]{1,0:T(8,128)(2,1)S(1)} %bitcast.108), custom_call_target="tpu_custom_call" | custom-call | tf_op jit(solution)/shard_map/pallas_call | solution.py:264
  173.7 8.6 %copy-done.1 = bf16[4,4,2,3200,128]{4,3,2,1,0:T(8,128)(2,1)} copy-done((bf16[4,4,2,3200,128]{4,3,2,1,0:T(8,128)(2,1)}, bf16[4,4,2,3200,128]{4,3,2,1,0:T(8,128)(2,1)S(1)}, u32[]{:S(2)}) %copy-start.1) | copy-done | bytes 26214424
  182.4 0.7 add_convert_fusion.refs_8_
  183.1 0.9 fusion.14
  184.0 0.7 broadcast_in_dim.44
  184.7 23.9 %shard_map.285 = (bf16[128,640]{1,0:T(8,128)(2,1)}, f32[128,640]{1,0:T(8,128)}, f32[128,640]{1,0:T(8,128)}, f32[128,640]{1,0:T(8,128)}, f32[128,640]{1,0:T(8,128...) custom-call(bf16[800,128,128]{2,1,0:T(8,128)(2,1)} %bitcast.102, ...), custom_call_target="tpu_custom_call" | custom-call | tf_op jit(solution)/shard_map/pallas_call | solution.py:800
  208.6 0.9 copy-done.5
  209.5 31.8 %shard_map.286 = bf16[4,4,2,128,640]{4,3,2,1,0:T(8,128)(2,1)S(1)} custom-call(bf16[128,640]{1,0:T(8,128)(2,1)S(1)} %copy-done.5), custom_call_target="tpu_custom_call" | custom-call | tf_op jit(solution)/shard_map/pallas_call | solution.py:264
  241.3 10.5 %fusion.41 = (f32[32,4,32]{2,1,0:T(4,128)S(1)}, f32[32,4,32,1024]{3,2,1,0:T(8,128)S(1)}) fusion(bf16[32,4,32,640]{3,2,1,0:T(8,128)(2,1)S(1)} %bitcast.103, f32[1024,640]{1,0:T(8,128)} %param.32), kind=kOutput, calls=%fused_computation.112 | convolution fusion | flops 5373554688 | bytes 24657920 | tf_op jit(solution)/shard_map/td,vd->tv/dot_general | solution.py:1012
  251.8 0.7 select_reduce_fusion
  252.4 3.0 exponential_reduce_fusion
  255.4 3.3 exponential_bitcast_fusion.1
  258.7 3.8 fusion.3
  262.8 12.8 %shard_map.287 = f32[96,128]{1,0:T(8,128)S(1)} custom-call(f32[96,128]{1,0:T(8,128)S(1)} %reshape.468.value), custom_call_target="tpu_custom_call" | custom-call | tf_op jit(solution)/shard_map/pallas_call | solution.py:492
  276.6 4.8 exponential_bitcast_fusion
  281.4 10.6 %broadcast_in_dim.48 = f32[32,3,32,1024]{3,2,1,0:T(8,128)} broadcast(f32[32,32,1024]{2,1,0:T(8,128)} %exponential_bitcast_fusion), dimensions={0,2,3} | broadcast | bytes 16777216 | tf_op jit(solution)/shard_map/broadcast_in_dim | solution.py:1031
  292.0 0.9 copy-done.7
  292.9 10.7 %fusion.1 = bf16[32,4,32,1024]{3,2,1,0:T(8,128)(2,1)} fusion(f32[32,3,32,1024]{3,2,1,0:T(8,128)} %broadcast_in_dim.48, f32[32,1,32,1024]{3,2,1,0:T(8,128)} %fusion.8, f32[32,4,32,1024]{3,2,1,0:T(8,128)S(1)} %copy-done.7, f32[32,32]{1,0:T(8,128)S(1)} %get-tuple-element.83, f32[32,4,32]{2,1,0:T(4,128)S(1)} %copy.68), kind=kLoop, calls=%fused_computation.2 | loop fusion | flops 20971520 | bytes 41963520 | tf_op jit(solution)/shard_map/convert_element_type | solution.py:1041
  303.6 10.1 %convolution_convert_fusion = bf16[4096,640]{1,0:T(8,128)(2,1)S(1)} fusion(bf16[4096,1024]{1,0:T(8,128)(2,1)} %bitcast.122, f32[1024,640]{1,0:T(8,128)} %param.32), kind=kOutput, calls=%fused_computation.10 | convolution fusion | flops 5371985920 | bytes 16252928 | tf_op jit(solution)/shard_map/dot_general | solution.py:589
  313.7 7.1 %fusion.42 = f32[1024,640]{1,0:T(8,128)S(1)} fusion(bf16[4096,1024]{1,0:T(8,128)(2,1)S(1)} %bitcast.123, bf16[4096,640]{1,0:T(8,128)(2,1)S(1)} %bitcast.106), kind=kOutput, calls=%fused_computation.113 | convolution fusion | flops 5368709120 | bytes 16252928 | tf_op jit(solution)/shard_map/tv,td->vd/dot_general | solution.py:1044
  320.8 30.0 %shard_map.288 = bf16[4,32,640]{2,1,0:T(8,128)(2,1)S(1)} custom-call(bf16[4,4,2,128,640]{4,3,2,1,0:T(8,128)(2,1)S(1)} %bitcast.107), custom_call_target="tpu_custom_call" | custom-call | tf_op jit(solution)/shard_map/pallas_call | solution.py:435
  350.8 0.7 copy-done.3
  351.5 42.0 %shard_map.289 = (bf16[800,128,128]{2,1,0:T(8,128)(2,1)}, f32[16,640]{1,0:T(8,128)}, bf16[256,640]{1,0:T(8,128)(2,1)}) custom-call(s32[800]{0:T(1024)} %select_reduce_fusion.1.refs_1_.refs_0_, bf16[128,640]{1,0:T(8,128)(2,1)} %bitcast.112, f32[128,640]{1,0:T(8,128)} %get-tuple-element.90.refs_2_, f32[128,640]{1,0:T(8,128)} %get-tuple-element.89.refs_3_, ...), custom_call_target="tpu_custom_call" | custom-call | tf_op jit(solution)/shard_map/pallas_call | solution.py:916
  393.5 1.0 copy-done.4
  394.5 25.3 %shard_map.291 = bf16[4,4,2,64,640]{4,3,2,1,0:T(8,128)(2,1)S(1)} custom-call(bf16[256,640]{1,0:T(8,128)(2,1)S(1)} %copy-done.4), custom_call_target="tpu_custom_call" | custom-call | tf_op jit(solution)/shard_map/pallas_call | solution.py:264
  419.7 5.0 fusion.11
  424.8 0.8 copy-done.23
  425.6 119.2 %shard_map.290 = f32[3200,128]{1,0:T(8,128)} custom-call(bf16[4,4,2,3200,128]{4,3,2,1,0:T(8,128)(2,1)} %bitcast.121), custom_call_target="tpu_custom_call" | custom-call | tf_op jit(solution)/shard_map/pallas_call | solution.py:435
  544.9 0.6 fusion.24
  546.1 2.5 multiply_reduce_fusion.1
  548.6 3.0 multiply_reduce_fusion
  552.9 17.2 %shard_map.292 = f32[72,128]{1,0:T(8,128)S(1)} custom-call(f32[72,128]{1,0:T(8,128)S(1)} %maximum_bitcast_fusion.1.value), custom_call_target="tpu_custom_call" | custom-call | tf_op jit(solution)/shard_map/pallas_call | solution.py:492
  570.2 0.6 multiply_reduce_fusion.2
  570.8 0.5 fusion.39
  572.7 1.5 broadcast_multiply_fusion
  574.2 1.8 multiply_add_fusion.3
  576.2 4.0 multiply_add_fusion.1
  580.2 4.7 multiply_add_fusion.2
  584.9 1.6 fusion.43
  586.6 3.2 multiply_subtract_fusion.1
  589.9 0.7 multiply_subtract_fusion.2
  590.5 4.6 multiply_subtract_fusion
  (90 shorter events, 2.5 us)
Async XLA Ops:
  7.2 577.7 %copy-start = (f32[25,128,128]{2,1,0:T(8,128)S(1)}, f32[25,128,128]{2,1,0:T(8,128)}, u32[]{:S(2)}) copy-start(f32[25,128,128]{2,1,0:T(8,128)} %param.30) | copy-start | bytes 4915204
  7.2 27.8 %copy-start.10 = (f32[25,128,128]{2,1,0:T(8,128)S(1)}, f32[25,128,128]{2,1,0:T(8,128)}, u32[]{:S(2)}) copy-start(f32[25,128,128]{2,1,0:T(8,128)} %param.26) | copy-start | bytes 4915204
  7.2 541.4 %all-reduce.3.cloned.1.call-start = ((), (), s32[]{:S(2)}) async-start(), calls=%async_computation | async-start | bytes 5242880 | tf_op jit(solution)/shard_map/psum | solution.py:1053
  70.2 112.9 %copy-start.19 = (f32[128,640]{1,0:T(8,128)S(1)}, f32[128,640]{1,0:T(8,128)}, u32[]{:S(2)}) copy-start(f32[128,640]{1,0:T(8,128)} %copy.65) | copy-start | bytes 983044
  173.7 8.6 %copy-start.1 = (bf16[4,4,2,3200,128]{4,3,2,1,0:T(8,128)(2,1)}, bf16[4,4,2,3200,128]{4,3,2,1,0:T(8,128)(2,1)S(1)}, u32[]{:S(2)}) copy-start(bf16[4,4,2,3200,128]{4,3,2,1,0:T(8,128)(2,1)S(1)} %shard_map.282) | copy-start | bytes 78643200
  208.5 0.9 copy-start.5
  241.3 10.5 %copy-start.2 = (bf16[4,4,2,128,640]{4,3,2,1,0:T(8,128)(2,1)}, bf16[4,4,2,128,640]{4,3,2,1,0:T(8,128)(2,1)S(1)}, u32[]{:S(2)}) copy-start(bf16[4,4,2,128,640]{4,3,2,1,0:T(8,128)(2,1)S(1)} %shard_map.286) | copy-start | bytes 15728644
  251.8 7.0 %copy-start.6 = (f32[32,4,32,1024]{3,2,1,0:T(8,128)}, f32[32,4,32,1024]{3,2,1,0:T(8,128)S(1)}, u32[]{:S(2)}) copy-start(f32[32,4,32,1024]{3,2,1,0:T(8,128)S(1)} %get-tuple-element.106) | copy-start | bytes 50331652
  281.4 11.5 %copy-start.7 = (f32[32,4,32,1024]{3,2,1,0:T(8,128)S(1)}, f32[32,4,32,1024]{3,2,1,0:T(8,128)}, u32[]{:S(2)}) copy-start(f32[32,4,32,1024]{3,2,1,0:T(8,128)} %copy-done.6) | copy-start | bytes 50331652
  292.9 20.8 %slice-start = ((s8[5242880]{0:T(1024)(128)(4,1)}), s8[1048576]{0:T(1024)(128)(4,1)S(1)}, s32[]{:S(2)}) async-start(s8[5242880]{0:T(1024)(128)(4,1)} %bitcast.104), calls=%async_computation.1 | async-start | bytes 2097152
  303.6 10.1 %slice-start.1 = ((s8[5242880]{0:T(1024)(128)(4,1)}), s8[4194304]{0:T(1024)(128)(4,1)S(1)}, s32[]{:S(2)}) async-start(s8[5242880]{0:T(1024)(128)(4,1)} %bitcast.104), calls=%async_computation.2 | async-start | bytes 8388608
  303.6 10.1 %copy-start.9 = (bf16[32,4,32,1024]{3,2,1,0:T(8,128)(2,1)S(1)}, bf16[32,4,32,1024]{3,2,1,0:T(8,128)(2,1)}, u32[]{:S(2)}) copy-start(bf16[32,4,32,1024]{3,2,1,0:T(8,128)(2,1)} %fusion.1) | copy-start | bytes 25165828
  350.8 0.7 copy-start.3
  393.5 1.0 copy-start.4
  424.8 0.8 copy-start.23
  574.2 1.9 copy-start.16
  576.2 8.7 %copy-start.12 = (f32[25,128,128]{2,1,0:T(8,128)}, f32[25,128,128]{2,1,0:T(8,128)S(1)}, u32[]{:S(2)}) copy-start(f32[25,128,128]{2,1,0:T(8,128)S(1)} %multiply_add_fusion.3) | copy-start | bytes 4915204
  576.2 4.0 copy-start.17
  580.2 6.4 %copy-start.18 = (f32[25,128,128]{2,1,0:T(8,128)S(1)}, f32[25,128,128]{2,1,0:T(8,128)}, u32[]{:S(2)}) copy-start(f32[25,128,128]{2,1,0:T(8,128)} %param.31) | copy-start | bytes 4915204
  580.2 10.4 %copy-start.15 = (f32[1024,640]{1,0:T(8,128)S(1)}, f32[1024,640]{1,0:T(8,128)}, u32[]{:S(2)}) copy-start(f32[1024,640]{1,0:T(8,128)} %param.34) | copy-start | bytes 7864324
  584.9 1.7 copy-start.11
  584.9 5.7 copy-start.14
  586.5 3.3 copy-start.20
  586.6 3.3 copy-start.21
  586.6 3.3 copy-start.22
  586.6 3.9 copy-start.8
  586.6 3.9 copy-start.13
Sparse Core Ops, SparseCore 0:
  424.9 99.7 all-reduce.2

commit v4 on v3

--- a/solution.py
+++ b/solution.py
@@ -1,4 +1,5 @@
 import functools
+import heapq
 import math
 
 import jax
@@ -100,16 +101,32 @@
 
 
 def in_turn(steps):
-    steps = list(steps)
-    while steps:
-        kept = []
-        for step in steps:
-            try:
-                next(step)
-                kept.append(step)
-            except StopIteration:
-                pass
-        steps = kept
+    heap, number, left = [], 0, {}
+    for step in steps:
+        heap.append((0, number, step, None))
+        number += 1
+    heapq.heapify(heap)
+    while heap:
+        now, own, step, parent = heapq.heappop(heap)
+        try:
+            given = next(step)
+        except StopIteration:
+            if parent is not None:
+                left[parent][0] -= 1
+                if left[parent][0] == 0:
+                    heapq.heappush(heap, (now, *left.pop(parent)[1]))
+            continue
+        if isinstance(given, list):
+            left[own] = [len(given), (own, step, parent)]
+            for child in given:
+                heapq.heappush(heap, (now, number, child, own))
+                number += 1
+        else:
+            heapq.heappush(heap, (now + given, own, step, parent))
+
+
+def size_of(ref):
+    return math.prod(ref.shape) * jnp.dtype(ref.dtype).itemsize
 
 
 def rows_of(start, count, half):
@@ -155,21 +172,61 @@
 
 def ring_gather(part, axis, copies, arrived):
     me, right, left, far = around(axis)
+    block = size_of(part(me, None))
     first = copies.push(part(me, None), part(me, None), axis, right)
     second = copies.push(part(me, None), part(me, None), axis, left)
-    yield
+    yield block
     first.wait_recv()
     third = copies.push(part(left, 0), part(left, 0), axis, right)
     arrived(part(left, None))
-    yield
+    yield 0
     second.wait_recv()
     fourth = copies.push(part(right, 1), part(right, 1), axis, left)
     arrived(part(right, None))
-    yield
+    yield block // 2
     third.wait_recv()
     fourth.wait_recv()
     arrived(part(far, None))
-    yield
+    yield 0
+
+
+def gather_flows(colours, value, out, copies):
+    z, x, c = (lax.axis_index(a) for a in ("tok_0", "tok_1", CORE))
+    crossing = []
+
+    def arrived(ref):
+        crossing.append(copies.push(ref, ref, CORE, 1 - c))
+
+    own = []
+    for order, (start, count) in colours:
+        if "y" in order:
+            count = count // 4
+            start = start + lax.axis_index("sub") * count
+        own.append(
+            (
+                view(value, (), (start, count)),
+                view(out, (z, x, c), (start, count)),
+            )
+        )
+    for copy in [copies.move(*pair) for pair in own]:
+        copy.wait()
+
+    def run(order, rows, ref):
+        by_sub = "y" in order
+        for stage, name in enumerate(order):
+            part = places(order, stage, rows, by_sub)
+
+            def here(i, half, part=part):
+                (first, second), span = part(i, half, True)
+                return view(out, (first, second, c), span)
+
+            steps = ring_gather(here, RING[name], copies, arrived)
+            if stage == 0:
+                yield next(steps)
+                arrived(ref)
+            yield from steps
+
+    return [run(*colour, ref) for colour, (_, ref) in zip(colours, own)], crossing
 
 
 def gather_kernel(colours, swap, axes, value, *refs):
@@ -178,7 +235,6 @@
     else:
         out, *refs = refs
     copies = Copies(*refs)
-    z, x, c = (lax.axis_index(a) for a in ("tok_0", "tok_1", CORE))
     greet(axes)
     if swap:
         me = lax.axis_index("sub")
@@ -202,42 +258,8 @@
                 added = added + mine[pl.ds(k * piece, piece)].astype(jnp.float32)
             joined[...] = added.astype(joined.dtype)
             value = joined
-    crossing = []
-
-    def arrived(ref):
-        crossing.append(copies.push(ref, ref, CORE, 1 - c))
-
-    own = []
-    for order, (start, count) in colours:
-        if "y" in order:
-            count = count // 4
-            start = start + lax.axis_index("sub") * count
-        own.append(
-            (
-                view(value, (), (start, count)),
-                view(out, (z, x, c), (start, count)),
-            )
-        )
-    for copy in [copies.move(*pair) for pair in own]:
-        copy.wait()
-
-    def run(order, rows):
-        by_sub = "y" in order
-        for stage, name in enumerate(order):
-            part = places(order, stage, rows, by_sub)
-
-            def here(i, half, part=part):
-                (first, second), span = part(i, half, True)
-                return view(out, (first, second, c), span)
-
-            yield from ring_gather(here, RING[name], copies, arrived)
-
-    steps = [run(order, rows) for order, rows in colours]
-    for step in steps:
-        next(step)
-    for _, ref in own:
-        arrived(ref)
-    in_turn(steps)
+    flows, crossing = gather_flows(colours, value, out, copies)
+    in_turn(flows)
     for copy in crossing:
         copy.wait_recv()
     copies.finish()
@@ -298,15 +320,42 @@
         target[...] = value
 
 
-def scatter_kernel(colours, ending, value, out, total, other, *refs):
-    count = sum(len(order) for order, _ in colours) * 6
-    slots, refs = refs[:count], refs[count:]
-    if ending != "gather":
-        mine, *refs = refs
-    copies = Copies(*refs)
+def ring_scatter(here, slots, axis, copies, ready, done):
+    me, right, left, far = around(axis)
+    r1_in, l1_in, r2_in, l2_in, r3_in, l3_in = slots
+    half = size_of(r1_in)
+    ready(0)
+    r1 = copies.push(here(far, 0), r1_in, axis, right)
+    l1 = copies.push(here(far, 1), l1_in, axis, left)
+    yield 0
+    ready(1)
+    r2 = copies.push(here(right, 1), r2_in, axis, right)
+    yield 0
+    ready(2)
+    l2 = copies.push(here(left, 0), l2_in, axis, left)
+    yield half
+    r1.wait_recv()
+    add_to(here(right, 0), r1_in)
+    r3 = copies.push(here(right, 0), r3_in, axis, right)
+    yield 0
+    l1.wait_recv()
+    add_to(here(left, 1), l1_in)
+    l3 = copies.push(here(left, 1), l3_in, axis, left)
+    yield half
+    ready(3)
+    l2.wait_recv()
+    r2.wait_recv()
+    yield half
+    r3.wait_recv()
+    done(0, l2_in, r3_in)
+    yield 0
+    l3.wait_recv()
+    done(1, r2_in, l3_in)
+    yield 0
+
+
+def scatter_flows(colours, ending, value, out, mine, total, other, slots, copies):
     c = lax.axis_index(CORE)
-    me_y = lax.axis_index("sub")
-    greet((CORE, "tok_0", "tok_1", "sub"))
     pending = {}
     for turn in range(4):
         for k, (order, rows) in enumerate(colours):
@@ -327,57 +376,32 @@
                 view(other, (first, second), span),
             )
 
-    def ready(k, turn):
-        across, inside, ours, theirs = pending[k, turn]
-        inside.wait()
-        across.wait_recv()
-        add_to(ours, theirs)
-
     def run(k, order, rows):
         at = 6 * sum(len(o) for o, _ in colours[:k])
+
+        def nothing(turn):
+            pass
+
+        def ready(turn):
+            across, inside, ours, theirs = pending[k, turn]
+            inside.wait()
+            across.wait_recv()
+            add_to(ours, theirs)
+
         for stage, name in enumerate(order):
             part = places(order, stage, rows, "y" in order)
             axis = RING[name]
-            me, right, left, far = around(axis)
-            r1_in, l1_in, r2_in, l2_in, r3_in, l3_in = slots[at : at + 6]
-            at += 6
+            me = lax.axis_index(axis)
 
             def here(i, half, part=part):
                 lead, span = part(i, half, False)
                 return view(total, lead, span)
 
-            if stage == 0:
-                ready(k, 0)
-            r1 = copies.push(here(far, 0), r1_in, axis, right)
-            l1 = copies.push(here(far, 1), l1_in, axis, left)
-            yield
-            if stage == 0:
-                ready(k, 1)
-            r2 = copies.push(here(right, 1), r2_in, axis, right)
-            if stage == 0:
-                ready(k, 2)
-            l2 = copies.push(here(left, 0), l2_in, axis, left)
-            yield
-            r1.wait_recv()
-            add_to(here(right, 0), r1_in)
-            r3 = copies.push(here(right, 0), r3_in, axis, right)
-            l1.wait_recv()
-            add_to(here(left, 1), l1_in)
-            l3 = copies.push(here(left, 1), l3_in, axis, left)
-            yield
-            if stage == 0:
-                ready(k, 3)
-            l2.wait_recv()
-            r2.wait_recv()
-            yield
-            r3.wait_recv()
-            l3.wait_recv()
-            last = stage == len(order) - 1
-            for half, one, two in ((0, l2_in, r3_in), (1, r2_in, l3_in)):
-                if not last:
+            def done(half, one, two, part=part, here=here, me=me, stage=stage):
+                if stage < len(order) - 1:
                     add_to(here(me, half), one, two)
-                    continue
-                lead, (start, size) = part(me, half, False)
+                    return
+                _, (start, size) = part(me, half, False)
                 value = here(me, half)[...].astype(jnp.float32)
                 value = value + one[...].astype(jnp.float32) + two[...].astype(jnp.float32)
                 if not isinstance(start, int):
@@ -386,7 +410,11 @@
                     mine[pl.ds(start, size)] = value.astype(mine.dtype)
                 else:
                     out[pl.ds(start, size)] = value
-            yield
+
+            yield from ring_scatter(
+                here, slots[at : at + 6], axis, copies, nothing if stage else ready, done
+            )
+            at += 6
         if ending == "gather":
             start, size = rows
             piece = size // 4
@@ -396,28 +424,72 @@
 
             yield from ring_gather(held, "sub", copies, lambda ref: None)
 
-    in_turn([run(k, order, rows) for k, (order, rows) in enumerate(colours)])
+    return [run(k, order, rows) for k, (order, rows) in enumerate(colours)]
+
+
+def to_sub(ending, mine, out, copies):
+    me = lax.axis_index("sub")
+    piece = mine.shape[0] // 4
+
+    def given(peer):
+        if ending == "spread":
+            return mine
+        return mine.at[pl.ds(pl.multiple_of(peer * piece, 16), piece)]
+
+    local = copies.move(given(me), out.at[me])
+    arrivals = [
+        copies.push(given(peer), out.at[me], "sub", peer)
+        for peer in (lax.rem(me + k, 4) for k in (1, 3, 2))
+    ]
+    yield size_of(mine)
+    local.wait()
+    for copy in arrivals:
+        copy.wait_recv()
+
+
+def scatter_kernel(colours, ending, value, *refs):
+    if ending == "gather":
+        table, out, table_out, total, other, table_in, *refs = refs
+    else:
+        out, total, other, *refs = refs
+    count = sum(len(order) for order, _ in colours) * 6
+    slots, refs = refs[:count], refs[count:]
+    mine = None
+    if ending == "gather":
+        table_slots, refs = refs[:6], refs[6:]
+    else:
+        mine, *refs = refs
+    copies = Copies(*refs)
+    greet((CORE, "tok_0", "tok_1", "sub"))
+    flows = scatter_flows(colours, ending, value, out, mine, total, other, slots, copies)
+    if ending == "gather":
+        loaded = copies.move(table, table_in)
+        piece = table.shape[0] // 4
+
+        def table_flow():
+            me = lax.axis_index("sub")
+            loaded.wait()
+
+            def here(i, half):
+                return view(table_in, (), rows_of(i * piece, piece, half))
+
+            def there(i, half):
+                return view(table_out, (), rows_of(i * piece, piece, half))
+
+            def done(half, one, two):
+                there(me, half)[...] = here(me, half)[...] + one[...] + two[...]
+
+            yield from ring_scatter(here, table_slots, "sub", copies, lambda turn: None, done)
+            yield from ring_gather(there, "sub", copies, lambda ref: None)
+
+        flows = [table_flow(), *flows]
+    in_turn(flows)
     if ending != "gather":
-        piece = mine.shape[0] // 4
-
-        def given(peer):
-            if ending == "spread":
-                return mine
-            return mine.at[pl.ds(pl.multiple_of(peer * piece, 16), piece)]
-
-        local = copies.move(given(me_y), out.at[me_y])
-        arrivals = [
-            copies.push(given(peer), out.at[me_y], "sub", peer)
-            for peer in (lax.rem(me_y + k, 4) for k in (1, 3, 2))
-        ]
-        local.wait()
-        for copy in arrivals:
-            copy.wait_recv()
+        in_turn([to_sub(ending, mine, out, copies)])
     copies.finish()
 
 
-def scatter_tok(value, number, colours, ending, limit):
-    rows, lanes = value.shape[3:]
+def scatter_slots(colours, lanes, kind):
     slots = []
     for order, (_, size) in colours:
         piece = size // 4 if "y" in order else size
@@ -427,24 +499,112 @@
             lead.pop(name, None)
             seen_y = seen_y or name == "y"
             height = (piece if seen_y else size) // 2
-            slots += [pltpu.VMEM((*lead.values(), height, lanes), value.dtype)] * 6
+            slots += [pltpu.VMEM((*lead.values(), height, lanes), kind)] * 6
+    return slots
+
+
+def scatter_tok(value, number, colours, ending, limit, table=None):
+    rows, lanes = value.shape[3:]
+    slots = scatter_slots(colours, lanes, value.dtype)
     stages = len(slots) // 6
-    mine = [] if ending == "gather" else [pltpu.VMEM((rows, lanes), value.dtype)]
     shape = {"gather": (rows, lanes), "spread": (4, rows, lanes), "swap": (4, rows // 4, lanes)}
     kind = jnp.float32 if ending == "gather" else value.dtype
-    return pl.pallas_call(
+    outs = [jax.ShapeDtypeStruct(shape[ending], kind)]
+    scratch = [pltpu.VMEM((4, 4, rows, lanes), value.dtype)] * 2
+    given = [value]
+    if table is None:
+        scratch += slots + [pltpu.VMEM((rows, lanes), value.dtype)]
+    else:
+        height, across = table.shape
+        given.append(table)
+        outs.append(jax.ShapeDtypeStruct(table.shape, table.dtype))
+        scratch += [pltpu.VMEM(table.shape, table.dtype)] + slots
+        scratch += [pltpu.VMEM((height // 8, across), table.dtype)] * 6
+    result = pl.pallas_call(
         functools.partial(scatter_kernel, colours, ending),
-        out_shape=jax.ShapeDtypeStruct(shape[ending], kind),
-        in_specs=[pl.BlockSpec(memory_space=pltpu.HBM)],
-        out_specs=pl.BlockSpec(memory_space=pltpu.VMEM),
-        scratch_shapes=[pltpu.VMEM((4, 4, rows, lanes), value.dtype)] * 2
-        + slots
-        + mine
-        + semaphores(6 * stages + 8 * len(colours) + 4, 4 * len(colours) + 1),
+        out_shape=outs,
+        in_specs=[pl.BlockSpec(memory_space=pltpu.HBM)] * len(given),
+        out_specs=[pl.BlockSpec(memory_space=pltpu.VMEM)] * len(outs),
+        scratch_shapes=scratch
+        + semaphores(6 * stages + 8 * len(colours) + 14, 4 * len(colours) + 2),
         compiler_params=pltpu.CompilerParams(
             collective_id=number, has_side_effects=True, vmem_limit_bytes=limit
         ),
-    )(value)
+    )(*given)
+    return result if table is not None else result[0]
+
+
+def open_kernel(weight_ways, row_ways, mine, table, blocks, ids, rows, slots, *refs):
+    picked, total, other, held, *refs = refs
+    count = sum(len(order) for order, _ in row_ways) * 6
+    inbox, refs = refs[:count], refs[count:]
+    copies = Copies(*refs)
+    greet((CORE, "tok_0", "tok_1", "sub"))
+    flows, crossing = gather_flows(weight_ways, blocks, slots, copies)
+    axes = ("tok_0", "tok_1", CORE)
+    shard_rows = table.shape[0]
+    slot_rows = picked.shape[3]
+
+    def row_flow():
+        spot = tuple(lax.axis_index(axis) for axis in axes)
+        copies.move(mine, ids.at[spot]).wait()
+        for depth in reversed(range(3)):
+            axis = axes[depth]
+            block = ids.at[spot[: depth + 1]]
+            arrivals = [
+                copies.push(block, block, axis, lax.rem(spot[depth] + k, lax.axis_size(axis)))
+                for k in range(1, lax.axis_size(axis))
+            ]
+            yield 1
+            for copy in arrivals:
+                copy.wait_recv()
+        first_row = lax.axis_index(axes) * shard_rows
+        numbers = lax.broadcasted_iota(jnp.int32, (shard_rows, HALF), 0) + first_row
+
+        def pick(k, carry):
+            z, x, c = lax.div(k, 8), lax.rem(lax.div(k, 2), 4), lax.rem(k, 2)
+            hits = (numbers == ids[z, x, c]).astype(jnp.float32).astype(low_type)
+            found = tn(hits, table[...])
+            picked[z, x, c] = found[:slot_rows].astype(low_type)
+            return carry
+
+        lax.fori_loop(0, 32, pick, 0)
+        yield scatter_flows(row_ways, "spread", picked, None, held, total, other, inbox, copies)
+        yield from to_sub("spread", held, rows, copies)
+
+    in_turn([*flows, row_flow()])
+    for copy in crossing:
+        copy.wait_recv()
+    copies.finish()
+
+
+def open_exchange(mine, table, blocks, number, weight_ways, row_ways, slot_rows):
+    lanes = table.shape[1]
+    inbox = scatter_slots(row_ways, lanes, low_type)
+    stages = sum(len(order) for order, _ in weight_ways)
+    return pl.pallas_call(
+        functools.partial(open_kernel, weight_ways, row_ways),
+        out_shape=[
+            jax.ShapeDtypeStruct((4, 4, 2, *mine.shape), mine.dtype),
+            jax.ShapeDtypeStruct((4, slot_rows, lanes), low_type),
+            jax.ShapeDtypeStruct((4, 4, 2, *blocks.shape), blocks.dtype),
+        ],
+        in_specs=[pl.BlockSpec(memory_space=pltpu.VMEM)] * 2
+        + [pl.BlockSpec(memory_space=pltpu.HBM)],
+        out_specs=[pl.BlockSpec(memory_space=pltpu.VMEM)] * 2
+        + [pl.BlockSpec(memory_space=pltpu.HBM)],
+        scratch_shapes=[
+            pltpu.VMEM((4, 4, 2, slot_rows, lanes), low_type),
+            pltpu.VMEM((4, 4, slot_rows, lanes), low_type),
+            pltpu.VMEM((4, 4, slot_rows, lanes), low_type),
+            pltpu.VMEM((slot_rows, lanes), low_type),
+        ]
+        + inbox
+        + semaphores(7 * stages + 8 + 7 + len(inbox) + 8 + 4, 16),
+        compiler_params=pltpu.CompilerParams(
+            collective_id=number, has_side_effects=True, vmem_limit_bytes=56 * MIB
+        ),
+    )(mine, table, blocks)
 
 
 def added(values):
@@ -502,38 +662,6 @@
     )(value)
 
 
-def push_kernel(axes, value, out, send, recv, local):
-    greet(axes)
-    copies = Copies(send, recv, local)
-    spot = tuple(lax.axis_index(axis) for axis in axes)
-    copies.move(value, out.at[spot]).wait()
-    for depth in reversed(range(len(axes))):
-        axis = axes[depth]
-        held = out.at[spot[: depth + 1]]
-        arrivals = [
-            copies.push(held, held, axis, lax.rem(spot[depth] + k, lax.axis_size(axis)))
-            for k in range(1, lax.axis_size(axis))
-        ]
-        for copy in arrivals:
-            copy.wait_recv()
-    copies.finish()
-
-
-def push_all(value, number, axes):
-    counts = [lax.axis_size(axis) for axis in axes]
-    sends = sum(counts) - len(axes)
-    return pl.pallas_call(
-        functools.partial(push_kernel, axes),
-        out_shape=jax.ShapeDtypeStruct((*counts, *value.shape), value.dtype),
-        in_specs=[pl.BlockSpec(memory_space=pltpu.VMEM)],
-        out_specs=pl.BlockSpec(memory_space=pltpu.VMEM),
-        scratch_shapes=semaphores(sends, 1),
-        compiler_params=pltpu.CompilerParams(
-            collective_id=number, has_side_effects=True, vmem_limit_bytes=16 * MIB
-        ),
-    )(value)
-
-
 def both_ways(rows):
     return ((("z", "x"), (0, rows // 2)), (("x", "z"), (rows // 2, rows // 2)))
 
@@ -544,7 +672,7 @@
 
 
 WEIGHT_WAYS = three_ways(896, 896, 1408, (("z", "x"), ("x", "z"), ("x", "z", "y")))
-GRAD_WAYS = three_ways(1024, 1024, 1152, (("z", "x", "y"), ("x", "y", "z"), ("y", "z", "x")))
+GRAD_WAYS = ((("z", "x", "y"), (0, 1664)), (("x", "z", "y"), (1664, 1536)))
 
 
 def doc_layout(lengths):
@@ -979,17 +1107,24 @@
         ]
     )
     table_low = table.astype(low_type)
-    heads_up = push_all(mine.reshape(1, HALF), 1, TOK).reshape(shards, HALF)
-    slots = gather_tok(master.astype(low_type).reshape(-1, BLK), 2, WEIGHT_WAYS)
+    heads_up, rows, slots = open_exchange(
+        mine.reshape(1, HALF),
+        table_low,
+        master.astype(low_type).reshape(-1, BLK),
+        1,
+        WEIGHT_WAYS,
+        both_ways(2 * piece),
+        2 * piece,
+    )
+    heads_up = heads_up.reshape(shards, HALF)
     slots = slots.reshape(-1, BLK, BLK)
+    rows = rows.astype(jnp.float32)
     all_targets = heads_up[:, 2 * piece : 3 * piece]
     weight = (all_targets >= 0).astype(jnp.float32)
     token_count = jnp.sum(heads_up[:, 3 * piece]).astype(jnp.float32)
     first_row = place * shard_rows
     local = (heads_up[:, : 2 * piece] - first_row).reshape(-1)
     picks = (local[:, None] == jnp.arange(shard_rows, dtype=jnp.int32)).astype(low_type)
-    picked = matmul(picks, table_low).astype(low_type).reshape(4, 4, 2, 2 * piece, D)
-    rows = scatter_tok(picked, 3, both_ways(2 * piece), "spread", 32 * MIB).astype(jnp.float32)
     rows = rows.reshape(groups, 2, piece, D).transpose(1, 0, 2, 3).reshape(2, HALF, D)
     used = slot_block < NBLK
     ranks = jnp.cumsum(1 - used.astype(jnp.int32)) - 1
@@ -1050,10 +1185,10 @@
     table_grad = table_grad + jnp.einsum(
         "rv,rd->vd", picks, all_rows, preferred_element_type=wide_type
     )
-    table_grad = lax.psum(table_grad, "sub")
-    own = scatter_tok(
-        slot_grads.reshape(4, 4, 2, -1, BLK), 8, GRAD_WAYS, "gather", 60 * MIB
-    ).reshape(master.shape)
+    own, table_grad = scatter_tok(
+        slot_grads.reshape(4, 4, 2, -1, BLK), 8, GRAD_WAYS, "gather", 60 * MIB, table_grad
+    )
+    own = own.reshape(master.shape)
     square = jnp.sum(own * own) + jnp.sum(table_grad * table_grad)
     small = jnp.concatenate(
         [

time: 611 us -> 585 us (0.957)
  local copies, waits for them, and re-layouts: 32.1 us -> 17.5 us
  between operations: 21.1 us -> 7.63 us
  Pallas kernels: 445 us -> 455 us
  matrix products: 52.1 us -> 43 us
    pallas_call x1, Pallas kernels: 12.2 us -> 157 us  [open_exchange(): pl.pallas_call(functools.partial(open_kernel, weight_ways, row_ways), out...]
    pallas_call x3 -> x2, Pallas kernels: 161 us -> 57.7 us  [gather_tok(): pl.pallas_call(functools.partial(gather_kernel, colours, swap, axes), out...]
    pallas_call x3 -> x2, Pallas kernels: 176 us -> 145 us  [scatter_tok(): pl.pallas_call(functools.partial(scatter_kernel, colours, ending), out_sh...]
    dot_general x2 -> x1, matrix products: 15.8 us -> 6.96 us  [matmul(): return jnp.dot(left, right, preferred_element_type=wide_type)]
    unnamed x54, local copies, waits for them, and re-layouts: 13.7 us -> 5.14 us
    broadcast_in_dim x1, local copies, waits for them, and re-layouts: 10.6 us -> 3.86 us  [on_device(): jnp.broadcast_to(jnp.exp(teacher - logs[:, :1, :, None]), (shards, groups...]
  transfers between devices with their start and end apart: 1 -> 0, of which waited for: 0 -> 0; matrix products, arithmetic and copies ran while one was open for 1% -> 0% of each run, Pallas kernels for 20% -> 0%
where the time goes in v4:
time: 585 us; the launch traced here: 581 us
  Pallas kernels  455 us (78%)
  other arithmetic  58.6 us (10%)
  matrix products  43 us (7%)
  local copies, waits for them, and re-layouts  17.5 us (3%)
  between operations  7.63 us (1%)
    pallas_call x1, Pallas kernels, open_exchange(): pl.pallas_call(functools.partial(open_kernel, weight_ways, row_ways), out...  157 us
    pallas_call x2, Pallas kernels, scatter_tok(): pl.pallas_call(functools.partial(scatter_kernel, colours, ending), out_sh...  145 us
    pallas_call x2, Pallas kernels, gather_tok(): pl.pallas_call(functools.partial(gather_kernel, colours, swap, axes), out...  57.7 us
    pallas_call x1, Pallas kernels, run_backward(): pl.pallas_call(backward_kernel, out_shape=[jax.ShapeDtypeStruct((order.sh...  41.9 us
    pallas_call x2, Pallas kernels, sum_all(): pl.pallas_call(functools.partial(sum_kernel, axes, combine), out_shape=ja...  28.8 us
    pallas_call x1, Pallas kernels, run_forward(): pl.pallas_call(forward_kernel, out_shape=small + mats, in_specs=in_hbm(1)...  23.7 us
    convert_element_type x1, other arithmetic, on_device(): back = back.astype(low_type).reshape(-1, shard_rows)  12.2 us

profile of v4, /device:TPU:0, one launch (start us, length us, event | category | flops | bytes accessed | tf_op | source)
XLA Modules:
  0.0 581.4 jit_solution(17895934084599021205)
XLA Ops:
  0.7 0.8 fusion.25
  1.5 0.7 fusion.27
  2.3 0.7 fusion.29
  3.0 0.8 fusion.34
  3.9 0.7 convert_element_type.112.refs_6_
  4.6 0.7 fusion.23
  5.9 0.7 compare_select_fusion
  6.6 1.0 select_reduce_fusion.1.refs_1_.refs_0_
  8.2 0.7 copy.62
  9.1 0.7 sub.116
  9.8 0.7 select_reduce_fusion.2
  10.5 0.6 broadcast_in_dim.41
  11.1 0.7 multiply_add_fusion.5
  12.5 0.7 broadcast_in_dim.44
  13.2 0.7 add_convert_fusion.refs_8_
  13.9 0.6 multiply_sine_fusion
  14.6 1.0 copy.64
  15.6 1.9 copy.65
  17.4 1.0 convert_element_type.104
  18.5 2.9 convert_element_type.103.table
  21.4 157.4 %shard_map.282 = (s32[4,4,2,1,128]{4,3,2,1,0:T(1,128)}, bf16[4,64,640]{2,1,0:T(8,128)(2,1)}, bf16[4,4,2,3200,128]{4,3,2,1,0:T(8,128)(2,1)}) custom-call(s32[1,128]{1,0:T(1,128)} %add_bitcast_fusion.1.mine, bf16[1024,640]{1,0:T(8,128)(2,1)} %convert_element_type.103.table, bf16[3200,128]{1,0:T(8,128)(2,1)} %bitcast.117), custom_call_target="tpu_custom_call" | custom-call | tf_op jit(solution)/shard_map/pallas_call | solution.py:585
  178.8 1.4 slice_reduce_fusion
  181.0 0.8 slice_subtract_fusion.2
  181.8 0.7 slice_subtract_fusion.1
  182.6 0.8 broadcast_select_fusion
  183.4 1.0 copy_bitcast_fusion
  184.5 0.9 fusion.11
  185.4 2.3 fusion.6
  187.7 23.7 %shard_map.283 = (bf16[128,640]{1,0:T(8,128)(2,1)}, f32[128,640]{1,0:T(8,128)}, f32[128,640]{1,0:T(8,128)}, f32[128,640]{1,0:T(8,128)}, f32[128,640]{1,0:T(8,128...) custom-call(bf16[800,128,128]{2,1,0:T(8,128)(2,1)} %bitcast.113, ...), custom_call_target="tpu_custom_call" | custom-call | tf_op jit(solution)/shard_map/pallas_call | solution.py:928
  211.4 0.9 copy-done.4
  212.3 31.8 %shard_map.284 = bf16[4,4,2,128,640]{4,3,2,1,0:T(8,128)(2,1)S(1)} custom-call(bf16[128,640]{1,0:T(8,128)(2,1)S(1)} %copy-done.4), custom_call_target="tpu_custom_call" | custom-call | tf_op jit(solution)/shard_map/pallas_call | solution.py:286
  244.1 7.1 %fusion.35 = (f32[32,4,32]{2,1,0:T(4,128)S(1)}, f32[32,4,32,1024]{3,2,1,0:T(8,128)S(1)}) fusion(bf16[32,4,32,640]{3,2,1,0:T(8,128)(2,1)S(1)} %bitcast.102, bf16[1024,640]{1,0:T(8,128)(2,1)S(1)} %copy-done.13), kind=kOutput, calls=%fused_computation.106 | convolution fusion | flops 5372899328 | bytes 23347200 | tf_op jit(solution)/shard_map/td,vd->tv/dot_general | solution.py:1147
  251.1 0.7 select_reduce_fusion
  251.8 3.1 exponential_reduce_fusion
  254.9 0.9 exponential_bitcast_fusion.1
  255.9 1.0 copy-done.5
  256.9 1.8 fusion.3
  258.9 12.8 %shard_map.285 = f32[96,128]{1,0:T(8,128)S(1)} custom-call(f32[96,128]{1,0:T(8,128)S(1)} %reshape.464.value), custom_call_target="tpu_custom_call" | custom-call | tf_op jit(solution)/shard_map/pallas_call | solution.py:652
  271.9 0.6 fusion.21
  273.3 4.7 exponential_bitcast_fusion
  278.0 3.9 broadcast_in_dim.48
  281.9 12.2 %fusion.1 = bf16[32,4,32,1024]{3,2,1,0:T(8,128)(2,1)} fusion(f32[32,3,32,1024]{3,2,1,0:T(8,128)S(1)} %broadcast_in_dim.48, f32[32,1,32,1024]{3,2,1,0:T(8,128)} %fusion.6, f32[32,4,32,1024]{3,2,1,0:T(8,128)} %copy-done.5, f32[32,32]{1,0:T(8,128)S(1)} %get-tuple-element.93, f32[32,4,32]{2,1,0:T(4,128)S(1)} %copy.68), kind=kLoop, calls=%fused_computation.2 | loop fusion | flops 20971520 | bytes 41963520 | tf_op jit(solution)/shard_map/convert_element_type | solution.py:1176
  294.1 10.4 %fusion.36 = f32[1024,640]{1,0:T(8,128)} fusion(bf16[4096,1024]{1,0:T(8,128)(2,1)} %bitcast.115, bf16[4096,640]{1,0:T(8,128)(2,1)S(1)} %bitcast.105), kind=kOutput, calls=%fused_computation.107 | convolution fusion | flops 5368709120 | bytes 16252928 | tf_op jit(solution)/shard_map/tv,td->vd/dot_general | solution.py:1179
  304.5 7.0 %convolution_convert_fusion = bf16[4096,640]{1,0:T(8,128)(2,1)S(1)} fusion(bf16[4096,1024]{1,0:T(8,128)(2,1)S(1)} %bitcast.116, bf16[1024,640]{1,0:T(8,128)(2,1)S(1)} %copy-done.13), kind=kOutput, calls=%fused_computation.9 | convolution fusion | flops 5371330560 | bytes 14942208 | tf_op jit(solution)/shard_map/dot_general | solution.py:717
  311.4 28.7 %shard_map.286 = bf16[4,32,640]{2,1,0:T(8,128)(2,1)S(1)} custom-call(bf16[4,4,2,128,640]{4,3,2,1,0:T(8,128)(2,1)S(1)} %bitcast.106), custom_call_target="tpu_custom_call" | custom-call | tf_op jit(solution)/shard_map/pallas_call | solution.py:523
  340.1 0.7 copy-done.2
  340.8 41.9 %shard_map.287 = (bf16[800,128,128]{2,1,0:T(8,128)(2,1)}, f32[16,640]{1,0:T(8,128)}, bf16[256,640]{1,0:T(8,128)(2,1)}) custom-call(s32[800]{0:T(1024)} %select_reduce_fusion.1.refs_1_.refs_0_, bf16[128,640]{1,0:T(8,128)(2,1)} %bitcast.108, f32[128,640]{1,0:T(8,128)} %get-tuple-element.100.refs_2_, f32[128,640]{1,0:T(8,128)} %get-tuple-element.99.refs_3_, ...), custom_call_target="tpu_custom_call" | custom-call | tf_op jit(solution)/shard_map/pallas_call | solution.py:1044
  382.7 0.8 reshape.469
  383.5 1.0 copy-done.3
  384.5 26.0 %shard_map.288 = bf16[4,4,2,64,640]{4,3,2,1,0:T(8,128)(2,1)S(1)} custom-call(bf16[256,640]{1,0:T(8,128)(2,1)S(1)} %copy-done.3), custom_call_target="tpu_custom_call" | custom-call | tf_op jit(solution)/shard_map/pallas_call | solution.py:286
  410.5 5.0 fusion.8.refs_0_
  415.5 116.3 %shard_map.289 = (f32[3200,128]{1,0:T(8,128)}, f32[1024,640]{1,0:T(8,128)}) custom-call(bf16[4,4,2,3200,128]{4,3,2,1,0:T(8,128)(2,1)} %bitcast.114, f32[1024,640]{1,0:T(8,128)} %fusion.8.refs_0_), custom_call_target="tpu_custom_call" | custom-call | tf_op jit(solution)/shard_map/pallas_call | solution.py:523
  531.9 3.1 multiply_reduce_fusion
  535.0 1.0 multiply_reduce_fusion.1
  537.4 16.0 %shard_map.290 = f32[72,128]{1,0:T(8,128)S(1)} custom-call(f32[72,128]{1,0:T(8,128)S(1)} %maximum_bitcast_fusion.1.value), custom_call_target="tpu_custom_call" | custom-call | tf_op jit(solution)/shard_map/pallas_call | solution.py:652
  553.4 0.6 multiply_reduce_fusion.2
  555.9 1.5 broadcast_multiply_fusion
  557.5 0.7 multiply_subtract_fusion.2
  558.1 1.7 multiply_add_fusion.3
  559.9 1.6 fusion.37
  562.4 3.2 multiply_subtract_fusion.1
  565.7 4.0 multiply_add_fusion.1
  569.7 4.7 multiply_add_fusion.2
  574.4 4.6 multiply_subtract_fusion
  (85 shorter events, 4.5 us)
Async XLA Ops:
  0.6 559.2 %copy-start = (f32[25,128,128]{2,1,0:T(8,128)S(1)}, f32[25,128,128]{2,1,0:T(8,128)}, u32[]{:S(2)}) copy-start(f32[25,128,128]{2,1,0:T(8,128)} %param.30) | copy-start | bytes 4915204
  0.7 16.8 %copy-start.9 = (f32[25,128,128]{2,1,0:T(8,128)S(1)}, f32[25,128,128]{2,1,0:T(8,128)}, u32[]{:S(2)}) copy-start(f32[25,128,128]{2,1,0:T(8,128)} %param.26) | copy-start | bytes 4915204
  21.4 163.0 %copy-start.19 = (f32[128,640]{1,0:T(8,128)S(1)}, f32[128,640]{1,0:T(8,128)}, u32[]{:S(2)}) copy-start(f32[128,640]{1,0:T(8,128)} %copy.65) | copy-start | bytes 983044
  211.3 0.9 copy-start.4
  212.3 31.8 %copy-start.13 = (bf16[1024,640]{1,0:T(8,128)(2,1)S(1)}, bf16[1024,640]{1,0:T(8,128)(2,1)}, u32[]{:S(2)}) copy-start(bf16[1024,640]{1,0:T(8,128)(2,1)} %convert_element_type.103.table) | copy-start | bytes 3932164
  244.1 7.1 %copy-start.1 = (bf16[4,4,2,128,640]{4,3,2,1,0:T(8,128)(2,1)}, bf16[4,4,2,128,640]{4,3,2,1,0:T(8,128)(2,1)S(1)}, u32[]{:S(2)}) copy-start(bf16[4,4,2,128,640]{4,3,2,1,0:T(8,128)(2,1)S(1)} %shard_map.284) | copy-start | bytes 15728644
  251.1 5.7 copy-start.5
  278.0 16.1 %slice-start = ((s8[5242880]{0:T(1024)(128)(4,1)}), s8[1048576]{0:T(1024)(128)(4,1)S(1)}, s32[]{:S(2)}) async-start(s8[5242880]{0:T(1024)(128)(4,1)} %bitcast.103), calls=%async_computation | async-start | bytes 2097152
  281.9 12.2 %slice-start.1 = ((s8[5242880]{0:T(1024)(128)(4,1)}), s8[4194304]{0:T(1024)(128)(4,1)S(1)}, s32[]{:S(2)}) async-start(s8[5242880]{0:T(1024)(128)(4,1)} %bitcast.103), calls=%async_computation.1 | async-start | bytes 8388608
  294.1 10.4 %copy-start.8 = (bf16[32,4,32,1024]{3,2,1,0:T(8,128)(2,1)S(1)}, bf16[32,4,32,1024]{3,2,1,0:T(8,128)(2,1)}, u32[]{:S(2)}) copy-start(bf16[32,4,32,1024]{3,2,1,0:T(8,128)(2,1)} %fusion.1) | copy-start | bytes 25165828
  340.1 0.7 copy-start.2
  383.5 1.0 copy-start.3
  384.5 26.0 %copy-start.23 = (f32[1024,640]{1,0:T(8,128)S(1)}, f32[1024,640]{1,0:T(8,128)}, u32[]{:S(2)}) copy-start(f32[1024,640]{1,0:T(8,128)} %fusion.36) | copy-start | bytes 7864324
  531.9 3.2 copy-start.12
  535.0 22.4 %copy-start.20 = (f32[14,640]{1,0:T(8,128)S(1)}, f32[14,640]{1,0:T(8,128)}, u32[]{:S(2)}) copy-start(f32[14,640]{1,0:T(8,128)} %refs_4_.3) | copy-start | bytes 107524
  535.0 22.4 %copy-start.21 = (f32[14,640]{1,0:T(8,128)S(1)}, f32[14,640]{1,0:T(8,128)}, u32[]{:S(2)}) copy-start(f32[14,640]{1,0:T(8,128)} %param.36) | copy-start | bytes 107524
  535.0 22.4 %copy-start.22 = (f32[14,640]{1,0:T(8,128)S(1)}, f32[14,640]{1,0:T(8,128)}, u32[]{:S(2)}) copy-start(f32[14,640]{1,0:T(8,128)} %param.37) | copy-start | bytes 107524
  559.9 5.8 copy-start.11
  559.9 2.0 copy-start.10
  559.9 2.5 copy-start.16
  562.4 3.3 copy-start.17
  562.4 7.3 %copy-start.18 = (f32[25,128,128]{2,1,0:T(8,128)S(1)}, f32[25,128,128]{2,1,0:T(8,128)}, u32[]{:S(2)}) copy-start(f32[25,128,128]{2,1,0:T(8,128)} %param.28) | copy-start | bytes 4915204
  565.6 8.7 %copy-start.14 = (f32[1024,640]{1,0:T(8,128)S(1)}, f32[1024,640]{1,0:T(8,128)}, u32[]{:S(2)}) copy-start(f32[1024,640]{1,0:T(8,128)} %param.33) | copy-start | bytes 7864324
  565.6 8.7 %copy-start.15 = (f32[1024,640]{1,0:T(8,128)S(1)}, f32[1024,640]{1,0:T(8,128)}, u32[]{:S(2)}) copy-start(f32[1024,640]{1,0:T(8,128)} %param.34) | copy-start | bytes 7864324
  569.7 4.7 copy-start.6
  569.7 4.7 copy-start.7

commit v5 on v4

--- a/solution.py
+++ b/solution.py
@@ -190,7 +190,7 @@
     yield 0
 
 
-def gather_flows(colours, value, out, copies):
+def gather_flows(colours, value, out, copies, hold=0):
     z, x, c = (lax.axis_index(a) for a in ("tok_0", "tok_1", CORE))
     crossing = []
 
@@ -224,6 +224,8 @@
             if stage == 0:
                 yield next(steps)
                 arrived(ref)
+            elif stage == 1 and hold:
+                yield hold
             yield from steps
 
     return [run(*colour, ref) for colour, (_, ref) in zip(colours, own)], crossing
@@ -357,24 +359,24 @@
 def scatter_flows(colours, ending, value, out, mine, total, other, slots, copies):
     c = lax.axis_index(CORE)
     pending = {}
-    for turn in range(4):
-        for k, (order, rows) in enumerate(colours):
-            part = places(order, 0, rows, "y" in order)
-            i = around(RING[order[0]])[(3, 1, 2, 0)[turn]]
-            (first, second), span = part(i, None, False)
-            pending[k, turn] = (
-                copies.push(
-                    view(value, (first, second, 1 - c), span),
-                    view(other, (first, second), span),
-                    CORE,
-                    1 - c,
-                ),
-                copies.move(
-                    view(value, (first, second, c), span), view(total, (first, second), span)
-                ),
-                view(total, (first, second), span),
-                view(other, (first, second), span),
-            )
+
+    def issue(k, turn):
+        order, rows = colours[k]
+        part = places(order, 0, rows, "y" in order)
+        i = around(RING[order[0]])[(3, 1, 2, 0)[turn]]
+        (first, second), span = part(i, None, False)
+        ours = view(total, (first, second), span)
+        theirs = view(other, (first, second), span)
+        pending[k, turn] = (
+            copies.push(view(value, (first, second, 1 - c), span), theirs, CORE, 1 - c),
+            copies.move(view(value, (first, second, c), span), ours),
+            ours,
+            theirs,
+        )
+
+    for turn in range(2):
+        for k in range(len(colours)):
+            issue(k, turn)
 
     def run(k, order, rows):
         at = 6 * sum(len(o) for o, _ in colours[:k])
@@ -386,6 +388,8 @@
             across, inside, ours, theirs = pending[k, turn]
             inside.wait()
             across.wait_recv()
+            if turn < 2:
+                issue(k, turn + 2)
             add_to(ours, theirs)
 
         for stage, name in enumerate(order):
@@ -415,14 +419,6 @@
                 here, slots[at : at + 6], axis, copies, nothing if stage else ready, done
             )
             at += 6
-        if ending == "gather":
-            start, size = rows
-            piece = size // 4
-
-            def held(i, half):
-                return view(out, (), rows_of(start + i * piece, piece, half))
-
-            yield from ring_gather(held, "sub", copies, lambda ref: None)
 
     return [run(k, order, rows) for k, (order, rows) in enumerate(colours)]
 
@@ -447,46 +443,158 @@
         copy.wait_recv()
 
 
-def scatter_kernel(colours, ending, value, *refs):
-    if ending == "gather":
-        table, out, table_out, total, other, table_in, *refs = refs
-    else:
-        out, total, other, *refs = refs
+def scatter_kernel(colours, ending, value, out, total, other, *refs):
+    count = sum(len(order) for order, _ in colours) * 6
+    slots, (mine, *refs) = refs[:count], refs[count:]
+    copies = Copies(*refs)
+    greet((CORE, "tok_0", "tok_1", "sub"))
+    in_turn(scatter_flows(colours, ending, value, out, mine, total, other, slots, copies))
+    in_turn([to_sub(ending, mine, out, copies)])
+    copies.finish()
+
+
+def swap_flow(value, mine, copies):
+    me = lax.axis_index("sub")
+    piece = value.shape[0] // 4
+
+    def part_of(ref, k):
+        return ref.at[pl.ds(pl.multiple_of(k * piece, 16), piece)]
+
+    local = copies.move(part_of(value, me), part_of(mine, me))
+    arrivals = [
+        copies.push(part_of(value, peer), part_of(mine, me), "sub", peer)
+        for peer in (lax.rem(me + k, 4) for k in (1, 3, 2))
+    ]
+    yield 1
+    local.wait()
+    for copy in arrivals:
+        copy.wait_recv()
+
+
+def close_kernel(colours, row_ways, grads, table, rows, ids, part, *refs):
+    own, table_out, sums, total, other, table_in, mine, joined, gathered, *refs = refs
+    boards, refs = refs[:4], refs[4:]
     count = sum(len(order) for order, _ in colours) * 6
     slots, refs = refs[:count], refs[count:]
-    mine = None
-    if ending == "gather":
-        table_slots, refs = refs[:6], refs[6:]
-    else:
-        mine, *refs = refs
+    table_slots, refs = refs[:6], refs[6:]
     copies = Copies(*refs)
     greet((CORE, "tok_0", "tok_1", "sub"))
-    flows = scatter_flows(colours, ending, value, out, mine, total, other, slots, copies)
-    if ending == "gather":
-        loaded = copies.move(table, table_in)
-        piece = table.shape[0] // 4
-
-        def table_flow():
-            me = lax.axis_index("sub")
-            loaded.wait()
-
-            def here(i, half):
-                return view(table_in, (), rows_of(i * piece, piece, half))
-
-            def there(i, half):
-                return view(table_out, (), rows_of(i * piece, piece, half))
-
-            def done(half, one, two):
-                there(me, half)[...] = here(me, half)[...] + one[...] + two[...]
-
-            yield from ring_scatter(here, table_slots, "sub", copies, lambda turn: None, done)
-            yield from ring_gather(there, "sub", copies, lambda ref: None)
-
-        flows = [table_flow(), *flows]
-    in_turn(flows)
-    if ending != "gather":
-        in_turn([to_sub(ending, mine, out, copies)])
+    loaded = copies.move(table, table_in)
+    in_turn([swap_flow(rows, mine, copies)])
+    piece = rows.shape[0] // 4
+    summed = mine[pl.ds(0, piece)].astype(jnp.float32)
+    for k in range(1, 4):
+        summed = summed + mine[pl.ds(k * piece, piece)].astype(jnp.float32)
+    joined[...] = summed.astype(joined.dtype)
+    row_flows, crossing = gather_flows(row_ways, joined, gathered, copies)
+    shard_rows, lanes = table.shape
+    me_y = lax.axis_index("sub")
+    high_rows = shard_rows // 4
+
+    def here(i, half):
+        return view(table_in, (), rows_of(i * high_rows, high_rows, half))
+
+    def there(i, half):
+        return view(table_out, (), rows_of(i * high_rows, high_rows, half))
+
+    def table_flow():
+        yield row_flows
+        for copy in crossing:
+            copy.wait_recv()
+        loaded.wait()
+        first_row = lax.axis_index(("tok_0", "tok_1", CORE)) * shard_rows
+        numbers = lax.broadcasted_iota(jnp.int32, (shard_rows, HALF), 0) + first_row
+
+        def put(z, carry):
+            hits = [
+                (numbers == ids[z, x]).astype(jnp.float32).astype(low_type) for x in range(4)
+            ]
+            found = gathered[z].reshape(4 * HALF, lanes)
+            table_in[...] = table_in[...] + matmul(jnp.concatenate(hits, 1), found)
+            return carry
+
+        lax.fori_loop(0, 4, put, 0)
+
+        def done(half, one, two):
+            there(me_y, half)[...] = here(me_y, half)[...] + one[...] + two[...]
+
+        yield from ring_scatter(here, table_slots, "sub", copies, lambda turn: None, done)
+
+    def block_flow(flow):
+        yield 1 << 20
+        yield from flow
+
+    def own_part(rows):
+        start, size = rows
+
+        def held(i, half):
+            return view(own, (), rows_of(start + i * (size // 4), size // 4, half))
+
+        return held
+
+    def norm_flow():
+        square = jnp.zeros((1, BLK), jnp.float32)
+        for ref in [there(me_y, None)] + [own_part(rows)(me_y, None) for _, rows in colours]:
+            value = ref[...]
+            value = jnp.sum(value * value, 0, keepdims=True)
+            for k in range(value.shape[1] // BLK):
+                square = square + value[:, k * BLK : (k + 1) * BLK]
+        line = lax.broadcasted_iota(jnp.int32, part.shape, 0)
+        sums[...] = part[...] + jnp.where(line == part.shape[0] - 2, square, 0.0)
+        for axis, board in zip((CORE, "tok_1", "tok_0", "sub"), boards):
+            size = lax.axis_size(axis)
+            me = lax.axis_index(axis)
+            board[me] = sums[...]
+            arrivals = [
+                copies.push(board.at[me], board.at[me], axis, lax.rem(me + k, size))
+                for k in range(1, size)
+            ]
+            yield 1
+            for copy in arrivals:
+                copy.wait_recv()
+            sums[...] = added([board[k] for k in range(size)])
+
+    def whole():
+        flows = scatter_flows(colours, "gather", grads, own, None, total, other, slots, copies)
+        yield [table_flow(), *[block_flow(flow) for flow in flows]]
+        ends = [there] + [own_part(rows) for _, rows in colours]
+        yield [norm_flow()] + [ring_gather(e, "sub", copies, lambda ref: None) for e in ends]
+
+    in_turn([whole()])
     copies.finish()
+
+
+def close_exchange(grads, table, rows, ids, part, number, colours, row_ways):
+    slots = scatter_slots(colours, BLK, low_type)
+    height, lanes = table.shape
+    piece = rows.shape[0] // 4
+    stages = len(slots) // 6
+    vmem = pl.BlockSpec(memory_space=pltpu.VMEM)
+    hbm = pl.BlockSpec(memory_space=pltpu.HBM)
+    return pl.pallas_call(
+        functools.partial(close_kernel, colours, row_ways),
+        out_shape=[
+            jax.ShapeDtypeStruct(grads.shape[3:], jnp.float32),
+            jax.ShapeDtypeStruct(table.shape, jnp.float32),
+            jax.ShapeDtypeStruct(part.shape, jnp.float32),
+        ],
+        in_specs=[hbm, hbm, vmem, vmem, vmem],
+        out_specs=[vmem] * 3,
+        scratch_shapes=[pltpu.VMEM((4, 4, *grads.shape[3:]), low_type)] * 2
+        + [
+            pltpu.VMEM(table.shape, jnp.float32),
+            pltpu.VMEM(rows.shape, low_type),
+            pltpu.VMEM((piece, lanes), low_type),
+            pltpu.VMEM((4, 4, 2, piece, lanes), low_type),
+        ]
+        + [pltpu.VMEM((n, *part.shape), jnp.float32) for n in (2, 4, 4, 4)]
+        + slots
+        + [pltpu.VMEM((height // 8, lanes), jnp.float32)] * 6
+        + semaphores(6 * stages + 8 * len(colours) + 7 * 4 + 3 + 6 + 12 + 10 + 8, 20),
+        compiler_params=pltpu.CompilerParams(
+            collective_id=number, has_side_effects=True, vmem_limit_bytes=61 * MIB
+        ),
+    )(grads, table, rows, ids, part)
 
 
 def scatter_slots(colours, lanes, kind):
@@ -503,35 +611,24 @@
     return slots
 
 
-def scatter_tok(value, number, colours, ending, limit, table=None):
+def scatter_tok(value, number, colours, ending, limit):
     rows, lanes = value.shape[3:]
     slots = scatter_slots(colours, lanes, value.dtype)
     stages = len(slots) // 6
-    shape = {"gather": (rows, lanes), "spread": (4, rows, lanes), "swap": (4, rows // 4, lanes)}
-    kind = jnp.float32 if ending == "gather" else value.dtype
-    outs = [jax.ShapeDtypeStruct(shape[ending], kind)]
-    scratch = [pltpu.VMEM((4, 4, rows, lanes), value.dtype)] * 2
-    given = [value]
-    if table is None:
-        scratch += slots + [pltpu.VMEM((rows, lanes), value.dtype)]
-    else:
-        height, across = table.shape
-        given.append(table)
-        outs.append(jax.ShapeDtypeStruct(table.shape, table.dtype))
-        scratch += [pltpu.VMEM(table.shape, table.dtype)] + slots
-        scratch += [pltpu.VMEM((height // 8, across), table.dtype)] * 6
-    result = pl.pallas_call(
+    shape = {"spread": (4, rows, lanes), "swap": (4, rows // 4, lanes)}
+    return pl.pallas_call(
         functools.partial(scatter_kernel, colours, ending),
-        out_shape=outs,
-        in_specs=[pl.BlockSpec(memory_space=pltpu.HBM)] * len(given),
-        out_specs=[pl.BlockSpec(memory_space=pltpu.VMEM)] * len(outs),
-        scratch_shapes=scratch
-        + semaphores(6 * stages + 8 * len(colours) + 14, 4 * len(colours) + 2),
+        out_shape=jax.ShapeDtypeStruct(shape[ending], value.dtype),
+        in_specs=[pl.BlockSpec(memory_space=pltpu.HBM)],
+        out_specs=pl.BlockSpec(memory_space=pltpu.VMEM),
+        scratch_shapes=[pltpu.VMEM((4, 4, rows, lanes), value.dtype)] * 2
+        + slots
+        + [pltpu.VMEM((rows, lanes), value.dtype)]
+        + semaphores(6 * stages + 8 * len(colours) + 4, 4 * len(colours) + 2),
         compiler_params=pltpu.CompilerParams(
             collective_id=number, has_side_effects=True, vmem_limit_bytes=limit
         ),
-    )(*given)
-    return result if table is not None else result[0]
+    )(value)
 
 
 def open_kernel(weight_ways, row_ways, mine, table, blocks, ids, rows, slots, *refs):
@@ -540,12 +637,11 @@
     inbox, refs = refs[:count], refs[count:]
     copies = Copies(*refs)
     greet((CORE, "tok_0", "tok_1", "sub"))
-    flows, crossing = gather_flows(weight_ways, blocks, slots, copies)
     axes = ("tok_0", "tok_1", CORE)
     shard_rows = table.shape[0]
     slot_rows = picked.shape[3]
 
-    def row_flow():
+    def id_flow():
         spot = tuple(lax.axis_index(axis) for axis in axes)
         copies.move(mine, ids.at[spot]).wait()
         for depth in reversed(range(3)):
@@ -558,6 +654,12 @@
             yield 1
             for copy in arrivals:
                 copy.wait_recv()
+
+    in_turn([id_flow()])
+    flows, crossing = gather_flows(weight_ways, blocks, slots, copies, 1 << 20)
+
+    def row_flow():
+        yield 1
         first_row = lax.axis_index(axes) * shard_rows
         numbers = lax.broadcasted_iota(jnp.int32, (shard_rows, HALF), 0) + first_row
 
@@ -1123,8 +1225,6 @@
     weight = (all_targets >= 0).astype(jnp.float32)
     token_count = jnp.sum(heads_up[:, 3 * piece]).astype(jnp.float32)
     first_row = place * shard_rows
-    local = (heads_up[:, : 2 * piece] - first_row).reshape(-1)
-    picks = (local[:, None] == jnp.arange(shard_rows, dtype=jnp.int32)).astype(low_type)
     rows = rows.reshape(groups, 2, piece, D).transpose(1, 0, 2, 3).reshape(2, HALF, D)
     used = slot_block < NBLK
     ranks = jnp.cumsum(1 - used.astype(jnp.int32)) - 1
@@ -1181,26 +1281,29 @@
         order, d_final.reshape(HALF, D), *common, kept, mats
     )
     vec_grad = vec_grad[: vec.shape[0]]
-    all_rows = gather_tok(d_rows, 7, both_ways(2 * piece), "sum").reshape(-1, D)
-    table_grad = table_grad + jnp.einsum(
-        "rv,rd->vd", picks, all_rows, preferred_element_type=wide_type
-    )
-    own, table_grad = scatter_tok(
-        slot_grads.reshape(4, 4, 2, -1, BLK), 8, GRAD_WAYS, "gather", 60 * MIB, table_grad
-    )
-    own = own.reshape(master.shape)
-    square = jnp.sum(own * own) + jnp.sum(table_grad * table_grad)
-    small = jnp.concatenate(
+    part = jnp.concatenate(
         [
             vec_grad.reshape(-1),
-            jnp.broadcast_to(square / groups, (BLK,)),
+            jnp.zeros((BLK,), wide_type),
             jnp.broadcast_to(loss_part / shards, (BLK,)),
         ]
     )
-    small = sum_all(small.reshape(-1, BLK), 9, (*TOK[::-1], "sub")).reshape(-1)
+    own, table_grad, small = close_exchange(
+        slot_grads.reshape(4, 4, 2, -1, BLK),
+        table_grad,
+        d_rows,
+        heads_up[:, : 2 * piece].reshape(4, 4, 1, HALF),
+        part.reshape(-1, BLK),
+        8,
+        GRAD_WAYS,
+        both_ways(2 * piece),
+    )
+    own = own.reshape(master.shape)
+    small = small.reshape(-1)
     vec_grad = small[: vec.size].reshape(vec.shape)
     loss_sum = small[vec.size + BLK]
-    grad_norm = jnp.sqrt(small[vec.size] + jnp.sum(vec_grad * vec_grad))
+    square = jnp.sum(small[vec.size : vec.size + BLK])
+    grad_norm = jnp.sqrt(square + jnp.sum(vec_grad * vec_grad))
     scale = jnp.minimum(1.0, clip_limit / grad_norm)
     grad = own * scale
     new_left = beta_stat * left_stat + (1.0 - beta_stat) * jnp.einsum(

time: 585 us -> 591 us (1.010)
  Pallas kernels: 455 us -> 469 us
    pallas_call x0 -> x1, Pallas kernels: none -> 177 us  [close_exchange(): pl.pallas_call(functools.partial(close_kernel, colours, row_ways), out_sh...]
    pallas_call x2 -> x1, Pallas kernels: 145 us -> 30.5 us  [scatter_tok(): pl.pallas_call(functools.partial(scatter_kernel, colours, ending), out_sh...]
    pallas_call x2 -> x1, Pallas kernels: 57.7 us -> 31 us  [gather_tok(): pl.pallas_call(functools.partial(gather_kernel, colours, swap, axes), out...]
    pallas_call x2 -> x1, Pallas kernels: 28.8 us -> 13.9 us  [sum_all(): pl.pallas_call(functools.partial(sum_kernel, axes, combine), out_shape=ja...]
    pallas_call x1, Pallas kernels: 157 us -> 151 us  [open_exchange(): pl.pallas_call(functools.partial(open_kernel, weight_ways, row_ways), out...]
where the time goes in v5:
time: 591 us; the launch traced here: 587 us
  Pallas kernels  469 us (79%)
  other arithmetic  55.7 us (9%)
  matrix products  38 us (6%)
  local copies, waits for them, and re-layouts  18.6 us (3%)
  between operations  6.33 us (1%)
    pallas_call x1, Pallas kernels, close_exchange(): pl.pallas_call(functools.partial(close_kernel, colours, row_ways), out_sh...  177 us
    pallas_call x1, Pallas kernels, open_exchange(): pl.pallas_call(functools.partial(open_kernel, weight_ways, row_ways), out...  151 us
    pallas_call x1, Pallas kernels, run_backward(): pl.pallas_call(backward_kernel, out_shape=[jax.ShapeDtypeStruct((order.sh...  41.9 us
    pallas_call x1, Pallas kernels, gather_tok(): pl.pallas_call(functools.partial(gather_kernel, colours, swap, axes), out...  31 us
    pallas_call x1, Pallas kernels, scatter_tok(): pl.pallas_call(functools.partial(scatter_kernel, colours, ending), out_sh...  30.5 us
    pallas_call x1, Pallas kernels, run_forward(): pl.pallas_call(forward_kernel, out_shape=small + mats, in_specs=in_hbm(1)...  23.7 us
    pallas_call x1, Pallas kernels, sum_all(): pl.pallas_call(functools.partial(sum_kernel, axes, combine), out_shape=ja...  13.9 us
    convert_element_type x1, other arithmetic, on_device(): back = back.astype(low_type).reshape(-1, shard_rows)  12.2 us

profile of v5, /device:TPU:0, one launch (start us, length us, event | category | flops | bytes accessed | tf_op | source)
XLA Modules:
  0.0 587.5 jit_solution(2946428749889330857)
XLA Ops:
  0.7 0.8 fusion.22
  1.5 0.7 fusion.24
  2.3 0.7 fusion.26
  3.0 0.8 fusion.30
  3.9 0.7 convert_element_type.111.refs_6_
  4.6 0.7 fusion.20
  5.9 0.7 compare_select_fusion
  6.6 1.0 select_reduce_fusion.1.refs_1_.refs_0_
  7.6 0.6 copy.79
  8.2 0.7 copy.62
  9.1 0.7 sub.110
  9.8 0.7 select_reduce_fusion.2
  10.5 0.6 broadcast_in_dim.41
  11.1 0.7 multiply_add_fusion.5
  11.9 0.6 add_bitcast_fusion.1.mine
  12.5 0.7 broadcast_in_dim.44
  13.2 0.7 add_convert_fusion.refs_8_
  13.9 0.6 multiply_sine_fusion
  14.6 1.0 copy.64
  15.6 1.9 copy.65
  17.4 1.0 convert_element_type.103
  18.5 2.9 convert_element_type.102.table
  21.4 151.4 %shard_map.282 = (s32[4,4,2,1,128]{4,3,2,1,0:T(1,128)}, bf16[4,64,640]{2,1,0:T(8,128)(2,1)}, bf16[4,4,2,3200,128]{4,3,2,1,0:T(8,128)(2,1)}) custom-call(s32[1,128]{1,0:T(1,128)} %add_bitcast_fusion.1.mine, bf16[1024,640]{1,0:T(8,128)(2,1)} %convert_element_type.102.table, bf16[3200,128]{1,0:T(8,128)(2,1)} %bitcast.113), custom_call_target="tpu_custom_call" | custom-call | tf_op jit(solution)/shard_map/pallas_call | solution.py:687
  172.8 1.4 slice_reduce_fusion
  174.9 1.4 reshape.471.ids
  176.3 0.8 slice_subtract_fusion.1
  177.1 1.0 copy_bitcast_fusion
  178.2 0.9 fusion.8
  179.2 2.3 fusion.4
  181.4 23.7 %shard_map.283 = (bf16[128,640]{1,0:T(8,128)(2,1)}, f32[128,640]{1,0:T(8,128)}, f32[128,640]{1,0:T(8,128)}, f32[128,640]{1,0:T(8,128)}, f32[128,640]{1,0:T(8,128...) custom-call(bf16[800,128,128]{2,1,0:T(8,128)(2,1)} %bitcast.109, ...), custom_call_target="tpu_custom_call" | custom-call | tf_op jit(solution)/shard_map/pallas_call | solution.py:1030
  205.1 0.9 copy-done.3
  206.0 31.0 %shard_map.284 = bf16[4,4,2,128,640]{4,3,2,1,0:T(8,128)(2,1)S(1)} custom-call(bf16[128,640]{1,0:T(8,128)(2,1)S(1)} %copy-done.3), custom_call_target="tpu_custom_call" | custom-call | tf_op jit(solution)/shard_map/pallas_call | solution.py:288
  237.0 7.1 %fusion.31 = (f32[32,4,32]{2,1,0:T(4,128)S(1)}, f32[32,4,32,1024]{3,2,1,0:T(8,128)S(1)}) fusion(bf16[32,4,32,640]{3,2,1,0:T(8,128)(2,1)S(1)} %bitcast.100, bf16[1024,640]{1,0:T(8,128)(2,1)S(1)} %copy-done.10), kind=kOutput, calls=%fused_computation.99 | convolution fusion | flops 5372899328 | bytes 23347200 | tf_op jit(solution)/shard_map/td,vd->tv/dot_general | solution.py:1247
  244.1 0.7 select_reduce_fusion
  244.8 3.1 exponential_reduce_fusion
  247.9 0.9 exponential_bitcast_fusion.1
  248.8 1.0 copy-done.4
  249.8 1.8 fusion.3
  251.9 13.9 %shard_map.285 = f32[96,128]{1,0:T(8,128)S(1)} custom-call(f32[96,128]{1,0:T(8,128)S(1)} %reshape.464.value), custom_call_target="tpu_custom_call" | custom-call | tf_op jit(solution)/shard_map/pallas_call | solution.py:754
  266.0 0.7 fusion.18
  267.4 4.7 exponential_bitcast_fusion
  272.1 3.9 broadcast_in_dim.84
  276.0 12.2 %fusion.1 = bf16[32,4,32,1024]{3,2,1,0:T(8,128)(2,1)} fusion(f32[32,3,32,1024]{3,2,1,0:T(8,128)S(1)} %broadcast_in_dim.84, f32[32,1,32,1024]{3,2,1,0:T(8,128)} %fusion.4, f32[32,4,32,1024]{3,2,1,0:T(8,128)} %copy-done.4, f32[32,32]{1,0:T(8,128)S(1)} %broadcast_select_fusion, f32[32,4,32]{2,1,0:T(4,128)S(1)} %copy.68), kind=kLoop, calls=%fused_computation.2 | loop fusion | flops 20971520 | bytes 41963520 | tf_op jit(solution)/shard_map/convert_element_type | solution.py:1276
  288.2 10.4 %fusion.32.table = f32[1024,640]{1,0:T(8,128)} fusion(bf16[4096,1024]{1,0:T(8,128)(2,1)} %bitcast.111, bf16[4096,640]{1,0:T(8,128)(2,1)S(1)} %bitcast.103), kind=kOutput, calls=%fused_computation.100 | convolution fusion | flops 5368709120 | bytes 16252928 | tf_op jit(solution)/shard_map/tv,td->vd/dot_general | solution.py:1279
  298.6 7.0 %convolution_convert_fusion = bf16[4096,640]{1,0:T(8,128)(2,1)S(1)} fusion(bf16[4096,1024]{1,0:T(8,128)(2,1)S(1)} %bitcast.112, bf16[1024,640]{1,0:T(8,128)(2,1)S(1)} %copy-done.10), kind=kOutput, calls=%fused_computation.7 | convolution fusion | flops 5371330560 | bytes 14942208 | tf_op jit(solution)/shard_map/dot_general | solution.py:819
  305.5 30.5 %shard_map.286 = bf16[4,32,640]{2,1,0:T(8,128)(2,1)S(1)} custom-call(bf16[4,4,2,128,640]{4,3,2,1,0:T(8,128)(2,1)S(1)} %bitcast.104), custom_call_target="tpu_custom_call" | custom-call | tf_op jit(solution)/shard_map/pallas_call | solution.py:619
  336.0 0.7 copy-done.2
  336.7 41.9 %shard_map.287 = (bf16[800,128,128]{2,1,0:T(8,128)(2,1)}, f32[16,640]{1,0:T(8,128)}, bf16[256,640]{1,0:T(8,128)(2,1)}) custom-call(s32[800]{0:T(1024)} %select_reduce_fusion.1.refs_1_.refs_0_, bf16[128,640]{1,0:T(8,128)(2,1)} %bitcast.105, f32[128,640]{1,0:T(8,128)} %get-tuple-element.102.refs_2_, f32[128,640]{1,0:T(8,128)} %get-tuple-element.101.refs_3_, ...), custom_call_target="tpu_custom_call" | custom-call | tf_op jit(solution)/shard_map/pallas_call | solution.py:1146
  378.6 0.8 reshape.472
  379.4 0.6 maximum_bitcast_fusion.1.part
  380.0 176.6 %shard_map.288 = (f32[3200,128]{1,0:T(8,128)}, f32[1024,640]{1,0:T(8,128)}, f32[72,128]{1,0:T(8,128)}) custom-call(bf16[4,4,2,3200,128]{4,3,2,1,0:T(8,128)(2,1)} %bitcast.110, f32[1024,640]{1,0:T(8,128)} %fusion.32.table, bf16[256,640]{1,0:T(8,128)(2,1)} %get-tuple-element.80.rows, s32[4,4,1,128]{3,2,1,0:T(1,128)} %reshape.471.ids, ...), custom_call_target="tpu_custom_call" | custom-call | tf_op jit(solution)/shard_map/pallas_call | solution.py:574
  556.7 1.4 multiply_reduce_fusion
  558.1 1.3 slice_reduce_fusion.2
  560.8 1.2 slice.119
  561.9 1.5 broadcast_multiply_fusion
  563.6 0.7 multiply_subtract_fusion.2
  564.2 1.7 multiply_add_fusion.3
  566.0 1.6 fusion.33
  567.6 0.3 copy-done.8
  568.0 0.5 copy-done.14
  568.5 3.2 multiply_subtract_fusion.1
  571.7 4.0 multiply_add_fusion.1
  575.7 4.7 multiply_add_fusion.2
  580.5 4.6 multiply_subtract_fusion
  (78 shorter events, 1.9 us)
Async XLA Ops:
  0.6 565.3 %copy-start = (f32[25,128,128]{2,1,0:T(8,128)S(1)}, f32[25,128,128]{2,1,0:T(8,128)}, u32[]{:S(2)}) copy-start(f32[25,128,128]{2,1,0:T(8,128)} %param.30) | copy-start | bytes 4915204
  0.7 16.8 %copy-start.7 = (f32[25,128,128]{2,1,0:T(8,128)S(1)}, f32[25,128,128]{2,1,0:T(8,128)}, u32[]{:S(2)}) copy-start(f32[25,128,128]{2,1,0:T(8,128)} %param.26) | copy-start | bytes 4915204
  21.4 156.8 %copy-start.17 = (f32[128,640]{1,0:T(8,128)S(1)}, f32[128,640]{1,0:T(8,128)}, u32[]{:S(2)}) copy-start(f32[128,640]{1,0:T(8,128)} %copy.65) | copy-start | bytes 983044
  205.1 0.9 copy-start.3
  206.0 31.0 %copy-start.10 = (bf16[1024,640]{1,0:T(8,128)(2,1)S(1)}, bf16[1024,640]{1,0:T(8,128)(2,1)}, u32[]{:S(2)}) copy-start(bf16[1024,640]{1,0:T(8,128)(2,1)} %convert_element_type.102.table) | copy-start | bytes 3932164
  237.0 7.1 %copy-start.1 = (bf16[4,4,2,128,640]{4,3,2,1,0:T(8,128)(2,1)}, bf16[4,4,2,128,640]{4,3,2,1,0:T(8,128)(2,1)S(1)}, u32[]{:S(2)}) copy-start(bf16[4,4,2,128,640]{4,3,2,1,0:T(8,128)(2,1)S(1)} %shard_map.284) | copy-start | bytes 15728644
  244.1 5.7 copy-start.4
  249.8 16.2 %copy-start.19 = (s32[4,4,2,1,128]{4,3,2,1,0:T(1,128)S(1)}, s32[4,4,2,1,128]{4,3,2,1,0:T(1,128)}, u32[]{:S(2)}) copy-start(s32[4,4,2,1,128]{4,3,2,1,0:T(1,128)} %get-tuple-element.52) | copy-start | bytes 49156
  272.1 16.1 %slice-start = ((s8[5242880]{0:T(1024)(128)(4,1)}), s8[1048576]{0:T(1024)(128)(4,1)S(1)}, s32[]{:S(2)}) async-start(s8[5242880]{0:T(1024)(128)(4,1)} %bitcast.101), calls=%async_computation | async-start | bytes 2097152
  276.0 12.2 %slice-start.1 = ((s8[5242880]{0:T(1024)(128)(4,1)}), s8[4194304]{0:T(1024)(128)(4,1)S(1)}, s32[]{:S(2)}) async-start(s8[5242880]{0:T(1024)(128)(4,1)} %bitcast.101), calls=%async_computation.1 | async-start | bytes 8388608
  288.2 10.4 %copy-start.6 = (bf16[32,4,32,1024]{3,2,1,0:T(8,128)(2,1)S(1)}, bf16[32,4,32,1024]{3,2,1,0:T(8,128)(2,1)}, u32[]{:S(2)}) copy-start(bf16[32,4,32,1024]{3,2,1,0:T(8,128)(2,1)} %fusion.1) | copy-start | bytes 25165828
  336.0 0.7 copy-start.2
  556.6 6.9 %copy-start.20 = (f32[72,128]{1,0:T(8,128)S(1)}, f32[72,128]{1,0:T(8,128)}, u32[]{:S(2)}) copy-start(f32[72,128]{1,0:T(8,128)} %get-tuple-element.82) | copy-start | bytes 110596
  556.6 6.9 %copy-start.18 = (f32[14,640]{1,0:T(8,128)S(1)}, f32[14,640]{1,0:T(8,128)}, u32[]{:S(2)}) copy-start(f32[14,640]{1,0:T(8,128)} %refs_4_.3) | copy-start | bytes 107524
  556.7 6.9 %copy-start.21 = (f32[14,640]{1,0:T(8,128)S(1)}, f32[14,640]{1,0:T(8,128)}, u32[]{:S(2)}) copy-start(f32[14,640]{1,0:T(8,128)} %param.36) | copy-start | bytes 107524
  556.7 6.9 %copy-start.22 = (f32[14,640]{1,0:T(8,128)S(1)}, f32[14,640]{1,0:T(8,128)}, u32[]{:S(2)}) copy-start(f32[14,640]{1,0:T(8,128)} %param.37) | copy-start | bytes 107524
  565.9 5.8 copy-start.9
  566.0 2.0 copy-start.8
  566.0 2.5 copy-start.14
  568.5 3.3 copy-start.15
  568.5 7.3 %copy-start.16 = (f32[25,128,128]{2,1,0:T(8,128)S(1)}, f32[25,128,128]{2,1,0:T(8,128)}, u32[]{:S(2)}) copy-start(f32[25,128,128]{2,1,0:T(8,128)} %param.28) | copy-start | bytes 4915204
  571.7 8.7 %copy-start.12 = (f32[1024,640]{1,0:T(8,128)S(1)}, f32[1024,640]{1,0:T(8,128)}, u32[]{:S(2)}) copy-start(f32[1024,640]{1,0:T(8,128)} %param.34) | copy-start | bytes 7864324
  571.7 8.7 %copy-start.13 = (f32[1024,640]{1,0:T(8,128)S(1)}, f32[1024,640]{1,0:T(8,128)}, u32[]{:S(2)}) copy-start(f32[1024,640]{1,0:T(8,128)} %get-tuple-element.84) | copy-start | bytes 7864324
  575.7 4.7 copy-start.5
  575.7 4.7 copy-start.11

commit v6 on v5

--- a/solution.py
+++ b/solution.py
@@ -170,12 +170,16 @@
     return part
 
 
-def ring_gather(part, axis, copies, arrived):
+def about(size, lag=3000):
+    return lag + size // 45
+
+
+def ring_gather(part, axis, copies, arrived, lag=3000):
     me, right, left, far = around(axis)
     block = size_of(part(me, None))
     first = copies.push(part(me, None), part(me, None), axis, right)
     second = copies.push(part(me, None), part(me, None), axis, left)
-    yield block
+    yield about(block, lag)
     first.wait_recv()
     third = copies.push(part(left, 0), part(left, 0), axis, right)
     arrived(part(left, None))
@@ -183,14 +187,14 @@
     second.wait_recv()
     fourth = copies.push(part(right, 1), part(right, 1), axis, left)
     arrived(part(right, None))
-    yield block // 2
+    yield about(block // 2, lag)
     third.wait_recv()
     fourth.wait_recv()
     arrived(part(far, None))
     yield 0
 
 
-def gather_flows(colours, value, out, copies, hold=0):
+def gather_flows(colours, value, out, copies, lag=3000):
     z, x, c = (lax.axis_index(a) for a in ("tok_0", "tok_1", CORE))
     crossing = []
 
@@ -220,12 +224,10 @@
                 (first, second), span = part(i, half, True)
                 return view(out, (first, second, c), span)
 
-            steps = ring_gather(here, RING[name], copies, arrived)
+            steps = ring_gather(here, RING[name], copies, arrived, lag)
             if stage == 0:
                 yield next(steps)
                 arrived(ref)
-            elif stage == 1 and hold:
-                yield hold
             yield from steps
 
     return [run(*colour, ref) for colour, (_, ref) in zip(colours, own)], crossing
@@ -322,20 +324,21 @@
         target[...] = value
 
 
-def ring_scatter(here, slots, axis, copies, ready, done):
+def ring_scatter(here, slots, axis, copies, ready, done, lag=3000, turn=0):
     me, right, left, far = around(axis)
     r1_in, l1_in, r2_in, l2_in, r3_in, l3_in = slots
-    half = size_of(r1_in)
+    half = about(size_of(r1_in), lag)
+    yield turn
     ready(0)
     r1 = copies.push(here(far, 0), r1_in, axis, right)
     l1 = copies.push(here(far, 1), l1_in, axis, left)
-    yield 0
+    yield turn
     ready(1)
     r2 = copies.push(here(right, 1), r2_in, axis, right)
-    yield 0
+    yield turn
     ready(2)
     l2 = copies.push(here(left, 0), l2_in, axis, left)
-    yield half
+    yield max(0, half - 2 * turn)
     r1.wait_recv()
     add_to(here(right, 0), r1_in)
     r3 = copies.push(here(right, 0), r3_in, axis, right)
@@ -343,7 +346,7 @@
     l1.wait_recv()
     add_to(here(left, 1), l1_in)
     l3 = copies.push(here(left, 1), l3_in, axis, left)
-    yield half
+    yield max(turn, half)
     ready(3)
     l2.wait_recv()
     r2.wait_recv()
@@ -356,7 +359,9 @@
     yield 0
 
 
-def scatter_flows(colours, ending, value, out, mine, total, other, slots, copies):
+def scatter_flows(
+    colours, ending, value, out, mine, total, other, slots, copies, lag=3000
+):
     c = lax.axis_index(CORE)
     pending = {}
 
@@ -415,8 +420,9 @@
                 else:
                     out[pl.ds(start, size)] = value
 
+            turn = 0 if stage else len(colours) * size_of(pending[k, 0][2]) // 280
             yield from ring_scatter(
-                here, slots[at : at + 6], axis, copies, nothing if stage else ready, done
+                here, slots[at : at + 6], axis, copies, nothing if stage else ready, done, lag, turn
             )
             at += 6
 
@@ -437,7 +443,7 @@
         copies.push(given(peer), out.at[me], "sub", peer)
         for peer in (lax.rem(me + k, 4) for k in (1, 3, 2))
     ]
-    yield size_of(mine)
+    yield about(size_of(mine), 5000)
     local.wait()
     for copy in arrivals:
         copy.wait_recv()
@@ -514,15 +520,12 @@
             return carry
 
         lax.fori_loop(0, 4, put, 0)
+        yield 8000
 
         def done(half, one, two):
             there(me_y, half)[...] = here(me_y, half)[...] + one[...] + two[...]
 
         yield from ring_scatter(here, table_slots, "sub", copies, lambda turn: None, done)
-
-    def block_flow(flow):
-        yield 1 << 20
-        yield from flow
 
     def own_part(rows):
         start, size = rows
@@ -549,14 +552,14 @@
                 copies.push(board.at[me], board.at[me], axis, lax.rem(me + k, size))
                 for k in range(1, size)
             ]
-            yield 1
+            yield 3500
             for copy in arrivals:
                 copy.wait_recv()
             sums[...] = added([board[k] for k in range(size)])
 
     def whole():
         flows = scatter_flows(colours, "gather", grads, own, None, total, other, slots, copies)
-        yield [table_flow(), *[block_flow(flow) for flow in flows]]
+        yield [table_flow(), *flows]
         ends = [there] + [own_part(rows) for _, rows in colours]
         yield [norm_flow()] + [ring_gather(e, "sub", copies, lambda ref: None) for e in ends]
 
@@ -656,7 +659,7 @@
                 copy.wait_recv()
 
     in_turn([id_flow()])
-    flows, crossing = gather_flows(weight_ways, blocks, slots, copies, 1 << 20)
+    flows, crossing = gather_flows(weight_ways, blocks, slots, copies)
 
     def row_flow():
         yield 1
@@ -671,7 +674,10 @@
             return carry
 
         lax.fori_loop(0, 32, pick, 0)
-        yield scatter_flows(row_ways, "spread", picked, None, held, total, other, inbox, copies)
+        yield 10000
+        yield scatter_flows(
+            row_ways, "spread", picked, None, held, total, other, inbox, copies, 5000
+        )
         yield from to_sub("spread", held, rows, copies)
 
     in_turn([*flows, row_flow()])
@@ -773,7 +779,7 @@
     return tuple((o, (s, n)) for o, s, n in zip(orders, starts, (first, second, last)))
 
 
-WEIGHT_WAYS = three_ways(896, 896, 1408, (("z", "x"), ("x", "z"), ("x", "z", "y")))
+WEIGHT_WAYS = three_ways(1088, 1088, 1024, (("z", "x"), ("x", "z"), ("x", "z", "y")))
 GRAD_WAYS = ((("z", "x", "y"), (0, 1664)), (("x", "z", "y"), (1664, 1536)))
 
 

time: 591 us -> 548 us (0.927)
  Pallas kernels: 469 us -> 425 us
    pallas_call x1, Pallas kernels: 177 us -> 153 us  [close_exchange(): pl.pallas_call(functools.partial(close_kernel, colours, row_ways), out_sh...]
    pallas_call x1, Pallas kernels: 151 us -> 134 us  [open_exchange(): pl.pallas_call(functools.partial(open_kernel, weight_ways, row_ways), out...]
where the time goes in v6:
time: 548 us; the launch traced here: 544 us
  Pallas kernels  425 us (78%)
  other arithmetic  55.7 us (10%)
  matrix products  37.9 us (7%)
  local copies, waits for them, and re-layouts  18.6 us (3%)
  between operations  6.33 us (1%)
    pallas_call x1, Pallas kernels, close_exchange(): pl.pallas_call(functools.partial(close_kernel, colours, row_ways), out_sh...  153 us
    pallas_call x1, Pallas kernels, open_exchange(): pl.pallas_call(functools.partial(open_kernel, weight_ways, row_ways), out...  134 us
    pallas_call x1, Pallas kernels, run_backward(): pl.pallas_call(backward_kernel, out_shape=[jax.ShapeDtypeStruct((order.sh...  42 us
    pallas_call x1, Pallas kernels, gather_tok(): pl.pallas_call(functools.partial(gather_kernel, colours, swap, axes), out...  30.4 us
    pallas_call x1, Pallas kernels, scatter_tok(): pl.pallas_call(functools.partial(scatter_kernel, colours, ending), out_sh...  28.5 us
    pallas_call x1, Pallas kernels, run_forward(): pl.pallas_call(forward_kernel, out_shape=small + mats, in_specs=in_hbm(1)...  23.7 us
    pallas_call x1, Pallas kernels, sum_all(): pl.pallas_call(functools.partial(sum_kernel, axes, combine), out_shape=ja...  13.8 us
    convert_element_type x1, other arithmetic, on_device(): back = back.astype(low_type).reshape(-1, shard_rows)  12.2 us

profile of v6, /device:TPU:0, one launch (start us, length us, event | category | flops | bytes accessed | tf_op | source)
XLA Modules:
  0.0 543.9 jit_solution(13136403813912367631)
XLA Ops:
  0.7 0.8 fusion.22
  1.5 0.7 fusion.24
  2.3 0.7 fusion.26
  3.0 0.8 fusion.30
  3.9 0.7 convert_element_type.111.refs_6_
  4.6 0.7 fusion.20
  5.9 0.7 compare_select_fusion
  6.6 1.0 select_reduce_fusion.1.refs_1_.refs_0_
  7.6 0.6 copy.79
  8.2 0.7 copy.62
  9.1 0.7 sub.110
  9.8 0.7 select_reduce_fusion.2
  10.5 0.6 broadcast_in_dim.41
  11.1 0.7 multiply_add_fusion.5
  11.9 0.6 add_bitcast_fusion.1.mine
  12.5 0.7 broadcast_in_dim.44
  13.2 0.7 add_convert_fusion.refs_8_
  13.9 0.6 multiply_sine_fusion
  14.6 1.0 copy.64
  15.6 1.9 copy.65
  17.4 1.0 convert_element_type.103
  18.5 2.9 convert_element_type.102.table
  21.4 134.5 %shard_map.282 = (s32[4,4,2,1,128]{4,3,2,1,0:T(1,128)}, bf16[4,64,640]{2,1,0:T(8,128)(2,1)}, bf16[4,4,2,3200,128]{4,3,2,1,0:T(8,128)(2,1)}) custom-call(s32[1,128]{1,0:T(1,128)} %add_bitcast_fusion.1.mine, bf16[1024,640]{1,0:T(8,128)(2,1)} %convert_element_type.102.table, bf16[3200,128]{1,0:T(8,128)(2,1)} %bitcast.113), custom_call_target="tpu_custom_call" | custom-call | tf_op jit(solution)/shard_map/pallas_call | solution.py:693
  155.9 1.4 slice_reduce_fusion
  158.0 1.4 reshape.471.ids
  159.4 0.8 slice_subtract_fusion.1
  160.2 1.0 copy_bitcast_fusion
  161.3 0.9 fusion.8
  162.2 2.3 fusion.4
  164.5 23.7 %shard_map.283 = (bf16[128,640]{1,0:T(8,128)(2,1)}, f32[128,640]{1,0:T(8,128)}, f32[128,640]{1,0:T(8,128)}, f32[128,640]{1,0:T(8,128)}, f32[128,640]{1,0:T(8,128...) custom-call(bf16[800,128,128]{2,1,0:T(8,128)(2,1)} %bitcast.109, ...), custom_call_target="tpu_custom_call" | custom-call | tf_op jit(solution)/shard_map/pallas_call | solution.py:1036
  188.2 0.9 copy-done.3
  189.1 30.4 %shard_map.284 = bf16[4,4,2,128,640]{4,3,2,1,0:T(8,128)(2,1)S(1)} custom-call(bf16[128,640]{1,0:T(8,128)(2,1)S(1)} %copy-done.3), custom_call_target="tpu_custom_call" | custom-call | tf_op jit(solution)/shard_map/pallas_call | solution.py:290
  219.5 7.1 %fusion.31 = (f32[32,4,32]{2,1,0:T(4,128)S(1)}, f32[32,4,32,1024]{3,2,1,0:T(8,128)S(1)}) fusion(bf16[32,4,32,640]{3,2,1,0:T(8,128)(2,1)S(1)} %bitcast.100, bf16[1024,640]{1,0:T(8,128)(2,1)S(1)} %copy-done.10), kind=kOutput, calls=%fused_computation.99 | convolution fusion | flops 5372899328 | bytes 23347200 | tf_op jit(solution)/shard_map/td,vd->tv/dot_general | solution.py:1253
  226.6 0.7 select_reduce_fusion
  227.3 3.1 exponential_reduce_fusion
  230.4 0.9 exponential_bitcast_fusion.1
  231.3 1.0 copy-done.4
  232.3 1.8 fusion.3
  234.4 13.8 %shard_map.285 = f32[96,128]{1,0:T(8,128)S(1)} custom-call(f32[96,128]{1,0:T(8,128)S(1)} %reshape.464.value), custom_call_target="tpu_custom_call" | custom-call | tf_op jit(solution)/shard_map/pallas_call | solution.py:760
  248.3 0.7 fusion.18
  249.8 4.7 exponential_bitcast_fusion
  254.5 3.9 broadcast_in_dim.84
  258.4 12.2 %fusion.1 = bf16[32,4,32,1024]{3,2,1,0:T(8,128)(2,1)} fusion(f32[32,3,32,1024]{3,2,1,0:T(8,128)S(1)} %broadcast_in_dim.84, f32[32,1,32,1024]{3,2,1,0:T(8,128)} %fusion.4, f32[32,4,32,1024]{3,2,1,0:T(8,128)} %copy-done.4, f32[32,32]{1,0:T(8,128)S(1)} %broadcast_select_fusion, f32[32,4,32]{2,1,0:T(4,128)S(1)} %copy.68), kind=kLoop, calls=%fused_computation.2 | loop fusion | flops 20971520 | bytes 41963520 | tf_op jit(solution)/shard_map/convert_element_type | solution.py:1282
  270.6 10.4 %fusion.32.table = f32[1024,640]{1,0:T(8,128)} fusion(bf16[4096,1024]{1,0:T(8,128)(2,1)} %bitcast.111, bf16[4096,640]{1,0:T(8,128)(2,1)S(1)} %bitcast.103), kind=kOutput, calls=%fused_computation.100 | convolution fusion | flops 5368709120 | bytes 16252928 | tf_op jit(solution)/shard_map/tv,td->vd/dot_general | solution.py:1285
  280.9 7.0 %convolution_convert_fusion = bf16[4096,640]{1,0:T(8,128)(2,1)S(1)} fusion(bf16[4096,1024]{1,0:T(8,128)(2,1)S(1)} %bitcast.112, bf16[1024,640]{1,0:T(8,128)(2,1)S(1)} %copy-done.10), kind=kOutput, calls=%fused_computation.7 | convolution fusion | flops 5371330560 | bytes 14942208 | tf_op jit(solution)/shard_map/dot_general | solution.py:825
  287.9 28.5 %shard_map.286 = bf16[4,32,640]{2,1,0:T(8,128)(2,1)S(1)} custom-call(bf16[4,4,2,128,640]{4,3,2,1,0:T(8,128)(2,1)S(1)} %bitcast.104), custom_call_target="tpu_custom_call" | custom-call | tf_op jit(solution)/shard_map/pallas_call | solution.py:622
  316.4 0.7 copy-done.2
  317.0 42.0 %shard_map.287 = (bf16[800,128,128]{2,1,0:T(8,128)(2,1)}, f32[16,640]{1,0:T(8,128)}, bf16[256,640]{1,0:T(8,128)(2,1)}) custom-call(s32[800]{0:T(1024)} %select_reduce_fusion.1.refs_1_.refs_0_, bf16[128,640]{1,0:T(8,128)(2,1)} %bitcast.105, f32[128,640]{1,0:T(8,128)} %get-tuple-element.102.refs_2_, f32[128,640]{1,0:T(8,128)} %get-tuple-element.101.refs_3_, ...), custom_call_target="tpu_custom_call" | custom-call | tf_op jit(solution)/shard_map/pallas_call | solution.py:1152
  359.0 0.8 reshape.472
  359.8 0.6 maximum_bitcast_fusion.1.part
  360.4 152.6 %shard_map.288 = (f32[3200,128]{1,0:T(8,128)}, f32[1024,640]{1,0:T(8,128)}, f32[72,128]{1,0:T(8,128)}) custom-call(bf16[4,4,2,3200,128]{4,3,2,1,0:T(8,128)(2,1)} %bitcast.110, f32[1024,640]{1,0:T(8,128)} %fusion.32.table, bf16[256,640]{1,0:T(8,128)(2,1)} %get-tuple-element.80.rows, s32[4,4,1,128]{3,2,1,0:T(1,128)} %reshape.471.ids, ...), custom_call_target="tpu_custom_call" | custom-call | tf_op jit(solution)/shard_map/pallas_call | solution.py:577
  513.1 1.4 multiply_reduce_fusion
  514.5 1.3 slice_reduce_fusion.2
  517.2 1.2 slice.119
  518.3 1.5 broadcast_multiply_fusion
  520.0 0.7 multiply_subtract_fusion.2
  520.6 1.7 multiply_add_fusion.3
  522.4 1.6 fusion.33
  524.0 0.3 copy-done.8
  524.4 0.5 copy-done.14
  524.9 3.2 multiply_subtract_fusion.1
  528.1 4.0 multiply_add_fusion.1
  532.1 4.7 multiply_add_fusion.2
  536.8 4.6 multiply_subtract_fusion
  (78 shorter events, 1.9 us)
Async XLA Ops:
  0.6 521.7 %copy-start = (f32[25,128,128]{2,1,0:T(8,128)S(1)}, f32[25,128,128]{2,1,0:T(8,128)}, u32[]{:S(2)}) copy-start(f32[25,128,128]{2,1,0:T(8,128)} %param.30) | copy-start | bytes 4915204
  0.7 16.8 %copy-start.7 = (f32[25,128,128]{2,1,0:T(8,128)S(1)}, f32[25,128,128]{2,1,0:T(8,128)}, u32[]{:S(2)}) copy-start(f32[25,128,128]{2,1,0:T(8,128)} %param.26) | copy-start | bytes 4915204
  21.4 139.9 %copy-start.17 = (f32[128,640]{1,0:T(8,128)S(1)}, f32[128,640]{1,0:T(8,128)}, u32[]{:S(2)}) copy-start(f32[128,640]{1,0:T(8,128)} %copy.65) | copy-start | bytes 983044
  188.2 0.9 copy-start.3
  189.1 30.4 %copy-start.10 = (bf16[1024,640]{1,0:T(8,128)(2,1)S(1)}, bf16[1024,640]{1,0:T(8,128)(2,1)}, u32[]{:S(2)}) copy-start(bf16[1024,640]{1,0:T(8,128)(2,1)} %convert_element_type.102.table) | copy-start | bytes 3932164
  219.5 7.1 %copy-start.1 = (bf16[4,4,2,128,640]{4,3,2,1,0:T(8,128)(2,1)}, bf16[4,4,2,128,640]{4,3,2,1,0:T(8,128)(2,1)S(1)}, u32[]{:S(2)}) copy-start(bf16[4,4,2,128,640]{4,3,2,1,0:T(8,128)(2,1)S(1)} %shard_map.284) | copy-start | bytes 15728644
  226.6 5.7 %copy-start.4 = (f32[32,4,32,1024]{3,2,1,0:T(8,128)}, f32[32,4,32,1024]{3,2,1,0:T(8,128)S(1)}, u32[]{:S(2)}) copy-start(f32[32,4,32,1024]{3,2,1,0:T(8,128)S(1)} %get-tuple-element.116) | copy-start | bytes 50331652
  232.3 16.1 %copy-start.19 = (s32[4,4,2,1,128]{4,3,2,1,0:T(1,128)S(1)}, s32[4,4,2,1,128]{4,3,2,1,0:T(1,128)}, u32[]{:S(2)}) copy-start(s32[4,4,2,1,128]{4,3,2,1,0:T(1,128)} %get-tuple-element.52) | copy-start | bytes 49156
  254.5 16.1 %slice-start = ((s8[5242880]{0:T(1024)(128)(4,1)}), s8[1048576]{0:T(1024)(128)(4,1)S(1)}, s32[]{:S(2)}) async-start(s8[5242880]{0:T(1024)(128)(4,1)} %bitcast.101), calls=%async_computation | async-start | bytes 2097152
  258.4 12.2 %slice-start.1 = ((s8[5242880]{0:T(1024)(128)(4,1)}), s8[4194304]{0:T(1024)(128)(4,1)S(1)}, s32[]{:S(2)}) async-start(s8[5242880]{0:T(1024)(128)(4,1)} %bitcast.101), calls=%async_computation.1 | async-start | bytes 8388608
  270.6 10.4 %copy-start.6 = (bf16[32,4,32,1024]{3,2,1,0:T(8,128)(2,1)S(1)}, bf16[32,4,32,1024]{3,2,1,0:T(8,128)(2,1)}, u32[]{:S(2)}) copy-start(bf16[32,4,32,1024]{3,2,1,0:T(8,128)(2,1)} %fusion.1) | copy-start | bytes 25165828
  316.4 0.7 copy-start.2
  513.0 6.9 %copy-start.20 = (f32[72,128]{1,0:T(8,128)S(1)}, f32[72,128]{1,0:T(8,128)}, u32[]{:S(2)}) copy-start(f32[72,128]{1,0:T(8,128)} %get-tuple-element.82) | copy-start | bytes 110596
  513.0 6.9 %copy-start.18 = (f32[14,640]{1,0:T(8,128)S(1)}, f32[14,640]{1,0:T(8,128)}, u32[]{:S(2)}) copy-start(f32[14,640]{1,0:T(8,128)} %refs_4_.3) | copy-start | bytes 107524
  513.1 6.9 %copy-start.21 = (f32[14,640]{1,0:T(8,128)S(1)}, f32[14,640]{1,0:T(8,128)}, u32[]{:S(2)}) copy-start(f32[14,640]{1,0:T(8,128)} %param.36) | copy-start | bytes 107524
  513.1 6.9 %copy-start.22 = (f32[14,640]{1,0:T(8,128)S(1)}, f32[14,640]{1,0:T(8,128)}, u32[]{:S(2)}) copy-start(f32[14,640]{1,0:T(8,128)} %param.37) | copy-start | bytes 107524
  522.3 5.8 %copy-start.9 = (f32[25,128,128]{2,1,0:T(8,128)}, f32[25,128,128]{2,1,0:T(8,128)S(1)}, u32[]{:S(2)}) copy-start(f32[25,128,128]{2,1,0:T(8,128)S(1)} %multiply_add_fusion.3) | copy-start | bytes 4915204
  522.4 2.0 copy-start.8
  522.4 2.5 copy-start.14
  524.9 3.3 copy-start.15
  524.9 7.3 %copy-start.16 = (f32[25,128,128]{2,1,0:T(8,128)S(1)}, f32[25,128,128]{2,1,0:T(8,128)}, u32[]{:S(2)}) copy-start(f32[25,128,128]{2,1,0:T(8,128)} %param.28) | copy-start | bytes 4915204
  528.1 8.7 %copy-start.12 = (f32[1024,640]{1,0:T(8,128)S(1)}, f32[1024,640]{1,0:T(8,128)}, u32[]{:S(2)}) copy-start(f32[1024,640]{1,0:T(8,128)} %param.34) | copy-start | bytes 7864324
  528.1 8.7 %copy-start.13 = (f32[1024,640]{1,0:T(8,128)S(1)}, f32[1024,640]{1,0:T(8,128)}, u32[]{:S(2)}) copy-start(f32[1024,640]{1,0:T(8,128)} %get-tuple-element.84) | copy-start | bytes 7864324
  532.1 4.7 copy-start.5
  532.1 4.7 copy-start.11
